TPU v7x, 512 devices: a whole 4x4x16 slice. The times are simulated.
512 devices in a mesh: pts: 128 (over x, z, core), chan: 4 (over y).
Axes of the slice: x: 4, y: 4, z: 16, core: 2. Of those that a mesh axis runs over, the one named last changes fastest.
Arguments:
- feats: bfloat16 [131072, 512], P('pts', 'chan'), may hold values from -6 to 6
- dest_pos: int32 [131072], P('pts'), may hold values from 0 to 131071, as said below
- cell_id: int32 [131072], P('pts'), may hold values from 0 to 16383, as said below
- ln1_gain: float32 [512], replicated, may hold values from 0.1 to 1.9
- w_qkv: bfloat16 [3, 512, 512], P(None, None, 'chan')
- w_out: bfloat16 [512, 512], P('chan'), may hold values from -1 to 1
- ln2_gain: float32 [512], replicated, may hold values from 0.1 to 1.9
- w_fc1: bfloat16 [512, 2048], P(None, 'chan'), may hold values from -0.25 to 0.25
- w_fc2: bfloat16 [2048, 512], P('chan'), may hold values from -0.25 to 0.25
- w_pool: bfloat16 [512, 512], P(None, 'chan'), may hold values from -0.25 to 0.25
Outputs:
- block_out: bfloat16 [131072, 512], P('pts', 'chan')
- pooled: bfloat16 [16384, 512], P('pts', 'chan')
Inputs may be any that keep to these rules, and one draw needn't show every extreme that they name: `dest_pos`: A permutation of the points. Device i of pts sends its points only to devices i - 3 to i + 3 and i + 128 / 2 (cyclic); every device sends the same number of points to the device at a given one of these eight offsets, 192 to one of them and fewer to the others. `cell_id`: never falls along the points; every cell has at least one point; the points of cells b * 128 to (b + 1) * 128 - 1 lie on devices b - 1, b and b + 1 of pts, on both neighbours for some b.
All inputs are finite; a program needn't handle non-finite values.
Results may differ from a plain program's by a relative error of at most 0.023.
The roundings to bfloat16 on the way count: a program that leaves them out, or rounds other values in their place, can miss the bound.
Values may be sent and summed in bfloat16 or wider, within the bound.
No kernel may reach another device: no remote copies, remote signals or barrier semaphores. Data moves between devices by JAX's collectives and lax.ppermute only.
A program may use at most 64 MiB of HBM per device.

v0:
```python
import jax
import jax.numpy as jnp
from jax import lax
from jax.sharding import PartitionSpec as P

PATCH = 1024
HEAD_DIM = 16


def from_behind(x, axis, by):
    count = lax.axis_size(axis)
    pairs = [(i, i + by) for i in range(count) if 0 <= i + by < count]
    return lax.ppermute(x, axis, pairs)


def layer_norm(values, gain):
    mean = jnp.mean(values, axis=-1, keepdims=True)
    centered = values - mean
    var = jnp.mean(centered * centered, axis=-1, keepdims=True)
    return centered * lax.rsqrt(var + 1e-05) * gain


def rank_within(groups, order):
    same = groups[:, None] == groups[None, :]
    earlier = order[None, :] < order[:, None]
    return jnp.sum((same & earlier).astype(jnp.int32), axis=1)


def split_product(left, right):
    high = right.astype(jnp.bfloat16)
    low = (right - high.astype(jnp.float32)).astype(jnp.bfloat16)
    return jnp.dot(left, high, preferred_element_type=jnp.float32) + jnp.dot(
        left, low, preferred_element_type=jnp.float32
    )


def attend(qkv, rows, width):
    heads_here = width // HEAD_DIM
    count = rows // PATCH
    shaped = qkv.reshape(3, count, PATCH, heads_here, HEAD_DIM).transpose(3, 0, 1, 2, 4)
    scale = 1.0 / jnp.sqrt(jnp.float32(HEAD_DIM))

    def one_head(parts):
        scores = (
            jnp.einsum("pqd,pkd->pqk", parts[0], parts[1], preferred_element_type=jnp.float32)
            * scale
        )
        probs = jax.nn.softmax(scores, axis=-1).astype(jnp.bfloat16)
        return jnp.einsum(
            "pqk,pkd->pqd", probs, parts[2], preferred_element_type=jnp.float32
        ).astype(jnp.bfloat16)

    outputs = lax.map(one_head, shaped)
    return outputs.transpose(1, 2, 0, 3).reshape(rows, width)


def body(feats, dest_pos, cell_id, ln1_gain, w_qkv, w_out, ln2_gain, w_fc1, w_fc2, w_pool):
    rows, width = feats.shape
    ndev = lax.axis_size("pts")
    here = lax.axis_index("pts")
    capacity = 3 * rows // 16
    local = jnp.arange(rows, dtype=jnp.int32)
    dest_dev = dest_pos // rows
    dest_local = dest_pos % rows
    slot = dest_dev * capacity + rank_within(dest_dev, local)
    send_rows = jnp.zeros((ndev * capacity, width), jnp.bfloat16).at[slot].set(feats)
    send_slots = jnp.full((ndev * capacity,), -1, jnp.int32).at[slot].set(dest_local)
    got_rows = lax.all_to_all(
        send_rows.reshape(ndev, capacity, width), "pts", split_axis=0, concat_axis=0, tiled=True
    )
    got_slots = lax.all_to_all(
        send_slots.reshape(ndev, capacity), "pts", split_axis=0, concat_axis=0, tiled=True
    )
    flat_slots = got_slots.reshape(-1)
    target = jnp.where(flat_slots < 0, rows, flat_slots)
    ordered = (
        jnp.zeros((rows + 1, width), jnp.bfloat16)
        .at[target]
        .set(got_rows.reshape(-1, width))[:rows]
    )
    full = lax.all_gather(ordered, "chan", axis=1, tiled=True)
    normed = layer_norm(full.astype(jnp.float32), ln1_gain).astype(jnp.bfloat16)
    qkv = jnp.einsum("rc,tcd->trd", normed, w_qkv, preferred_element_type=jnp.float32).astype(
        jnp.bfloat16
    )
    attn = attend(qkv, rows, width)
    partial_value = jnp.dot(attn, w_out, preferred_element_type=jnp.float32)
    summed = lax.psum_scatter(
        partial_value.astype(jnp.bfloat16), "chan", scatter_dimension=1, tiled=True
    ).astype(jnp.float32)
    mid = (ordered.astype(jnp.float32) + summed).astype(jnp.bfloat16)
    mid_full = lax.all_gather(mid, "chan", axis=1, tiled=True)
    normed2 = layer_norm(mid_full.astype(jnp.float32), ln2_gain).astype(jnp.bfloat16)
    act = jax.nn.gelu(
        jnp.dot(normed2, w_fc1, preferred_element_type=jnp.float32), approximate=False
    ).astype(jnp.bfloat16)
    mlp_sum = lax.psum_scatter(
        jnp.dot(act, w_fc2, preferred_element_type=jnp.float32).astype(jnp.bfloat16),
        "chan",
        scatter_dimension=1,
        tiled=True,
    ).astype(jnp.float32)
    block_out = (mid.astype(jnp.float32) + mlp_sum).astype(jnp.bfloat16)
    cells = rows // 8
    relative_cell = cell_id - (here - 1) * cells
    member = relative_cell[None, :] == jnp.arange(3 * cells, dtype=jnp.int32)[:, None]
    counts = jnp.sum(member.astype(jnp.float32), axis=1)
    member_bf = member.astype(jnp.bfloat16)
    block_full = lax.all_gather(block_out, "chan", axis=1, tiled=True)
    lin = jnp.dot(block_full, w_pool, preferred_element_type=jnp.float32)
    sums = split_product(member_bf, lin)
    from_below = (
        from_behind(sums[2 * cells :].astype(jnp.bfloat16), "pts", 1).astype(jnp.float32),
        from_behind(counts[2 * cells :].astype(jnp.bfloat16), "pts", 1).astype(jnp.float32),
    )
    from_above = (
        from_behind(sums[:cells].astype(jnp.bfloat16), "pts", -1).astype(jnp.float32),
        from_behind(counts[:cells].astype(jnp.bfloat16), "pts", -1).astype(jnp.float32),
    )
    total = sums[cells : 2 * cells] + from_below[0] + from_above[0]
    number = counts[cells : 2 * cells] + from_below[1] + from_above[1]
    mean = total / number[:, None]
    pooled = jax.nn.gelu(mean, approximate=False).astype(jnp.bfloat16)
    return (block_out, pooled)


def solution(mesh):
    return jax.shard_map(
        body,
        mesh=mesh,
        in_specs=(
            P("pts", "chan"),
            P("pts"),
            P("pts"),
            P(),
            P(None, None, "chan"),
            P("chan", None),
            P(),
            P(None, "chan"),
            P("chan", None),
            P(None, "chan"),
        ),
        out_specs=(P("pts", "chan"), P("pts", "chan")),
        check_vma=False,
    )
```

profile of v0, /device:TPU:1, one launch (start us, length us, event | category | flops | bytes accessed | tf_op | source)
XLA Modules:
  0.0 652.6 jit_solution(12499390952111390912)
XLA Ops:
  9.2 4.4 scatter_custom_fusion
  14.4 20.4 %all-to-all-start = ((s32[128,1,192]{2,1,0:T(1,128)}), s32[128,1,192]{2,1,0:T(1,128)S(1)}, u32[]{:S(2)}, u32[]{:S(2)}) async-start(s32[128,1,192]{2,1,0:T(1,128)} %all_to_all.12), calls=%async_computation | async-start | bytes 262144 | tf_op jit(solution)/shard_map/all_to_all | solution.py:71
  34.8 7.5 %scatter_custom_fusion.1 = bf16[24576,128]{1,0:T(8,128)(2,1)} fusion(s32[1024]{0:T(1024)S(1)} %get-tuple-element.31, bf16[1024,128]{1,0:T(8,128)(2,1)} %param.12, bf16[]{:T(256)} %constant.57.clone.1), kind=kCustom, calls=%fused_computation.22 | custom fusion | bytes 6291968 | tf_op jit(solution)/shard_map/scatter | solution.py:66
  42.3 9.9 %all-to-all-done = s32[128,1,192]{2,1,0:T(1,128)S(1)} async-done(((s32[128,1,192]{2,1,0:T(1,128)}), s32[128,1,192]{2,1,0:T(1,128)S(1)}, u32[]{:S(2)}, u32[]{:S(2)}) %all-to-all-start) | async-done | bytes 98336 | tf_op jit(solution)/shard_map/all_to_all | solution.py:71
  52.2 8.2 %all-to-all-start.1 = ((bf16[128,192,128]{2,1,0:T(8,128)(2,1)}), bf16[128,192,128]{2,1,0:T(8,128)(2,1)}, u32[]{:S(2)}, u32[]{:S(2)}) async-start(bf16[128,192,128]{2,1,0:T(8,128)(2,1)} %bitcast.52), calls=%async_computation.1 | async-start | bytes 12582912 | tf_op jit(solution)/shard_map/all_to_all | solution.py:68
  61.3 273.7 %all-to-all-done.1 = bf16[128,192,128]{2,1,0:T(8,128)(2,1)} async-done(((bf16[128,192,128]{2,1,0:T(8,128)(2,1)}), bf16[128,192,128]{2,1,0:T(8,128)(2,1)}, u32[]{:S(2)}, u32[]{:S(2)}) %all-to-all-start.1) | async-done | bytes 6291488 | tf_op jit(solution)/shard_map/all_to_all | solution.py:68
  335.0 61.6 %scatter_custom_fusion.2 = bf16[1025,128]{1,0:T(8,128)(2,1)S(1)} fusion(s32[24576]{0:T(1024)S(1)} %bitcast.62, bf16[24576,128]{1,0:T(8,128)(2,1)} %bitcast.6, bf16[]{:T(256)} %constant.57.clone.1), kind=kCustom, calls=%fused_computation.109 | custom fusion | bytes 262912 | tf_op jit(solution)/shard_map/scatter | solution.py:79
  397.6 30.4 %all-gather.4.cloned.1.call-done = bf16[1024,512]{1,0:T(8,128)(2,1)} async-done(((bf16[1024,128]{1,0:T(8,128)(2,1)}), bf16[1024,512]{1,0:T(8,128)(2,1)}) %all-gather.4.cloned.1.call-update) | async-done | bytes 1048592 | tf_op jit(solution)/shard_map/all_gather | solution.py:81
  432.2 52.0 %while.10 = (s32[]{:T(128)}, bf16[8,1,1024,16]{2,3,1,0:T(8,128)(2,1)S(1)}, bf16[8,3,1,1024,16]{3,4,2,1,0:T(8,128)(2,1)S(1)}, s32[]{:T(128)}, s32[]{:T(128)}, /*index=5*/s32[]{}, s32[]{}) while((s32[]{:T(128)}, bf16[8,1,1024,16]{2,3,1,0:T(8,128)(2,1)S(1)}, bf16[8,3,1,1024,16]{3,4,2,1,0:T(8,128)(2,1)S(1)}, s32[]{:T(128)}, s32[]{:T(128)}, ...), condition=%wide.region_9.10_spmd, body=%wide.region_6.9_spmd.sunk | while | flops 76560384 | bytes 29513864 | solution.py:53
  435.7 3.1 fusion.148
  442.2 3.1 fusion.148
  448.6 3.1 fusion.148
  455.1 3.1 fusion.148
  461.6 3.1 fusion.148
  468.1 3.1 fusion.148
  474.6 3.1 fusion.148
  486.0 31.9 %reduce-scatter.7.cloned.1.call-done = bf16[128,1024]{1,0:T(8,128)(2,1)} async-done(((bf16[512,1024]{1,0:T(8,128)(2,1)}), bf16[128,1024]{1,0:T(8,128)(2,1)}) %reduce-scatter.7.cloned.1.call-update) | async-done | bytes 262160
  520.1 34.5 %all-gather.6.cloned.1.call-done = bf16[1024,512]{1,0:T(8,128)(2,1)} async-done(((bf16[1024,128]{1,0:T(8,128)(2,1)}), bf16[1024,512]{1,0:T(8,128)(2,1)}) %all-gather.6.cloned.1.call-update) | async-done | bytes 1048592 | tf_op jit(solution)/shard_map/all_gather | solution.py:92
  557.9 5.3 convolution_convert_fusion.1
  564.6 31.9 %reduce-scatter.9.cloned.1.call-done = bf16[128,1024]{1,0:T(8,128)(2,1)} async-done(((bf16[512,1024]{1,0:T(8,128)(2,1)}), bf16[128,1024]{1,0:T(8,128)(2,1)}) %reduce-scatter.9.cloned.1.call-update) | async-done | bytes 262160
  598.8 5.1 collective-permute-start.2
  605.8 27.1 %all-gather.8.cloned.1.call-done = bf16[1024,512]{1,0:T(8,128)(2,1)} async-done(((bf16[1024,128]{1,0:T(8,128)(2,1)}), bf16[1024,512]{1,0:T(8,128)(2,1)}) %all-gather.8.cloned.1.call-update) | async-done | bytes 1048592 | tf_op jit(solution)/shard_map/all_gather | solution.py:109
  635.3 4.6 collective-permute-start
  641.9 3.3 collective-permute-done.1
  (108 shorter events, 57.2 us)
Async XLA Ops:
  7.2 550.7 %copy-start = (bf16[512,512]{1,0:T(8,128)(2,1)S(1)}, bf16[512,512]{1,0:T(8,128)(2,1)}, u32[]{:S(2)}) copy-start(bf16[512,512]{1,0:T(8,128)(2,1)} %param.20) | copy-start | bytes 1572868
  14.4 37.8 %all-to-all-start = ((s32[128,1,192]{2,1,0:T(1,128)}), s32[128,1,192]{2,1,0:T(1,128)S(1)}, u32[]{:S(2)}, u32[]{:S(2)}) async-start(s32[128,1,192]{2,1,0:T(1,128)} %all_to_all.12), calls=%async_computation | async-start | bytes 262144 | tf_op jit(solution)/shard_map/all_to_all | solution.py:71
  52.2 345.2 %copy-start.5 = (bf16[3,512,128]{2,1,0:T(8,128)(2,1)S(1)}, bf16[3,512,128]{2,1,0:T(8,128)(2,1)}, u32[]{:S(2)}) copy-start(bf16[3,512,128]{2,1,0:T(8,128)(2,1)} %param.16) | copy-start | bytes 1179652
  52.2 282.8 %all-to-all-start.1 = ((bf16[128,192,128]{2,1,0:T(8,128)(2,1)}), bf16[128,192,128]{2,1,0:T(8,128)(2,1)}, u32[]{:S(2)}, u32[]{:S(2)}) async-start(bf16[128,192,128]{2,1,0:T(8,128)(2,1)} %bitcast.52), calls=%async_computation.1 | async-start | bytes 12582912 | tf_op jit(solution)/shard_map/all_to_all | solution.py:68
  60.4 367.5 %all-gather.4.cloned.1.call-start = ((), (), s32[]{:S(2)}) async-start(), calls=%async_computation.4 | async-start | bytes 1310720 | tf_op jit(solution)/shard_map/all_gather | solution.py:81
  61.1 370.1 %copy-start.10 = (f32[512]{0:T(512)S(1)}, f32[512]{0:T(512)}, u32[]{:S(2)}) copy-start(f32[512]{0:T(512)} %param.15) | copy-start | bytes 6148
  397.3 120.6 %reduce-scatter.7.cloned.1.call-start = ((), (), s32[]{:S(2)}) async-start(), calls=%async_computation.7 | async-start | bytes 1310720
  427.9 3.3 copy-start.2
  432.2 52.0 %copy-start.6 = (bf16[128,512]{1,0:T(8,128)(2,1)S(1)}, bf16[128,512]{1,0:T(8,128)(2,1)}, u32[]{:S(2)}) copy-start(bf16[128,512]{1,0:T(8,128)(2,1)} %param.17) | copy-start | bytes 393220
  433.0 1.9 copy-start.1
  465.5 1.9 copy-start.1
  486.0 71.9 %copy-start.9 = (bf16[512,512]{1,0:T(8,128)(2,1)S(1)}, bf16[512,512]{1,0:T(8,128)(2,1)}, u32[]{:S(2)}) copy-start(bf16[512,512]{1,0:T(8,128)(2,1)} %param.19) | copy-start | bytes 1572868
  486.0 71.9 %copy-start.11 = (f32[512]{0:T(512)S(1)}, f32[512]{0:T(512)}, u32[]{:S(2)}) copy-start(f32[512]{0:T(512)} %param.18) | copy-start | bytes 6148
  486.0 68.6 %all-gather.6.cloned.1.call-start = ((), (), s32[]{:S(2)}) async-start(), calls=%async_computation.5 | async-start | bytes 1310720 | tf_op jit(solution)/shard_map/all_gather | solution.py:92
  519.9 76.7 %reduce-scatter.9.cloned.1.call-start = ((), (), s32[]{:S(2)}) async-start(), calls=%async_computation.8 | async-start | bytes 1310720
  554.6 3.3 copy-start.3
  563.2 34.4 %copy-start.4 = (bf16[1024,128]{1,0:T(8,128)(2,1)S(1)}, bf16[1024,128]{1,0:T(8,128)(2,1)}, u32[]{:S(2)}) copy-start(bf16[1024,128]{1,0:T(8,128)(2,1)} %add_convert_fusion.1) | copy-start | bytes 786436
  563.2 35.3 %copy-start.8 = (s32[1024]{0:T(1024)S(1)}, s32[1024]{0:T(1024)}, u32[]{:S(2)}) copy-start(s32[1024]{0:T(1024)} %param.14) | copy-start | bytes 12292
  563.2 69.7 %copy-start.7 = (bf16[512,128]{1,0:T(8,128)(2,1)S(1)}, bf16[512,128]{1,0:T(8,128)(2,1)}, u32[]{:S(2)}) copy-start(bf16[512,128]{1,0:T(8,128)(2,1)} %param.21) | copy-start | bytes 393220
  564.6 68.3 %all-gather.8.cloned.1.call-start = ((), (), s32[]{:S(2)}) async-start(), calls=%async_computation.6 | async-start | bytes 1310720 | tf_op jit(solution)/shard_map/all_gather | solution.py:109
  598.8 43.1 %collective-permute-start.2 = (bf16[128]{0:T(256)(128)(2,1)S(1)}, bf16[128]{0:T(256)(128)(2,1)S(1)}, u32[]{:S(2)}, u32[]{:S(2)}) collective-permute-start(bf16[128]{0:T(256)(128)(2,1)S(1)} %get-tuple-element.32), channel_id=1, source_target_pairs={{0,4},{4,8},{8,12},{12,16},{16,20},{20,24},{24,28},{28,32},{32,36}... | collective-permute-start | bytes 776 | tf_op jit(solution)/shard_map/ppermute | solution.py:13
  603.8 38.1 %collective-permute-start.3 = (bf16[128]{0:T(256)(128)(2,1)S(1)}, bf16[128]{0:T(256)(128)(2,1)S(1)}, u32[]{:S(2)}, u32[]{:S(2)}) collective-permute-start(bf16[128]{0:T(256)(128)(2,1)S(1)} %get-tuple-element.33), channel_id=1, source_target_pairs={{4,0},{8,4},{12,8},{16,12},{20,16},{24,20},{28,24},{32,28},{36,32}... | collective-permute-start | bytes 776 | tf_op jit(solution)/shard_map/ppermute | solution.py:13
  635.3 6.6 %collective-permute-start = (bf16[128,128]{1,0:T(8,128)(2,1)S(1)}, bf16[128,128]{1,0:T(8,128)(2,1)S(1)}, u32[]{:S(2)}, u32[]{:S(2)}) collective-permute-start(bf16[128,128]{1,0:T(8,128)(2,1)S(1)} %get-tuple-element.28), channel_id=1, source_target_pairs={{0,4},{4,8},{8,12},{12,16},{16,20},{20,24},{24,28},{28,32},{32,36}... | collective-permute-start | bytes 98312 | tf_op jit(solution)/shard_map/ppermute | solution.py:13
  640.0 5.2 collective-permute-start.1
  (6 other events, 11.6 us)
Sparse Core Ops, SparseCore 0:
  397.4 30.4 all-gather.3
  486.1 31.8 reduce-scatter.6
  520.8 33.7 all-gather.5
  564.7 31.8 reduce-scatter.8
  599.1 33.7 all-gather.7
where the time goes:
time: 654 us; the launch traced here: 653 us
  waiting for transfers between devices  443 us (68%)
  local copies, waits for them, and re-layouts  95.8 us (15%)
  starting transfers between devices  42.7 us (7%)
  matrix products  39.5 us (6%)
  other arithmetic  17.5 us (3%)
  between operations  14.2 us (2%)
    all_to_all x1, waiting for transfers between devices, body(): lax.all_to_all(send_rows.reshape(ndev, capacity, width), 'pts', split_axi...  274 us
    unnamed x7, waiting for transfers between devices  63.9 us
    scatter x1, local copies, waits for them, and re-layouts, body(): ordered = jnp.zeros((rows + 1, width), jnp.bfloat16).at[target].set(got_r...  61.6 us
    all_gather x1, waiting for transfers between devices, body(): mid_full = lax.all_gather(mid, 'chan', axis=1, tiled=True)  34.5 us
    all_gather x1, waiting for transfers between devices, body(): full = lax.all_gather(ordered, 'chan', axis=1, tiled=True)  30.4 us
    all_gather x1, waiting for transfers between devices, body(): block_full = lax.all_gather(block_out, 'chan', axis=1, tiled=True)  27.1 us
    dot_general x8, matrix products, one_head(): jnp.einsum('pqk,pkd->pqd', probs, parts[2], preferred_element_type=jnp.fl...  24.5 us
    all_to_all x1, starting transfers between devices, body(): lax.all_to_all(send_slots.reshape(ndev, capacity), 'pts', split_axis=0, c...  20.4 us
  transfers between devices with their start and end apart: 11, of which 8 were waited for; matrix products, arithmetic and copies ran while one was open for 2% of the time, Pallas kernels for 0%

commit v1 on v0

v1 whole, which is shorter than its diff:
```python
import jax
import jax.numpy as jnp
from jax import lax
from jax.experimental import pallas as pl
from jax.experimental.pallas import tpu as pltpu
from jax.sharding import PartitionSpec as P

F32 = jnp.float32
BF16 = jnp.bfloat16

N_PTS = 128
N_CHAN = 4
ROWS = 1024
C = 512
LANES = 128
HEADS_HERE = 8
HEAD_DIM = 16
QUARTER = ROWS // N_CHAN
CELLS = ROWS // 8
CAP = 192
BLOCK = CAP + 16
KINDS = 8
SLOTS = KINDS * CAP
HALF = 256
WROWS = 768
MESSAGE = QUARTER + 3 * CELLS
VMEM_LIMIT = 48 * 1024 * 1024


def chip_up(i):
    return (i + 2 if (i >> 1) % 2 == 0 else i - 2) % N_PTS


def chip_down(i):
    return (i - 2 if (i >> 1) % 2 == 0 else i + 2) % N_PTS


def core_swap(i):
    return i ^ 1


def next_pair(i):
    return (i - 1 if i % 2 == 0 else i + 1) % N_PTS


def far_pair(i):
    return (i - 3 if i % 2 == 0 else i + 3) % N_PTS


def across(i):
    return (i + N_PTS // 2) % N_PTS


def exchange(x, partner):
    return lax.ppermute(x, "pts", [(i, partner(i)) for i in range(N_PTS)])


def offsets_of(me):
    core = lax.rem(me, 2)
    chip = lax.rem(me // 2, 2)
    up = 2 - 4 * chip
    swap = 1 - 2 * core
    return [0 * me, up, up + swap, -up, swap - up, swap, 6 * core - 3, 0 * me + 64]


def matmul(a, b):
    return jnp.dot(a, b, preferred_element_type=F32)


def matmul_nt(a, b):
    return lax.dot_general(a, b, (((1,), (1,)), ((), ())), preferred_element_type=F32)


def matmul_tn(a, b):
    return lax.dot_general(a, b, (((0,), (0,)), ((), ())), preferred_element_type=F32)


def one_hot(row, height):
    index = lax.broadcasted_iota(jnp.int32, (height, row.shape[1]), 0)
    return jnp.where(index == row, 1.0, 0.0).astype(BF16)


def gelu(x):
    return 0.5 * x * (1.0 + lax.erf(x * 0.7071067811865476))


def normed_chunks(chunks, gains):
    total = chunks[0]
    for x in chunks[1:]:
        total = total + x
    mean = jnp.sum(total, axis=-1, keepdims=True) * (1.0 / C)
    centered = [x - mean for x in chunks]
    square = centered[0] * centered[0]
    for x in centered[1:]:
        square = square + x * x
    var = jnp.sum(square, axis=-1, keepdims=True) * (1.0 / C)
    scale = lax.rsqrt(var + 1e-05)
    return [(x * scale * g).astype(BF16) for x, g in zip(centered, gains)]


def pack_kernel(
    feats_ref, dest_ref, cell_ref, w_out_ref, w_fc1_ref, w_fc2_ref, w_pool_ref,
    own_ref, up_ref, down_ref, swap_ref, far_ref, across_ref, weights_ref,
):
    me = lax.axis_index("pts")
    core = lax.rem(me, 2)

    for side in range(2):

        @pl.when(core == side)
        def _():
            cols = slice(side * HALF, (side + 1) * HALF)
            weights_ref[0:256, 0:256] = w_fc1_ref[0:256, cols]
            weights_ref[0:256, 256:512] = w_fc1_ref[256:512, cols]
            weights_ref[256:512, :] = w_fc2_ref[cols, :]

    weights_ref[512:640, :] = w_out_ref[...]
    for r in range(4):
        weights_ref[640:768, r * 128 : (r + 1) * 128] = w_pool_ref[r * 128 : (r + 1) * 128, :]

    offsets = offsets_of(me)
    dest = dest_ref[...]
    away = ((dest >> 10) - me) & (N_PTS - 1)
    local = dest & (ROWS - 1)
    kind = jnp.zeros_like(dest)
    for m in range(1, KINDS):
        kind = jnp.where(away == (offsets[m] & (N_PTS - 1)), m, kind)

    kinds = one_hot(kind, 16)
    before = lax.broadcasted_iota(jnp.int32, (ROWS, ROWS), 0)
    after = lax.broadcasted_iota(jnp.int32, (ROWS, ROWS), 1)
    earlier = jnp.where(before < after, 1.0, 0.0).astype(BF16)
    ranks = matmul(kinds, earlier) * kinds.astype(F32)
    rank = jnp.sum(ranks, axis=0, keepdims=True).astype(jnp.int32)
    slot = jnp.where(rank < 128, kind * 128 + rank, 1024 - 128 + kind * 64 + rank)

    chosen = one_hot(slot, SLOTS)
    packed = matmul(chosen, feats_ref[...]).astype(BF16)
    line = lax.broadcasted_iota(jnp.int32, (16, ROWS), 0)
    digits = jnp.where(line == 0, (local >> 5) + 1, jnp.where(line == 1, local & 31, 0))
    places = matmul_nt(digits.astype(F32).astype(BF16), chosen)

    relative = cell_ref[...] - (me - 1) * CELLS
    counts = matmul_nt(jnp.full((16, ROWS), 1.0, BF16), one_hot(relative, 3 * CELLS))
    counts = counts[0:1, :].astype(jnp.int32)

    small = lax.broadcasted_iota(jnp.int32, (16, 128), 0)
    lane = lax.broadcasted_iota(jnp.int32, (1, 128), 1)
    homes = [
        (own_ref, 0), (up_ref, 0), (up_ref, BLOCK), (down_ref, 0),
        (down_ref, BLOCK), (swap_ref, 0), (far_ref, 0), (across_ref, 0),
    ]
    for m, (ref, base) in enumerate(homes):
        ref[base : base + 128, :] = packed[m * 128 : (m + 1) * 128, :]
        ref[base + 128 : base + CAP, :] = packed[1024 + m * 64 : 1024 + (m + 1) * 64, :]
        first = places[0:2, m * 128 : (m + 1) * 128]
        mine = (lane >= 64) if m % 2 else (lane < 64)
        tile = 1024 + (m // 2) * 128
        second = jnp.where(mine, places[0:2, tile : tile + 128], 0.0)
        if m == 0:
            count = counts[:, CELLS : 2 * CELLS]
        else:
            ahead = (offsets[m] == 1).astype(jnp.int32)
            behind = (offsets[m] == -1).astype(jnp.int32)
            count = counts[:, 2 * CELLS :] * ahead + counts[:, :CELLS] * behind
        rows = [
            first[0:1], first[1:2], second[0:1], second[1:2],
            (count >> 5).astype(F32), (count & 31).astype(F32),
        ]
        notes = jnp.zeros((16, 128), F32)
        for r, value in enumerate(rows):
            notes = jnp.where(small == r, value, notes)
        ref[base + CAP : base + BLOCK, :] = notes.astype(BF16)


def unpack_kernel(own_ref, up_ref, down_ref, far_ref, across_ref, swap_ref, out_ref, count_ref, held):
    homes = [
        (own_ref, 0), (up_ref, 0), (swap_ref, BLOCK), (down_ref, 0),
        (swap_ref, 2 * BLOCK), (swap_ref, 0), (far_ref, 0), (across_ref, 0),
    ]
    firsts, seconds = [], []
    count = jnp.zeros((1, 128), F32)
    for m, (ref, base) in enumerate(homes):
        held[m * 128 : (m + 1) * 128, :] = ref[base : base + 128, :]
        held[1024 + m * 64 : 1024 + (m + 1) * 64, :] = ref[base + 128 : base + CAP, :]
        notes = ref[base + CAP : base + BLOCK, :].astype(F32)
        firsts.append(notes[0:1] * 32.0 + notes[1:2] - 32.0)
        seconds.append(notes[2:3] * 32.0 + notes[3:4])
        count = count + notes[4:5] * 32.0 + notes[5:6]
    pairs = [seconds[m] + seconds[m + 1] - 32.0 for m in range(0, KINDS, 2)]
    places = jnp.concatenate(firsts + pairs, axis=1).astype(jnp.int32)
    ordered = matmul(one_hot(places, ROWS), held[...]).astype(BF16)
    for c in range(N_CHAN):
        out_ref[c * ROWS : (c + 1) * ROWS, :] = ordered
    count_ref[...] = jnp.broadcast_to(count, (128, 128)).T


def attention_kernel(x_ref, gain_ref, w_ref, out_ref, normed, q_ref, k_ref, v_ref):
    gains = [gain_ref[:, c * 128 : (c + 1) * 128] for c in range(4)]
    for r in range(4):
        rows = slice(r * 256, (r + 1) * 256)
        chunks = [x_ref[c * ROWS + r * 256 : c * ROWS + (r + 1) * 256, :].astype(F32) for c in range(4)]
        for c, part in enumerate(normed_chunks(chunks, gains)):
            normed[rows, c * 128 : (c + 1) * 128] = part
    everything = normed[...]
    q_ref[...] = (matmul(everything, w_ref[0]).astype(BF16).astype(F32) * 0.25).astype(BF16)
    k_ref[...] = matmul(everything, w_ref[1]).astype(BF16)
    v_ref[...] = matmul(everything, w_ref[2]).T.astype(BF16)
    head_of = lax.broadcasted_iota(jnp.int32, (256, LANES), 1) // HEAD_DIM

    def head(h, carry):
        values = v_ref[pl.ds(pl.multiple_of(h * HEAD_DIM, HEAD_DIM), HEAD_DIM), :]
        for part in range(4):
            query = q_ref[part * 256 : (part + 1) * 256, :].astype(F32)
            query = jnp.where(head_of == h, query, 0.0).astype(BF16)
            scores = matmul_nt(k_ref[...], query)
            top = jnp.max(scores, axis=0, keepdims=True)
            grown = jnp.exp(scores - top)
            share = 1.0 / jnp.sum(grown, axis=0, keepdims=True)
            probs = (grown * share).astype(BF16)
            result = matmul(values, probs).astype(BF16)
            start = pl.multiple_of(part * 128 + h * HEAD_DIM, HEAD_DIM)
            out_ref[pl.ds(start, HEAD_DIM), :] = result
        return carry

    lax.fori_loop(0, HEADS_HERE, head, 0)


def mlp_kernel(
    attn_ref, x_ref, gain_ref, cell_ref, mine_ref, other_ref, out_ref,
    x_rows, w_out, w_fc1, w_fc2, w_pool, sems,
):
    chan = lax.axis_index("chan")
    me = lax.axis_index("pts")
    row = pl.multiple_of(chan * QUARTER, QUARTER)
    copies = []

    def start(group, src, dst):
        copy = pltpu.make_async_copy(src, dst, sems.at[len(copies)])
        copy.start()
        copies.append(copy)
        group.append(copy)

    def wait(group):
        for copy in group:
            copy.wait()

    early, late, stages = [], [], []
    for c in range(4):
        start(early, x_ref.at[pl.ds(c * ROWS + row, QUARTER), :], x_rows.at[:, c * 128 : (c + 1) * 128])
        start(early, mine_ref.at[c * WROWS + 512 : c * WROWS + 640, :], w_out.at[c * 128 : (c + 1) * 128, :])
    for s, ref in enumerate((mine_ref, other_ref)):
        for c in range(4):
            stage = []
            k = s * 4 + c
            base = c * WROWS
            start(stage, ref.at[base : base + 256, 0:256], w_fc1.at[k, 0:256, :])
            start(stage, ref.at[base : base + 256, 256:512], w_fc1.at[k, 256:512, :])
            start(stage, ref.at[base + 256 : base + 512, :], w_fc2.at[k])
            stages.append(stage)
    for c in range(4):
        for r in range(4):
            src = mine_ref.at[c * WROWS + 640 : c * WROWS + 768, r * 128 : (r + 1) * 128]
            start(late, src, w_pool.at[r * 128 : (r + 1) * 128, c * 128 : (c + 1) * 128])

    wait(early)
    mid = (x_rows[...].astype(F32) + matmul_tn(attn_ref[...], w_out[...])).astype(BF16)
    mid = mid.astype(F32)
    normed = normed_chunks([mid], [gain_ref[...]])[0]
    total = mid
    for k, stage in enumerate(stages):
        wait(stage)
        act = gelu(matmul(normed, w_fc1[k])).astype(BF16)
        term = matmul(act, w_fc2[k])
        summed = term if k == 0 else summed + term
    block = (total + summed).astype(BF16)
    wait(late)
    lin = matmul(block, w_pool[...])
    high = lin.astype(BF16)
    low = (lin - high.astype(F32)).astype(BF16)
    member = one_hot(cell_ref[pl.ds(chan, 1), :] - (me - 1) * CELLS, 3 * CELLS)
    sums = (matmul(member, high) + matmul(member, low)).astype(BF16)
    for c in range(4):
        cols = slice(c * 128, (c + 1) * 128)
        out_ref[c * MESSAGE : c * MESSAGE + QUARTER, :] = block[:, cols]
        out_ref[c * MESSAGE + QUARTER : (c + 1) * MESSAGE, :] = sums[:, cols]


def gather_kernel(got_ref, block_ref, own_ref, swap_ref, next_ref):
    core = lax.rem(lax.axis_index("pts"), 2)
    sums = jnp.zeros((3 * CELLS, LANES), F32)
    for c in range(4):
        block_ref[c * QUARTER : (c + 1) * QUARTER, :] = got_ref[c * MESSAGE : c * MESSAGE + QUARTER, :]
        sums = sums + got_ref[c * MESSAGE + QUARTER : (c + 1) * MESSAGE, :].astype(F32)
    own_ref[...] = sums[CELLS : 2 * CELLS]
    before = sums[:CELLS].astype(BF16)
    after = sums[2 * CELLS :].astype(BF16)

    @pl.when(core == 0)
    def _():
        swap_ref[...] = after
        next_ref[...] = before

    @pl.when(core == 1)
    def _():
        swap_ref[...] = before
        next_ref[...] = after


def pool_kernel(own_ref, swap_ref, next_ref, count_ref, out_ref):
    total = own_ref[...] + swap_ref[...].astype(F32) + next_ref[...].astype(F32)
    out_ref[...] = gelu(total / count_ref[...]).astype(BF16)


def call(kernel, outs, args, scratch=(), anywhere=(), flops=0, bytes_accessed=0):
    vmem = pl.BlockSpec(memory_space=pltpu.VMEM)
    return pl.pallas_call(
        kernel,
        out_shape=[jax.ShapeDtypeStruct(shape, dtype) for shape, dtype in outs],
        in_specs=[pl.BlockSpec(memory_space=pl.ANY) if i in anywhere else vmem for i in range(len(args))],
        out_specs=[vmem] * len(outs),
        scratch_shapes=list(scratch),
        compiler_params=pltpu.CompilerParams(vmem_limit_bytes=VMEM_LIMIT),
    )(*args)


def body(feats, dest_pos, cell_id, ln1_gain, w_qkv, w_out, ln2_gain, w_fc1, w_fc2, w_pool):
    def block(count=1):
        return ((count * BLOCK, LANES), BF16)

    own, up, down, swap, far, over, weights = call(
        pack_kernel,
        [block(), block(2), block(2), block(), block(), block(), ((WROWS, C), BF16)],
        (feats, dest_pos.reshape(1, ROWS), cell_id.reshape(1, ROWS), w_out, w_fc1, w_fc2, w_pool),
    )
    gathered = lax.all_gather(weights, "chan", axis=0, tiled=True)
    up = exchange(up, chip_up)
    down = exchange(down, chip_down)
    far = exchange(far, far_pair)
    over = exchange(over, across)
    swap = exchange(jnp.concatenate([swap, up[BLOCK:], down[BLOCK:]], axis=0), core_swap)
    ordered, count = call(
        unpack_kernel,
        [((N_CHAN * ROWS, LANES), BF16), ((128, 128), F32)],
        (own, up, down, far, over, swap),
        scratch=[pltpu.VMEM((SLOTS, LANES), BF16)],
    )
    full = lax.all_to_all(ordered, "chan", split_axis=0, concat_axis=0, tiled=True)
    (attn,) = call(
        attention_kernel,
        [((N_CHAN * LANES, QUARTER), BF16)],
        (full, ln1_gain.reshape(1, C), w_qkv),
        scratch=[
            pltpu.VMEM((ROWS, C), BF16),
            pltpu.VMEM((ROWS, LANES), BF16),
            pltpu.VMEM((ROWS, LANES), BF16),
            pltpu.VMEM((LANES, ROWS), BF16),
        ],
    )
    attn, gathered = lax.optimization_barrier((attn, gathered))
    others = exchange(gathered, core_swap)
    attn = lax.all_to_all(attn, "chan", split_axis=0, concat_axis=0, tiled=True)
    (message,) = call(
        mlp_kernel,
        [((N_CHAN * MESSAGE, LANES), BF16)],
        (attn, full, ln2_gain.reshape(1, C), cell_id.reshape(N_CHAN, QUARTER), gathered, others),
        anywhere=(1, 4, 5),
        scratch=[
            pltpu.VMEM((QUARTER, C), BF16),
            pltpu.VMEM((C, C), BF16),
            pltpu.VMEM((8, C, HALF), BF16),
            pltpu.VMEM((8, HALF, C), BF16),
            pltpu.VMEM((C, C), BF16),
            pltpu.SemaphoreType.DMA((48,)),
        ],
    )
    got = lax.all_to_all(message, "chan", split_axis=0, concat_axis=0, tiled=True)
    cell_sum = ((CELLS, LANES), BF16)
    block_out, mine, for_swap, for_next = call(
        gather_kernel,
        [((ROWS, LANES), BF16), ((CELLS, LANES), F32), cell_sum, cell_sum],
        (got,),
    )
    from_swap = exchange(for_swap, core_swap)
    from_next = exchange(for_next, next_pair)
    (pooled,) = call(pool_kernel, [cell_sum], (mine, from_swap, from_next, count))
    return (block_out, pooled)


def solution(mesh):
    return jax.shard_map(
        body,
        mesh=mesh,
        in_specs=(
            P("pts", "chan"),
            P("pts"),
            P("pts"),
            P(),
            P(None, None, "chan"),
            P("chan", None),
            P(),
            P(None, "chan"),
            P("chan", None),
            P(None, "chan"),
        ),
        out_specs=(P("pts", "chan"), P("pts", "chan")),
        check_vma=False,
    )
```

time: 654 us -> 161 us (0.25)
  waiting for transfers between devices: 443 us -> 15.6 us
  local copies, waits for them, and re-layouts: 95.8 us -> 8.13 us
  blocking collectives: 0 us -> 41.7 us
  matrix products: 39.5 us -> 0 us
  Pallas kernels: 0 us -> 39.5 us
  other arithmetic: 17.5 us -> 0.01 us
    all_to_all x2 -> x1, waiting for transfers between devices: 284 us -> 6.77 us  [body(): attn = lax.all_to_all(attn, 'chan', split_axis=0, concat_axis=0, tiled=True)]
    all_gather x3 -> x1, waiting for transfers between devices: 92 us -> 0.01 us  [body(): gathered = lax.all_gather(weights, 'chan', axis=0, tiled=True)]
    scatter x3 -> x0, local copies, waits for them, and re-layouts: 73.4 us -> none  [the longest x1 61.6 us: body(): ordered = jnp.zeros((rows + 1, width), jnp.bfloat16).at[target].set(got_r...]
    unnamed x7 -> x1, waiting for transfers between devices: 63.9 us -> 0.02 us
    all_to_all x0 -> x2, blocking collectives: none -> 41.7 us  [the longest x1 29.3 us: body(): lax.all_to_all(ordered, 'chan', split_axis=0, concat_axis=0, tiled=True)]
    pallas_call x0 -> x6, Pallas kernels: none -> 39.5 us  [call(): pl.pallas_call(kernel, out_shape=[jax.ShapeDtypeStruct(shape, dtype) for...]
    dot_general x21 -> x0, matrix products: 38.8 us -> none  [the longest x8 24.5 us: one_head(): jnp.einsum('pqk,pkd->pqd', probs, parts[2], preferred_element_type=jnp.fl...]
    all_to_all x2 -> x1, starting transfers between devices: 28.6 us -> 3.42 us  [body(): attn = lax.all_to_all(attn, 'chan', split_axis=0, concat_axis=0, tiled=True)]
  transfers between devices with their start and end apart: 11 -> 10, of which waited for: 8 -> 5; matrix products, arithmetic and copies ran while one was open for 2% -> 0% of each run, Pallas kernels for 0% -> 19%
where the time goes in v1:
time: 161 us; the launch traced here: 159 us
  blocking collectives  41.7 us (26%)
  starting transfers between devices  39.6 us (25%)
  Pallas kernels  39.5 us (25%)
  waiting for transfers between devices  15.6 us (10%)
  between operations  14.2 us (9%)
  local copies, waits for them, and re-layouts  8.13 us (5%)
    pallas_call x6, Pallas kernels, call(): pl.pallas_call(kernel, out_shape=[jax.ShapeDtypeStruct(shape, dtype) for...  39.5 us
    ppermute x8, starting transfers between devices, exchange(): return lax.ppermute(x, 'pts', [(i, partner(i)) for i in range(N_PTS)])  36.2 us
    all_to_all x1, blocking collectives, body(): lax.all_to_all(ordered, 'chan', split_axis=0, concat_axis=0, tiled=True)  29.3 us
    all_to_all x1, blocking collectives, body(): lax.all_to_all(message, 'chan', split_axis=0, concat_axis=0, tiled=True)  12.3 us
    ppermute x8, waiting for transfers between devices, exchange(): return lax.ppermute(x, 'pts', [(i, partner(i)) for i in range(N_PTS)])  8.8 us
    unnamed x24, local copies, waits for them, and re-layouts  8.11 us
    all_to_all x1, waiting for transfers between devices, body(): attn = lax.all_to_all(attn, 'chan', split_axis=0, concat_axis=0, tiled=True)  6.77 us
    all_to_all x1, starting transfers between devices, body(): attn = lax.all_to_all(attn, 'chan', split_axis=0, concat_axis=0, tiled=True)  3.42 us
  transfers between devices with their start and end apart: 10, of which 5 were waited for; matrix products, arithmetic and copies ran while one was open for 0% of the time, Pallas kernels for 19%

profile of v1, /device:TPU:1, one launch (start us, length us, event | category | flops | bytes accessed | tf_op | source)
XLA Modules:
  0.0 158.7 jit_solution(13664016240424826284)
XLA Ops:
  7.2 1.0 copy-done.1
  8.3 1.0 copy-done.2
  9.3 0.9 copy-done.4
  13.4 3.2 %shard_map.113 = (bf16[208,128]{1,0:T(8,128)(2,1)S(1)}, bf16[416,128]{1,0:T(8,128)(2,1)S(1)}, bf16[416,128]{1,0:T(8,128)(2,1)S(1)}, bf16[208,128]{1,0:T(8,128)(2...) custom-call(bf16[1024,128]{1,0:T(8,128)(2,1)S(1)} %copy-done.4, ...), custom_call_target="tpu_custom_call" | custom-call | tf_op jit(solution)/shard_map/pallas_call | solution.py:317
  16.7 4.4 %collective-permute-start = (bf16[416,128]{1,0:T(8,128)(2,1)S(1)}, bf16[416,128]{1,0:T(8,128)(2,1)S(1)}, u32[]{:S(2)}, u32[]{:S(2)}) collective-permute-start(bf16[416,128]{1,0:T(8,128)(2,1)S(1)} %get-tuple-element.18), channel_id=1, source_target_pairs={{0,8},{4,12},{8,0},{12,4},{16,24},{20,28},{24,16},{28,20},{32,40},... | collective-permute-start | bytes 319496 | tf_op jit(solution)/shard_map/ppermute | solution.py:55
  21.1 12.4 %collective-permute-start.1 = (bf16[416,128]{1,0:T(8,128)(2,1)S(1)}, bf16[416,128]{1,0:T(8,128)(2,1)S(1)}, u32[]{:S(2)}, u32[]{:S(2)}) collective-permute-start(bf16[416,128]{1,0:T(8,128)(2,1)S(1)} %get-tuple-element.19), channel_id=1, source_target_pairs={{0,504},{4,508},{8,16},{12,20},{16,8},{20,12},{24,32},{28,36},{32,... | collective-permute-start | bytes 319496 | tf_op jit(solution)/shard_map/ppermute | solution.py:55
  33.5 2.1 %collective-permute-done.1.down_ref = bf16[416,128]{1,0:T(8,128)(2,1)S(1)} collective-permute-done((bf16[416,128]{1,0:T(8,128)(2,1)S(1)}, bf16[416,128]{1,0:T(8,128)(2,1)S(1)}, u32[]{:S(2)}, u32[]{:S(2)}) %collective-permute-start.1) | collective-permute-done | bytes 106528 | tf_op jit(solution)/shard_map/ppermute | solution.py:55
  35.6 3.7 %collective-permute-start.4 = (bf16[624,128]{1,0:T(8,128)(2,1)S(1)}, bf16[624,128]{1,0:T(8,128)(2,1)S(1)}, u32[]{:S(2)}, u32[]{:S(2)}) collective-permute-start(bf16[624,128]{1,0:T(8,128)(2,1)S(1)} %pad_maximum_fusion), channel_id=1, source_target_pairs={{0,4},{4,0},{8,12},{12,8},{16,20},{20,16},{24,28},{28,24},{32,36},... | collective-permute-start | bytes 479240 | tf_op jit(solution)/shard_map/ppermute | solution.py:55
  39.3 1.9 %collective-permute-start.2 = (bf16[208,128]{1,0:T(8,128)(2,1)S(1)}, bf16[208,128]{1,0:T(8,128)(2,1)S(1)}, u32[]{:S(2)}, u32[]{:S(2)}) collective-permute-start(bf16[208,128]{1,0:T(8,128)(2,1)S(1)} %get-tuple-element.20), channel_id=1, source_target_pairs={{0,500},{4,16},{8,508},{12,24},{16,4},{20,32},{24,12},{28,40},{32,... | collective-permute-start | bytes 159752 | tf_op jit(solution)/shard_map/ppermute | solution.py:55
  41.3 2.4 %collective-permute-start.3 = (bf16[208,128]{1,0:T(8,128)(2,1)S(1)}, bf16[208,128]{1,0:T(8,128)(2,1)S(1)}, u32[]{:S(2)}, u32[]{:S(2)}) collective-permute-start(bf16[208,128]{1,0:T(8,128)(2,1)S(1)} %get-tuple-element.21), channel_id=1, source_target_pairs={{0,256},{4,260},{8,264},{12,268},{16,272},{20,276},{24,280},{28,28... | collective-permute-start | bytes 159752 | tf_op jit(solution)/shard_map/ppermute | solution.py:55
  43.7 2.4 %collective-permute-done.2.far_ref = bf16[208,128]{1,0:T(8,128)(2,1)S(1)} collective-permute-done((bf16[208,128]{1,0:T(8,128)(2,1)S(1)}, bf16[208,128]{1,0:T(8,128)(2,1)S(1)}, u32[]{:S(2)}, u32[]{:S(2)}) %collective-permute-start.2) | collective-permute-done | bytes 53280 | tf_op jit(solution)/shard_map/ppermute | solution.py:55
  46.1 2.2 %collective-permute-done.3.across_ref = bf16[208,128]{1,0:T(8,128)(2,1)S(1)} collective-permute-done((bf16[208,128]{1,0:T(8,128)(2,1)S(1)}, bf16[208,128]{1,0:T(8,128)(2,1)S(1)}, u32[]{:S(2)}, u32[]{:S(2)}) %collective-permute-start.3) | collective-permute-done | bytes 53280 | tf_op jit(solution)/shard_map/ppermute | solution.py:55
  48.3 1.0 shard_map.114
  49.3 29.3 %all_to_all.33 = bf16[4,1024,128]{2,1,0:T(8,128)(2,1)S(1)} all-to-all(bf16[4,1024,128]{2,1,0:T(8,128)(2,1)S(1)} %bitcast.15), channel_id=1, replica_groups=mesh['pts'=128,'chan'=4] {'chan'}, dimensions={0} | all-to-all | bytes 2097152 | tf_op jit(solution)/shard_map/all_to_all | solution.py:348
  78.7 28.5 %shard_map.115 = bf16[512,256]{1,0:T(8,128)(2,1)} custom-call(bf16[4096,128]{1,0:T(8,128)(2,1)S(1)} %bitcast.10, f32[1,512]{1,0:T(1,128)S(1)} %bitcast.18, bf16[3,512,128]{2,1,0:T(8,128)(2,1)S(1)} %copy-done.3), custom_call_target="tpu_custom_call" | custom-call | tf_op jit(solution)/shard_map/pallas_call | solution.py:317
  107.1 4.4 %collective-permute-start.5 = (bf16[3072,512]{1,0:T(8,128)(2,1)}, bf16[3072,512]{1,0:T(8,128)(2,1)}, u32[]{:S(2)}, u32[]{:S(2)}) collective-permute-start(bf16[3072,512]{1,0:T(8,128)(2,1)} %all-gather.2.cloned.1.call-done.mine_ref), channel_id=1, source_target_pairs={{0,4},{4,0},{8,12},{12,8},{16,20},{20,16},{24,28},{28,24},{32,36},... | collective-permute-start | bytes 9437192 | tf_op jit(solution)/shard_map/ppermute | solution.py:55
  111.6 3.4 %all-to-all-start.1 = ((bf16[4,128,256]{2,1,0:T(8,128)(2,1)}), bf16[4,128,256]{2,1,0:T(8,128)(2,1)S(1)}, u32[]{:S(2)}, u32[]{:S(2)}) async-start(bf16[4,128,256]{2,1,0:T(8,128)(2,1)} %bitcast.5), calls=%async_computation.1 | async-start | bytes 524288 | tf_op jit(solution)/shard_map/all_to_all | solution.py:362
  115.0 6.8 %all-to-all-done.1 = bf16[4,128,256]{2,1,0:T(8,128)(2,1)S(1)} async-done(((bf16[4,128,256]{2,1,0:T(8,128)(2,1)}), bf16[4,128,256]{2,1,0:T(8,128)(2,1)S(1)}, u32[]{:S(2)}, u32[]{:S(2)}) %all-to-all-start.1) | async-done | bytes 262176 | tf_op jit(solution)/shard_map/all_to_all | solution.py:362
  121.8 1.9 %copy-done = bf16[3072,512]{1,0:T(8,128)(2,1)S(1)} copy-done((bf16[3072,512]{1,0:T(8,128)(2,1)S(1)}, bf16[3072,512]{1,0:T(8,128)(2,1)}, u32[]{:S(2)}) %copy-start) | copy-done | bytes 3145752
  123.7 5.4 %shard_map.116 = bf16[2560,128]{1,0:T(8,128)(2,1)S(1)} custom-call(bf16[512,256]{1,0:T(8,128)(2,1)S(1)} %bitcast.14, bf16[4096,128]{1,0:T(8,128)(2,1)S(1)} %bitcast.11, f32[1,512]{1,0:T(1,128)S(1)} %bitcast.19, s32[4,256]{1,0:T(4,128)S(1)} %reshape.29.cell_ref, bf16[3072,512]{1,0:T(8,128)(2,1)S(1)} %copy-done, bf16[3072,512]{1,0:T(8,128)(2,1)} %collective-permute-done.5.other_ref), custom_call_target="tpu_custom_call" | custom-call | tf_op jit(solution)/shard_map/pallas_call | solution.py:317
  129.1 12.3 %all_to_all.34 = bf16[4,640,128]{2,1,0:T(8,128)(2,1)S(1)} all-to-all(bf16[4,640,128]{2,1,0:T(8,128)(2,1)S(1)} %bitcast.12), channel_id=1, replica_groups=mesh['pts'=128,'chan'=4] {'chan'}, dimensions={0} | all-to-all | bytes 1310720 | tf_op jit(solution)/shard_map/all_to_all | solution.py:377
  142.2 3.8 %collective-permute-start.6 = (bf16[128,128]{1,0:T(8,128)(2,1)S(1)}, bf16[128,128]{1,0:T(8,128)(2,1)S(1)}, u32[]{:S(2)}, u32[]{:S(2)}) collective-permute-start(bf16[128,128]{1,0:T(8,128)(2,1)S(1)} %get-tuple-element.29), channel_id=1, source_target_pairs={{0,4},{4,0},{8,12},{12,8},{16,20},{20,16},{24,28},{28,24},{32,36},... | collective-permute-start | bytes 98312 | tf_op jit(solution)/shard_map/ppermute | solution.py:55
  146.0 3.1 %collective-permute-start.7 = (bf16[128,128]{1,0:T(8,128)(2,1)S(1)}, bf16[128,128]{1,0:T(8,128)(2,1)S(1)}, u32[]{:S(2)}, u32[]{:S(2)}) collective-permute-start(bf16[128,128]{1,0:T(8,128)(2,1)S(1)} %get-tuple-element.30), channel_id=1, source_target_pairs={{0,508},{4,8},{8,4},{12,16},{16,12},{20,24},{24,20},{28,32},{32,28... | collective-permute-start | bytes 98312 | tf_op jit(solution)/shard_map/ppermute | solution.py:55
  149.1 2.1 %collective-permute-done.7.next_ref = bf16[128,128]{1,0:T(8,128)(2,1)S(1)} collective-permute-done((bf16[128,128]{1,0:T(8,128)(2,1)S(1)}, bf16[128,128]{1,0:T(8,128)(2,1)S(1)}, u32[]{:S(2)}, u32[]{:S(2)}) %collective-permute-start.7) | collective-permute-done | bytes 32800 | tf_op jit(solution)/shard_map/ppermute | solution.py:55
  (33 shorter events, 4.7 us)
Async XLA Ops:
  7.2 71.5 %copy-start.10 = (f32[512]{0:T(512)S(1)}, f32[512]{0:T(512)}, u32[]{:S(2)}) copy-start(f32[512]{0:T(512)} %param.13) | copy-start | bytes 6148
  7.2 100.0 %all-gather.2.cloned.1.call-start = ((), (), s32[]{:S(2)}) async-start(), calls=%async_computation.3 | async-start | bytes 3932160 | tf_op jit(solution)/shard_map/all_gather | solution.py:336
  7.2 1.0 copy-start.1
  8.3 1.0 copy-start.2
  9.3 0.9 copy-start.4
  10.3 0.9 copy-start.5
  11.2 0.9 copy-start.6
  12.1 0.7 copy-start.7
  12.8 0.7 copy-start.9
  13.4 65.2 %copy-start.3 = (bf16[3,512,128]{2,1,0:T(8,128)(2,1)S(1)}, bf16[3,512,128]{2,1,0:T(8,128)(2,1)}, u32[]{:S(2)}) copy-start(bf16[3,512,128]{2,1,0:T(8,128)(2,1)} %w_ref.1) | copy-start | bytes 1179652
  16.7 98.3 %copy-start.8 = (s32[1024]{0:T(1024)S(1)}, s32[1024]{0:T(1024)}, u32[]{:S(2)}) copy-start(s32[1024]{0:T(1024)} %param.12) | copy-start | bytes 12292
  16.7 105.1 %copy-start.11 = (f32[512]{0:T(512)S(1)}, f32[512]{0:T(512)}, u32[]{:S(2)}) copy-start(f32[512]{0:T(512)} %param.16) | copy-start | bytes 6148
  16.7 16.8 %collective-permute-start = (bf16[416,128]{1,0:T(8,128)(2,1)S(1)}, bf16[416,128]{1,0:T(8,128)(2,1)S(1)}, u32[]{:S(2)}, u32[]{:S(2)}) collective-permute-start(bf16[416,128]{1,0:T(8,128)(2,1)S(1)} %get-tuple-element.18), channel_id=1, source_target_pairs={{0,8},{4,12},{8,0},{12,4},{16,24},{20,28},{24,16},{28,20},{32,40},... | collective-permute-start | bytes 319496 | tf_op jit(solution)/shard_map/ppermute | solution.py:55
  21.1 14.5 %collective-permute-start.1 = (bf16[416,128]{1,0:T(8,128)(2,1)S(1)}, bf16[416,128]{1,0:T(8,128)(2,1)S(1)}, u32[]{:S(2)}, u32[]{:S(2)}) collective-permute-start(bf16[416,128]{1,0:T(8,128)(2,1)S(1)} %get-tuple-element.19), channel_id=1, source_target_pairs={{0,504},{4,508},{8,16},{12,20},{16,8},{20,12},{24,32},{28,36},{32,... | collective-permute-start | bytes 319496 | tf_op jit(solution)/shard_map/ppermute | solution.py:55
  35.6 12.7 %collective-permute-start.4 = (bf16[624,128]{1,0:T(8,128)(2,1)S(1)}, bf16[624,128]{1,0:T(8,128)(2,1)S(1)}, u32[]{:S(2)}, u32[]{:S(2)}) collective-permute-start(bf16[624,128]{1,0:T(8,128)(2,1)S(1)} %pad_maximum_fusion), channel_id=1, source_target_pairs={{0,4},{4,0},{8,12},{12,8},{16,20},{20,16},{24,28},{28,24},{32,36},... | collective-permute-start | bytes 479240 | tf_op jit(solution)/shard_map/ppermute | solution.py:55
  39.3 6.8 %collective-permute-start.2 = (bf16[208,128]{1,0:T(8,128)(2,1)S(1)}, bf16[208,128]{1,0:T(8,128)(2,1)S(1)}, u32[]{:S(2)}, u32[]{:S(2)}) collective-permute-start(bf16[208,128]{1,0:T(8,128)(2,1)S(1)} %get-tuple-element.20), channel_id=1, source_target_pairs={{0,500},{4,16},{8,508},{12,24},{16,4},{20,32},{24,12},{28,40},{32,... | collective-permute-start | bytes 159752 | tf_op jit(solution)/shard_map/ppermute | solution.py:55
  41.3 7.0 %collective-permute-start.3 = (bf16[208,128]{1,0:T(8,128)(2,1)S(1)}, bf16[208,128]{1,0:T(8,128)(2,1)S(1)}, u32[]{:S(2)}, u32[]{:S(2)}) collective-permute-start(bf16[208,128]{1,0:T(8,128)(2,1)S(1)} %get-tuple-element.21), channel_id=1, source_target_pairs={{0,256},{4,260},{8,264},{12,268},{16,272},{20,276},{24,280},{28,28... | collective-permute-start | bytes 159752 | tf_op jit(solution)/shard_map/ppermute | solution.py:55
  107.1 14.6 %collective-permute-start.5 = (bf16[3072,512]{1,0:T(8,128)(2,1)}, bf16[3072,512]{1,0:T(8,128)(2,1)}, u32[]{:S(2)}, u32[]{:S(2)}) collective-permute-start(bf16[3072,512]{1,0:T(8,128)(2,1)} %all-gather.2.cloned.1.call-done.mine_ref), channel_id=1, source_target_pairs={{0,4},{4,0},{8,12},{12,8},{16,20},{20,16},{24,28},{28,24},{32,36},... | collective-permute-start | bytes 9437192 | tf_op jit(solution)/shard_map/ppermute | solution.py:55
  111.6 10.2 %all-to-all-start.1 = ((bf16[4,128,256]{2,1,0:T(8,128)(2,1)}), bf16[4,128,256]{2,1,0:T(8,128)(2,1)S(1)}, u32[]{:S(2)}, u32[]{:S(2)}) async-start(bf16[4,128,256]{2,1,0:T(8,128)(2,1)} %bitcast.5), calls=%async_computation.1 | async-start | bytes 524288 | tf_op jit(solution)/shard_map/all_to_all | solution.py:362
  121.8 1.9 %copy-start = (bf16[3072,512]{1,0:T(8,128)(2,1)S(1)}, bf16[3072,512]{1,0:T(8,128)(2,1)}, u32[]{:S(2)}) copy-start(bf16[3072,512]{1,0:T(8,128)(2,1)} %all-gather.2.cloned.1.call-done.mine_ref) | copy-start | bytes 9437188
  142.2 6.9 %collective-permute-start.6 = (bf16[128,128]{1,0:T(8,128)(2,1)S(1)}, bf16[128,128]{1,0:T(8,128)(2,1)S(1)}, u32[]{:S(2)}, u32[]{:S(2)}) collective-permute-start(bf16[128,128]{1,0:T(8,128)(2,1)S(1)} %get-tuple-element.29), channel_id=1, source_target_pairs={{0,4},{4,0},{8,12},{12,8},{16,20},{20,16},{24,28},{28,24},{32,36},... | collective-permute-start | bytes 98312 | tf_op jit(solution)/shard_map/ppermute | solution.py:55
  146.0 5.2 %collective-permute-start.7 = (bf16[128,128]{1,0:T(8,128)(2,1)S(1)}, bf16[128,128]{1,0:T(8,128)(2,1)S(1)}, u32[]{:S(2)}, u32[]{:S(2)}) collective-permute-start(bf16[128,128]{1,0:T(8,128)(2,1)S(1)} %get-tuple-element.30), channel_id=1, source_target_pairs={{0,508},{4,8},{8,4},{12,16},{16,12},{20,24},{24,20},{28,32},{32,28... | collective-permute-start | bytes 98312 | tf_op jit(solution)/shard_map/ppermute | solution.py:55
Sparse Core Ops, SparseCore 0:
  16.8 63.0 all-gather.1

commit v2 on v1

--- a/solution.py
+++ b/solution.py
@@ -22,9 +22,12 @@
 KINDS = 8
 SLOTS = KINDS * CAP
 HALF = 256
-WROWS = 768
+STEP = 512
+FC1, FC2, POOL, WROWS = 256, 1280, 2304, 2560
 MESSAGE = QUARTER + 3 * CELLS
 VMEM_LIMIT = 48 * 1024 * 1024
+MOST_VMEM = 61 * 1024 * 1024 + 512 * 1024
+ALL_VMEM = 63 * 1024 * 1024 + 512 * 1024
 
 
 def chip_up(i):
@@ -98,71 +101,53 @@
     return [(x * scale * g).astype(BF16) for x, g in zip(centered, gains)]
 
 
-def pack_kernel(
-    feats_ref, dest_ref, cell_ref, w_out_ref, w_fc1_ref, w_fc2_ref, w_pool_ref,
-    own_ref, up_ref, down_ref, swap_ref, far_ref, across_ref, weights_ref,
-):
-    me = lax.axis_index("pts")
-    core = lax.rem(me, 2)
-
-    for side in range(2):
-
-        @pl.when(core == side)
-        def _():
-            cols = slice(side * HALF, (side + 1) * HALF)
-            weights_ref[0:256, 0:256] = w_fc1_ref[0:256, cols]
-            weights_ref[0:256, 256:512] = w_fc1_ref[256:512, cols]
-            weights_ref[256:512, :] = w_fc2_ref[cols, :]
-
-    weights_ref[512:640, :] = w_out_ref[...]
-    for r in range(4):
-        weights_ref[640:768, r * 128 : (r + 1) * 128] = w_pool_ref[r * 128 : (r + 1) * 128, :]
-
-    offsets = offsets_of(me)
-    dest = dest_ref[...]
-    away = ((dest >> 10) - me) & (N_PTS - 1)
+def copier(sems):
+    copies = []
+
+    def start(src, dst):
+        copy = pltpu.make_async_copy(src, dst, sems.at[len(copies)])
+        copy.start()
+        copies.append(copy)
+        return copy
+
+    return start
+
+
+def wait(copies):
+    for copy in copies:
+        copy.wait()
+
+
+def digits_of(dest):
     local = dest & (ROWS - 1)
-    kind = jnp.zeros_like(dest)
-    for m in range(1, KINDS):
-        kind = jnp.where(away == (offsets[m] & (N_PTS - 1)), m, kind)
-
-    kinds = one_hot(kind, 16)
-    before = lax.broadcasted_iota(jnp.int32, (ROWS, ROWS), 0)
-    after = lax.broadcasted_iota(jnp.int32, (ROWS, ROWS), 1)
-    earlier = jnp.where(before < after, 1.0, 0.0).astype(BF16)
-    ranks = matmul(kinds, earlier) * kinds.astype(F32)
-    rank = jnp.sum(ranks, axis=0, keepdims=True).astype(jnp.int32)
-    slot = jnp.where(rank < 128, kind * 128 + rank, 1024 - 128 + kind * 64 + rank)
-
-    chosen = one_hot(slot, SLOTS)
-    packed = matmul(chosen, feats_ref[...]).astype(BF16)
     line = lax.broadcasted_iota(jnp.int32, (16, ROWS), 0)
     digits = jnp.where(line == 0, (local >> 5) + 1, jnp.where(line == 1, local & 31, 0))
-    places = matmul_nt(digits.astype(F32).astype(BF16), chosen)
-
-    relative = cell_ref[...] - (me - 1) * CELLS
+    return digits.astype(F32).astype(BF16)
+
+
+def cell_counts(cell, me):
+    relative = cell - (me - 1) * CELLS
     counts = matmul_nt(jnp.full((16, ROWS), 1.0, BF16), one_hot(relative, 3 * CELLS))
-    counts = counts[0:1, :].astype(jnp.int32)
-
+    return counts[0:1, :].astype(jnp.int32)
+
+
+def write_blocks(slot, dest, feats, blocks, counts):
     small = lax.broadcasted_iota(jnp.int32, (16, 128), 0)
     lane = lax.broadcasted_iota(jnp.int32, (1, 128), 1)
-    homes = [
-        (own_ref, 0), (up_ref, 0), (up_ref, BLOCK), (down_ref, 0),
-        (down_ref, BLOCK), (swap_ref, 0), (far_ref, 0), (across_ref, 0),
-    ]
-    for m, (ref, base) in enumerate(homes):
+    chosen = one_hot(slot, SLOTS)
+    packed = matmul(chosen, feats).astype(BF16)
+    places = matmul_nt(digits_of(dest), chosen)
+    for m, (ref, base, offset) in enumerate(blocks):
         ref[base : base + 128, :] = packed[m * 128 : (m + 1) * 128, :]
         ref[base + 128 : base + CAP, :] = packed[1024 + m * 64 : 1024 + (m + 1) * 64, :]
         first = places[0:2, m * 128 : (m + 1) * 128]
         mine = (lane >= 64) if m % 2 else (lane < 64)
         tile = 1024 + (m // 2) * 128
         second = jnp.where(mine, places[0:2, tile : tile + 128], 0.0)
-        if m == 0:
-            count = counts[:, CELLS : 2 * CELLS]
-        else:
-            ahead = (offsets[m] == 1).astype(jnp.int32)
-            behind = (offsets[m] == -1).astype(jnp.int32)
-            count = counts[:, 2 * CELLS :] * ahead + counts[:, :CELLS] * behind
+        count = jnp.zeros((1, CELLS), jnp.int32)
+        for away in (-1, 0, 1):
+            near = jnp.where(offset == away, 1, 0)
+            count = count + counts[:, (away + 1) * CELLS : (away + 2) * CELLS] * near
         rows = [
             first[0:1], first[1:2], second[0:1], second[1:2],
             (count >> 5).astype(F32), (count & 31).astype(F32),
@@ -171,6 +156,59 @@
         for r, value in enumerate(rows):
             notes = jnp.where(small == r, value, notes)
         ref[base + CAP : base + BLOCK, :] = notes.astype(BF16)
+
+
+def pack_kernel(
+    feats_ref, dest_ref, cell_ref, w_out_ref, w_fc1_ref, w_fc2_ref, w_pool_ref,
+    own_ref, up_ref, down_ref, swap_ref, far_ref, across_ref, weights_ref,
+    feats_here, dest_here, cell_here, sems,
+):
+    me = lax.axis_index("pts")
+    core = lax.rem(me, 2)
+    start = copier(sems)
+    dest_copy = start(dest_ref, dest_here)
+    cell_copy = start(cell_ref, cell_here)
+    feats_copy = start(feats_ref, feats_here)
+
+    half = pl.multiple_of(core * HALF, HALF)
+    quarter = pl.multiple_of(core * 64, 64)
+    weight_copies = []
+    for r in range(2):
+        src = w_fc1_ref.at[:, pl.ds(pl.multiple_of(half + r * 128, 128), 128)]
+        weight_copies.append(start(src, weights_ref.at[FC1 + r * C : FC1 + (r + 1) * C, :]))
+    for r in range(4):
+        cols = slice(r * 128, (r + 1) * 128)
+        dst = weights_ref.at[FC2 + r * HALF : FC2 + (r + 1) * HALF, :]
+        weight_copies.append(start(w_fc2_ref.at[pl.ds(half, HALF), cols], dst))
+        dst = weights_ref.at[r * 64 : (r + 1) * 64, :]
+        weight_copies.append(start(w_out_ref.at[pl.ds(quarter, 64), cols], dst))
+    weight_copies.append(start(w_pool_ref.at[pl.ds(half, HALF), :], weights_ref.at[POOL:WROWS, :]))
+
+    before = lax.broadcasted_iota(jnp.int32, (ROWS, ROWS), 0)
+    after = lax.broadcasted_iota(jnp.int32, (ROWS, ROWS), 1)
+    earlier = jnp.where(before < after, 1.0, 0.0).astype(BF16)
+    wait([dest_copy])
+    offsets = offsets_of(me)
+    dest = dest_here[...]
+    away = ((dest >> 10) - me) & (N_PTS - 1)
+    kind = jnp.zeros_like(dest)
+    for m in range(1, KINDS):
+        kind = jnp.where(away == (offsets[m] & (N_PTS - 1)), m, kind)
+
+    kinds = one_hot(kind, 16)
+    ranks = matmul(kinds, earlier) * kinds.astype(F32)
+    rank = jnp.sum(ranks, axis=0, keepdims=True).astype(jnp.int32)
+    slot = jnp.where(rank < 128, kind * 128 + rank, 1024 - 128 + kind * 64 + rank)
+    homes = [
+        (own_ref, 0), (up_ref, 0), (up_ref, BLOCK), (down_ref, 0),
+        (down_ref, BLOCK), (swap_ref, 0), (far_ref, 0), (across_ref, 0),
+    ]
+    blocks = [home + (offset,) for home, offset in zip(homes, offsets)]
+    wait([cell_copy])
+    counts = cell_counts(cell_here[...], me)
+    wait([feats_copy])
+    write_blocks(slot, dest, feats_here[...], blocks, counts)
+    wait(weight_copies)
 
 
 def unpack_kernel(own_ref, up_ref, down_ref, far_ref, across_ref, swap_ref, out_ref, count_ref, held):
@@ -206,76 +244,74 @@
     q_ref[...] = (matmul(everything, w_ref[0]).astype(BF16).astype(F32) * 0.25).astype(BF16)
     k_ref[...] = matmul(everything, w_ref[1]).astype(BF16)
     v_ref[...] = matmul(everything, w_ref[2]).T.astype(BF16)
-    head_of = lax.broadcasted_iota(jnp.int32, (256, LANES), 1) // HEAD_DIM
-
-    def head(h, carry):
-        values = v_ref[pl.ds(pl.multiple_of(h * HEAD_DIM, HEAD_DIM), HEAD_DIM), :]
-        for part in range(4):
-            query = q_ref[part * 256 : (part + 1) * 256, :].astype(F32)
-            query = jnp.where(head_of == h, query, 0.0).astype(BF16)
-            scores = matmul_nt(k_ref[...], query)
-            top = jnp.max(scores, axis=0, keepdims=True)
-            grown = jnp.exp(scores - top)
-            share = 1.0 / jnp.sum(grown, axis=0, keepdims=True)
-            probs = (grown * share).astype(BF16)
-            result = matmul(values, probs).astype(BF16)
-            start = pl.multiple_of(part * 128 + h * HEAD_DIM, HEAD_DIM)
-            out_ref[pl.ds(start, HEAD_DIM), :] = result
-        return carry
-
-    lax.fori_loop(0, HEADS_HERE, head, 0)
+    head_of = lax.broadcasted_iota(jnp.int32, (STEP, LANES), 1) // HEAD_DIM
+    work = [(h, part) for h in range(HEADS_HERE) for part in range(ROWS // STEP)]
+
+    def scores_of(h, part):
+        query = q_ref[part * STEP : (part + 1) * STEP, :].astype(F32)
+        query = jnp.where(head_of == h, query, 0.0).astype(BF16)
+        return matmul_nt(k_ref[...], query)
+
+    scores = scores_of(*work[0])
+    for n, (h, part) in enumerate(work):
+        following = scores_of(*work[n + 1]) if n + 1 < len(work) else None
+        top = jnp.max(scores, axis=0, keepdims=True)
+        grown = jnp.exp(scores - top)
+        share = 1.0 / jnp.sum(grown, axis=0, keepdims=True)
+        probs = (grown * share).astype(BF16)
+        result = matmul(v_ref[h * HEAD_DIM : (h + 1) * HEAD_DIM, :], probs).astype(BF16)
+        for u in range(STEP // QUARTER):
+            row = (part * (STEP // QUARTER) + u) * LANES + h * HEAD_DIM
+            out_ref[row : row + HEAD_DIM, :] = result[:, u * QUARTER : (u + 1) * QUARTER]
+        scores = following
 
 
 def mlp_kernel(
-    attn_ref, x_ref, gain_ref, cell_ref, mine_ref, other_ref, out_ref,
-    x_rows, w_out, w_fc1, w_fc2, w_pool, sems,
+    attn_ref, x_ref, gain_ref, cell_ref, mine_ref, other_ref, out_ref, x_rows, held, sems,
 ):
     chan = lax.axis_index("chan")
     me = lax.axis_index("pts")
+    core = lax.rem(me, 2)
     row = pl.multiple_of(chan * QUARTER, QUARTER)
-    copies = []
-
-    def start(group, src, dst):
-        copy = pltpu.make_async_copy(src, dst, sems.at[len(copies)])
-        copy.start()
-        copies.append(copy)
-        group.append(copy)
-
-    def wait(group):
-        for copy in group:
-            copy.wait()
-
-    early, late, stages = [], [], []
+    start = copier(sems)
+    sources = [(s, c) for s in range(2) for c in range(4)]
+    refs = (mine_ref, other_ref)
+    early, late = [], []
     for c in range(4):
-        start(early, x_ref.at[pl.ds(c * ROWS + row, QUARTER), :], x_rows.at[:, c * 128 : (c + 1) * 128])
-        start(early, mine_ref.at[c * WROWS + 512 : c * WROWS + 640, :], w_out.at[c * 128 : (c + 1) * 128, :])
-    for s, ref in enumerate((mine_ref, other_ref)):
-        for c in range(4):
-            stage = []
-            k = s * 4 + c
-            base = c * WROWS
-            start(stage, ref.at[base : base + 256, 0:256], w_fc1.at[k, 0:256, :])
-            start(stage, ref.at[base : base + 256, 256:512], w_fc1.at[k, 256:512, :])
-            start(stage, ref.at[base + 256 : base + 512, :], w_fc2.at[k])
-            stages.append(stage)
-    for c in range(4):
-        for r in range(4):
-            src = mine_ref.at[c * WROWS + 640 : c * WROWS + 768, r * 128 : (r + 1) * 128]
-            start(late, src, w_pool.at[r * 128 : (r + 1) * 128, c * 128 : (c + 1) * 128])
+        src = x_ref.at[pl.ds(c * ROWS + row, QUARTER), :]
+        early.append(start(src, x_rows.at[:, c * 128 : (c + 1) * 128]))
+    for s, c in sources:
+        early.append(start(refs[s].at[c * WROWS : c * WROWS + FC1, :], held.at[s, c, 0:FC1, :]))
+    for s, c in sources:
+        src = refs[s].at[c * WROWS + FC1 : (c + 1) * WROWS, :]
+        late.append(start(src, held.at[s, c, FC1:WROWS, :]))
+
+    def part(s, c, row, height, count):
+        pieces = [held[s, c, row + r * height : row + (r + 1) * height, :] for r in range(count)]
+        return jnp.concatenate(pieces, axis=1)
 
     wait(early)
-    mid = (x_rows[...].astype(F32) + matmul_tn(attn_ref[...], w_out[...])).astype(BF16)
-    mid = mid.astype(F32)
+    halves = (core, 1 - core)
+    attn = jnp.concatenate(
+        [attn_ref[pl.ds(pl.multiple_of(c * 128 + halves[s] * 64, 64), 64), :] for s, c in sources], axis=0
+    )
+    w_out = jnp.concatenate([part(s, c, 0, 64, 4) for s, c in sources], axis=0)
+    mid = (x_rows[...].astype(F32) + matmul_tn(attn, w_out)).astype(BF16).astype(F32)
     normed = normed_chunks([mid], [gain_ref[...]])[0]
-    total = mid
-    for k, stage in enumerate(stages):
-        wait(stage)
-        act = gelu(matmul(normed, w_fc1[k])).astype(BF16)
-        term = matmul(act, w_fc2[k])
-        summed = term if k == 0 else summed + term
-    block = (total + summed).astype(BF16)
-    wait(late)
-    lin = matmul(block, w_pool[...])
+    summed = None
+    for k, (s, c) in enumerate(sources):
+        wait([late[k]])
+        act = gelu(matmul(normed, part(s, c, FC1, C, 2))).astype(BF16)
+        term = matmul(act, part(s, c, FC2, HALF, 4))
+        summed = term if summed is None else summed + term
+    block = (mid + summed).astype(BF16)
+    left, right = block[:, :HALF].astype(F32), block[:, HALF:].astype(F32)
+    lin = None
+    for s in range(2):
+        mine = jnp.where(halves[s] == 0, left, right).astype(BF16)
+        w_pool = jnp.concatenate([held[s, c, POOL:WROWS, :] for c in range(4)], axis=1)
+        term = matmul(mine, w_pool)
+        lin = term if lin is None else lin + term
     high = lin.astype(BF16)
     low = (lin - high.astype(F32)).astype(BF16)
     member = one_hot(cell_ref[pl.ds(chan, 1), :] - (me - 1) * CELLS, 3 * CELLS)
@@ -312,15 +348,16 @@
     out_ref[...] = gelu(total / count_ref[...]).astype(BF16)
 
 
-def call(kernel, outs, args, scratch=(), anywhere=(), flops=0, bytes_accessed=0):
+def call(kernel, outs, args, scratch=(), in_hbm=(), out_hbm=(), limit=VMEM_LIMIT):
     vmem = pl.BlockSpec(memory_space=pltpu.VMEM)
+    hbm = pl.BlockSpec(memory_space=pltpu.HBM)
     return pl.pallas_call(
         kernel,
         out_shape=[jax.ShapeDtypeStruct(shape, dtype) for shape, dtype in outs],
-        in_specs=[pl.BlockSpec(memory_space=pl.ANY) if i in anywhere else vmem for i in range(len(args))],
-        out_specs=[vmem] * len(outs),
+        in_specs=[hbm if i in in_hbm else vmem for i in range(len(args))],
+        out_specs=[hbm if i in out_hbm else vmem for i in range(len(outs))],
         scratch_shapes=list(scratch),
-        compiler_params=pltpu.CompilerParams(vmem_limit_bytes=VMEM_LIMIT),
+        compiler_params=pltpu.CompilerParams(vmem_limit_bytes=limit),
     )(*args)
 
 
@@ -330,14 +367,24 @@
 
     own, up, down, swap, far, over, weights = call(
         pack_kernel,
-        [block(), block(2), block(2), block(), block(), block(), ((WROWS, C), BF16)],
+        [block(), block(2), block(2), block(), block(), block(), ((WROWS, LANES), BF16)],
         (feats, dest_pos.reshape(1, ROWS), cell_id.reshape(1, ROWS), w_out, w_fc1, w_fc2, w_pool),
+        scratch=[
+            pltpu.VMEM((ROWS, LANES), BF16),
+            pltpu.VMEM((1, ROWS), jnp.int32),
+            pltpu.VMEM((1, ROWS), jnp.int32),
+            pltpu.SemaphoreType.DMA((14,)),
+        ],
+        limit=ALL_VMEM,
+        in_hbm=range(7),
+        out_hbm=(6,),
     )
     gathered = lax.all_gather(weights, "chan", axis=0, tiled=True)
+    far = exchange(far, far_pair)
+    over = exchange(over, across)
     up = exchange(up, chip_up)
     down = exchange(down, chip_down)
-    far = exchange(far, far_pair)
-    over = exchange(over, across)
+    swap, far, over = lax.optimization_barrier((swap, far, over))
     swap = exchange(jnp.concatenate([swap, up[BLOCK:], down[BLOCK:]], axis=0), core_swap)
     ordered, count = call(
         unpack_kernel,
@@ -364,14 +411,12 @@
         mlp_kernel,
         [((N_CHAN * MESSAGE, LANES), BF16)],
         (attn, full, ln2_gain.reshape(1, C), cell_id.reshape(N_CHAN, QUARTER), gathered, others),
-        anywhere=(1, 4, 5),
+        limit=MOST_VMEM,
+        in_hbm=(4, 5),
         scratch=[
             pltpu.VMEM((QUARTER, C), BF16),
-            pltpu.VMEM((C, C), BF16),
-            pltpu.VMEM((8, C, HALF), BF16),
-            pltpu.VMEM((8, HALF, C), BF16),
-            pltpu.VMEM((C, C), BF16),
-            pltpu.SemaphoreType.DMA((48,)),
+            pltpu.VMEM((2, N_CHAN, WROWS, LANES), BF16),
+            pltpu.SemaphoreType.DMA((20,)),
         ],
     )
     got = lax.all_to_all(message, "chan", split_axis=0, concat_axis=0, tiled=True)

time: 161 us -> 155 us (0.963)
  local copies, waits for them, and re-layouts: 8.13 us -> 2.13 us
  Pallas kernels: 39.5 us -> 44.1 us
  blocking collectives: 41.7 us -> 38.3 us
  waiting for transfers between devices: 15.6 us -> 13.3 us
    unnamed x24 -> x12, local copies, waits for them, and re-layouts: 8.11 us -> 1.52 us
    pallas_call x6, Pallas kernels: 39.5 us -> 44.1 us  [call(): pl.pallas_call(kernel, out_shape=[jax.ShapeDtypeStruct(shape, dtype) for...]
    all_to_all x1, blocking collectives: 29.3 us -> 25 us  [body(): lax.all_to_all(ordered, 'chan', split_axis=0, concat_axis=0, tiled=True)]
  transfers between devices with their start and end apart: 10 -> 10, of which waited for: 5 -> 5; matrix products, arithmetic and copies ran while one was open for 0% -> 1% of each run, Pallas kernels for 19% -> 9%
where the time goes in v2:
time: 155 us; the launch traced here: 153 us
  Pallas kernels  44.1 us (28%)
  starting transfers between devices  39.7 us (26%)
  blocking collectives  38.3 us (25%)
  between operations  14.2 us (9%)
  waiting for transfers between devices  13.3 us (9%)
  local copies, waits for them, and re-layouts  2.13 us (1%)
    pallas_call x6, Pallas kernels, call(): pl.pallas_call(kernel, out_shape=[jax.ShapeDtypeStruct(shape, dtype) for...  44.1 us
    ppermute x8, starting transfers between devices, exchange(): return lax.ppermute(x, 'pts', [(i, partner(i)) for i in range(N_PTS)])  36.1 us
    all_to_all x1, blocking collectives, body(): lax.all_to_all(ordered, 'chan', split_axis=0, concat_axis=0, tiled=True)  25 us
    all_to_all x1, blocking collectives, body(): lax.all_to_all(message, 'chan', split_axis=0, concat_axis=0, tiled=True)  13.4 us
    ppermute x8, waiting for transfers between devices, exchange(): return lax.ppermute(x, 'pts', [(i, partner(i)) for i in range(N_PTS)])  7.31 us
    all_to_all x1, waiting for transfers between devices, body(): attn = lax.all_to_all(attn, 'chan', split_axis=0, concat_axis=0, tiled=True)  5.96 us
    all_to_all x1, starting transfers between devices, body(): attn = lax.all_to_all(attn, 'chan', split_axis=0, concat_axis=0, tiled=True)  3.64 us
  transfers between devices with their start and end apart: 10, of which 5 were waited for; matrix products, arithmetic and copies ran while one was open for 1% of the time, Pallas kernels for 9%

profile of v2, /device:TPU:1, one launch (start us, length us, event | category | flops | bytes accessed | tf_op | source)
XLA Modules:
  0.0 152.6 jit_solution(13708586140035251724)
XLA Ops:
  7.2 21.8 %shard_map.113 = (bf16[208,128]{1,0:T(8,128)(2,1)}, bf16[416,128]{1,0:T(8,128)(2,1)}, bf16[416,128]{1,0:T(8,128)(2,1)}, bf16[208,128]{1,0:T(8,128)(2,1)}, bf16[2...) custom-call(bf16[1024,128]{1,0:T(8,128)(2,1)} %feats_ref.1, s32[1,1024]{1,0:T(1,128)} %bitcast.18, ...), custom_call_target="tpu_custom_call" | custom-call | tf_op jit(solution)/shard_map/pallas_call | solution.py:354
  29.1 4.4 %collective-permute-start = (bf16[416,128]{1,0:T(8,128)(2,1)}, bf16[416,128]{1,0:T(8,128)(2,1)S(1)}, u32[]{:S(2)}, u32[]{:S(2)}) collective-permute-start(bf16[416,128]{1,0:T(8,128)(2,1)} %get-tuple-element.21), channel_id=1, source_target_pairs={{0,8},{4,12},{8,0},{12,4},{16,24},{20,28},{24,16},{28,20},{32,40},... | collective-permute-start | bytes 319496 | tf_op jit(solution)/shard_map/ppermute | solution.py:58
  33.5 12.4 %collective-permute-start.1 = (bf16[416,128]{1,0:T(8,128)(2,1)}, bf16[416,128]{1,0:T(8,128)(2,1)S(1)}, u32[]{:S(2)}, u32[]{:S(2)}) collective-permute-start(bf16[416,128]{1,0:T(8,128)(2,1)} %get-tuple-element.22), channel_id=1, source_target_pairs={{0,504},{4,508},{8,16},{12,20},{16,8},{20,12},{24,32},{28,36},{32,... | collective-permute-start | bytes 319496 | tf_op jit(solution)/shard_map/ppermute | solution.py:58
  45.9 1.9 %collective-permute-start.2 = (bf16[208,128]{1,0:T(8,128)(2,1)}, bf16[208,128]{1,0:T(8,128)(2,1)S(1)}, u32[]{:S(2)}, u32[]{:S(2)}) collective-permute-start(bf16[208,128]{1,0:T(8,128)(2,1)} %get-tuple-element.24), channel_id=1, source_target_pairs={{0,500},{4,16},{8,508},{12,24},{16,4},{20,32},{24,12},{28,40},{32,... | collective-permute-start | bytes 159752 | tf_op jit(solution)/shard_map/ppermute | solution.py:58
  47.8 2.4 %collective-permute-start.3 = (bf16[208,128]{1,0:T(8,128)(2,1)}, bf16[208,128]{1,0:T(8,128)(2,1)S(1)}, u32[]{:S(2)}, u32[]{:S(2)}) collective-permute-start(bf16[208,128]{1,0:T(8,128)(2,1)} %get-tuple-element.25), channel_id=1, source_target_pairs={{0,256},{4,260},{8,264},{12,268},{16,272},{20,276},{24,280},{28,28... | collective-permute-start | bytes 159752 | tf_op jit(solution)/shard_map/ppermute | solution.py:58
  50.3 2.2 %collective-permute-done.2.far_ref = bf16[208,128]{1,0:T(8,128)(2,1)S(1)} collective-permute-done((bf16[208,128]{1,0:T(8,128)(2,1)}, bf16[208,128]{1,0:T(8,128)(2,1)S(1)}, u32[]{:S(2)}, u32[]{:S(2)}) %collective-permute-start.2) | collective-permute-done | bytes 53280 | tf_op jit(solution)/shard_map/ppermute | solution.py:58
  52.5 2.0 %collective-permute-done.3.across_ref = bf16[208,128]{1,0:T(8,128)(2,1)S(1)} collective-permute-done((bf16[208,128]{1,0:T(8,128)(2,1)}, bf16[208,128]{1,0:T(8,128)(2,1)S(1)}, u32[]{:S(2)}, u32[]{:S(2)}) %collective-permute-start.3) | collective-permute-done | bytes 53280 | tf_op jit(solution)/shard_map/ppermute | solution.py:58
  54.5 0.8 pad_maximum_fusion
  55.3 5.1 %collective-permute-start.4 = (bf16[624,128]{1,0:T(8,128)(2,1)S(1)}, bf16[624,128]{1,0:T(8,128)(2,1)S(1)}, u32[]{:S(2)}, u32[]{:S(2)}) collective-permute-start(bf16[624,128]{1,0:T(8,128)(2,1)S(1)} %pad_maximum_fusion), channel_id=1, source_target_pairs={{0,4},{4,0},{8,12},{12,8},{16,20},{20,16},{24,28},{28,24},{32,36},... | collective-permute-start | bytes 479240 | tf_op jit(solution)/shard_map/ppermute | solution.py:58
  60.4 1.0 collective-permute-done.4.swap_ref
  61.4 0.8 copy-done.2
  62.2 1.0 shard_map.114
  63.2 25.0 %all_to_all.33 = bf16[4,1024,128]{2,1,0:T(8,128)(2,1)S(1)} all-to-all(bf16[4,1024,128]{2,1,0:T(8,128)(2,1)S(1)} %bitcast.13), channel_id=1, replica_groups=mesh['pts'=128,'chan'=4] {'chan'}, dimensions={0} | all-to-all | bytes 2097152 | tf_op jit(solution)/shard_map/all_to_all | solution.py:395
  88.2 12.6 %shard_map.115 = bf16[512,256]{1,0:T(8,128)(2,1)} custom-call(bf16[4096,128]{1,0:T(8,128)(2,1)S(1)} %bitcast.10, f32[1,512]{1,0:T(1,128)S(1)} %bitcast.14, bf16[3,512,128]{2,1,0:T(8,128)(2,1)S(1)} %copy-done.1), custom_call_target="tpu_custom_call" | custom-call | tf_op jit(solution)/shard_map/pallas_call | solution.py:354
  100.8 3.0 %collective-permute-start.5 = (bf16[10240,128]{1,0:T(8,128)(2,1)}, bf16[10240,128]{1,0:T(8,128)(2,1)}, u32[]{:S(2)}, u32[]{:S(2)}) collective-permute-start(bf16[10240,128]{1,0:T(8,128)(2,1)} %all-gather.2.cloned.1.call-done.mine_ref), channel_id=1, source_target_pairs={{0,4},{4,0},{8,12},{12,8},{16,20},{20,16},{24,28},{28,24},{32,36},... | collective-permute-start | bytes 7864328 | tf_op jit(solution)/shard_map/ppermute | solution.py:58
  103.8 3.6 %all-to-all-start.1 = ((bf16[4,128,256]{2,1,0:T(8,128)(2,1)}), bf16[4,128,256]{2,1,0:T(8,128)(2,1)S(1)}, u32[]{:S(2)}, u32[]{:S(2)}) async-start(bf16[4,128,256]{2,1,0:T(8,128)(2,1)} %bitcast.5), calls=%async_computation.1 | async-start | bytes 524288 | tf_op jit(solution)/shard_map/all_to_all | solution.py:409
  108.1 6.0 %all-to-all-done.1 = bf16[4,128,256]{2,1,0:T(8,128)(2,1)S(1)} async-done(((bf16[4,128,256]{2,1,0:T(8,128)(2,1)}), bf16[4,128,256]{2,1,0:T(8,128)(2,1)S(1)}, u32[]{:S(2)}, u32[]{:S(2)}) %all-to-all-start.1) | async-done | bytes 262176 | tf_op jit(solution)/shard_map/all_to_all | solution.py:409
  114.0 0.7 copy-done.4
  114.7 7.2 %shard_map.116 = bf16[2560,128]{1,0:T(8,128)(2,1)} custom-call(bf16[512,256]{1,0:T(8,128)(2,1)} %bitcast.16, bf16[4096,128]{1,0:T(8,128)(2,1)} %bitcast.11, f32[1,512]{1,0:T(1,128)} %bitcast.19, s32[4,256]{1,0:T(4,128)} %reshape.29.cell_ref, bf16[10240,128]{1,0:T(8,128)(2,1)} %all-gather.2.cloned.1.call-done.mine_ref, ...), custom_call_target="tpu_custom_call" | custom-call | tf_op jit(solution)/shard_map/pallas_call | solution.py:354
  121.9 13.4 %all_to_all.34 = bf16[4,640,128]{2,1,0:T(8,128)(2,1)S(1)} all-to-all(bf16[4,640,128]{2,1,0:T(8,128)(2,1)} %bitcast.15), channel_id=1, replica_groups=mesh['pts'=128,'chan'=4] {'chan'}, dimensions={0} | all-to-all | bytes 1310720 | tf_op jit(solution)/shard_map/all_to_all | solution.py:422
  135.3 0.8 shard_map.117
  136.1 3.8 %collective-permute-start.6 = (bf16[128,128]{1,0:T(8,128)(2,1)S(1)}, bf16[128,128]{1,0:T(8,128)(2,1)S(1)}, u32[]{:S(2)}, u32[]{:S(2)}) collective-permute-start(bf16[128,128]{1,0:T(8,128)(2,1)S(1)} %get-tuple-element.35), channel_id=1, source_target_pairs={{0,4},{4,0},{8,12},{12,8},{16,20},{20,16},{24,28},{28,24},{32,36},... | collective-permute-start | bytes 98312 | tf_op jit(solution)/shard_map/ppermute | solution.py:58
  139.9 3.1 %collective-permute-start.7 = (bf16[128,128]{1,0:T(8,128)(2,1)S(1)}, bf16[128,128]{1,0:T(8,128)(2,1)S(1)}, u32[]{:S(2)}, u32[]{:S(2)}) collective-permute-start(bf16[128,128]{1,0:T(8,128)(2,1)S(1)} %get-tuple-element.36), channel_id=1, source_target_pairs={{0,508},{4,8},{8,4},{12,16},{16,12},{20,24},{24,20},{28,32},{32,28... | collective-permute-start | bytes 98312 | tf_op jit(solution)/shard_map/ppermute | solution.py:58
  143.0 2.1 %collective-permute-done.7.next_ref = bf16[128,128]{1,0:T(8,128)(2,1)S(1)} collective-permute-done((bf16[128,128]{1,0:T(8,128)(2,1)S(1)}, bf16[128,128]{1,0:T(8,128)(2,1)S(1)}, u32[]{:S(2)}, u32[]{:S(2)}) %collective-permute-start.7) | collective-permute-done | bytes 32800 | tf_op jit(solution)/shard_map/ppermute | solution.py:58
  (21 shorter events, 1.3 us)
Async XLA Ops:
  7.2 93.7 %all-gather.2.cloned.1.call-start = ((), (), s32[]{:S(2)}) async-start(), calls=%async_computation.3 | async-start | bytes 3276800 | tf_op jit(solution)/shard_map/all_gather | solution.py:382
  7.2 81.0 %copy-start.1 = (bf16[3,512,128]{2,1,0:T(8,128)(2,1)S(1)}, bf16[3,512,128]{2,1,0:T(8,128)(2,1)}, u32[]{:S(2)}) copy-start(bf16[3,512,128]{2,1,0:T(8,128)(2,1)} %w_ref.1) | copy-start | bytes 1179652
  7.2 81.0 %copy-start.3 = (f32[512]{0:T(512)S(1)}, f32[512]{0:T(512)}, u32[]{:S(2)}) copy-start(f32[512]{0:T(512)} %param.13) | copy-start | bytes 6148
  29.1 25.3 %collective-permute-start = (bf16[416,128]{1,0:T(8,128)(2,1)}, bf16[416,128]{1,0:T(8,128)(2,1)S(1)}, u32[]{:S(2)}, u32[]{:S(2)}) collective-permute-start(bf16[416,128]{1,0:T(8,128)(2,1)} %get-tuple-element.21), channel_id=1, source_target_pairs={{0,8},{4,12},{8,0},{12,4},{16,24},{20,28},{24,16},{28,20},{32,40},... | collective-permute-start | bytes 319496 | tf_op jit(solution)/shard_map/ppermute | solution.py:58
  33.5 20.9 %collective-permute-start.1 = (bf16[416,128]{1,0:T(8,128)(2,1)}, bf16[416,128]{1,0:T(8,128)(2,1)S(1)}, u32[]{:S(2)}, u32[]{:S(2)}) collective-permute-start(bf16[416,128]{1,0:T(8,128)(2,1)} %get-tuple-element.22), channel_id=1, source_target_pairs={{0,504},{4,508},{8,16},{12,20},{16,8},{20,12},{24,32},{28,36},{32,... | collective-permute-start | bytes 319496 | tf_op jit(solution)/shard_map/ppermute | solution.py:58
  45.9 6.6 %collective-permute-start.2 = (bf16[208,128]{1,0:T(8,128)(2,1)}, bf16[208,128]{1,0:T(8,128)(2,1)S(1)}, u32[]{:S(2)}, u32[]{:S(2)}) collective-permute-start(bf16[208,128]{1,0:T(8,128)(2,1)} %get-tuple-element.24), channel_id=1, source_target_pairs={{0,500},{4,16},{8,508},{12,24},{16,4},{20,32},{24,12},{28,40},{32,... | collective-permute-start | bytes 159752 | tf_op jit(solution)/shard_map/ppermute | solution.py:58
  47.8 6.6 %collective-permute-start.3 = (bf16[208,128]{1,0:T(8,128)(2,1)}, bf16[208,128]{1,0:T(8,128)(2,1)S(1)}, u32[]{:S(2)}, u32[]{:S(2)}) collective-permute-start(bf16[208,128]{1,0:T(8,128)(2,1)} %get-tuple-element.25), channel_id=1, source_target_pairs={{0,256},{4,260},{8,264},{12,268},{16,272},{20,276},{24,280},{28,28... | collective-permute-start | bytes 159752 | tf_op jit(solution)/shard_map/ppermute | solution.py:58
  54.4 53.0 %copy-start.5 = (s32[1024]{0:T(1024)S(1)}, s32[1024]{0:T(1024)}, u32[]{:S(2)}) copy-start(s32[1024]{0:T(1024)} %param.12) | copy-start | bytes 12292
  55.3 6.1 %collective-permute-start.4 = (bf16[624,128]{1,0:T(8,128)(2,1)S(1)}, bf16[624,128]{1,0:T(8,128)(2,1)S(1)}, u32[]{:S(2)}, u32[]{:S(2)}) collective-permute-start(bf16[624,128]{1,0:T(8,128)(2,1)S(1)} %pad_maximum_fusion), channel_id=1, source_target_pairs={{0,4},{4,0},{8,12},{12,8},{16,20},{20,16},{24,28},{28,24},{32,36},... | collective-permute-start | bytes 479240 | tf_op jit(solution)/shard_map/ppermute | solution.py:58
  61.4 0.8 copy-start.2
  88.2 25.8 %copy-start = (bf16[4,1024,128]{2,1,0:T(8,128)(2,1)}, bf16[4,1024,128]{2,1,0:T(8,128)(2,1)S(1)}, u32[]{:S(2)}) copy-start(bf16[4,1024,128]{2,1,0:T(8,128)(2,1)S(1)} %all_to_all.33) | copy-start | bytes 3145732
  100.8 13.2 %collective-permute-start.5 = (bf16[10240,128]{1,0:T(8,128)(2,1)}, bf16[10240,128]{1,0:T(8,128)(2,1)}, u32[]{:S(2)}, u32[]{:S(2)}) collective-permute-start(bf16[10240,128]{1,0:T(8,128)(2,1)} %all-gather.2.cloned.1.call-done.mine_ref), channel_id=1, source_target_pairs={{0,4},{4,0},{8,12},{12,8},{16,20},{20,16},{24,28},{28,24},{32,36},... | collective-permute-start | bytes 7864328 | tf_op jit(solution)/shard_map/ppermute | solution.py:58
  103.8 10.2 %all-to-all-start.1 = ((bf16[4,128,256]{2,1,0:T(8,128)(2,1)}), bf16[4,128,256]{2,1,0:T(8,128)(2,1)S(1)}, u32[]{:S(2)}, u32[]{:S(2)}) async-start(bf16[4,128,256]{2,1,0:T(8,128)(2,1)} %bitcast.5), calls=%async_computation.1 | async-start | bytes 524288 | tf_op jit(solution)/shard_map/all_to_all | solution.py:409
  114.0 0.7 copy-start.4
  136.1 6.9 %collective-permute-start.6 = (bf16[128,128]{1,0:T(8,128)(2,1)S(1)}, bf16[128,128]{1,0:T(8,128)(2,1)S(1)}, u32[]{:S(2)}, u32[]{:S(2)}) collective-permute-start(bf16[128,128]{1,0:T(8,128)(2,1)S(1)} %get-tuple-element.35), channel_id=1, source_target_pairs={{0,4},{4,0},{8,12},{12,8},{16,20},{20,16},{24,28},{28,24},{32,36},... | collective-permute-start | bytes 98312 | tf_op jit(solution)/shard_map/ppermute | solution.py:58
  139.9 5.2 %collective-permute-start.7 = (bf16[128,128]{1,0:T(8,128)(2,1)S(1)}, bf16[128,128]{1,0:T(8,128)(2,1)S(1)}, u32[]{:S(2)}, u32[]{:S(2)}) collective-permute-start(bf16[128,128]{1,0:T(8,128)(2,1)S(1)} %get-tuple-element.36), channel_id=1, source_target_pairs={{0,508},{4,8},{8,4},{12,16},{16,12},{20,24},{24,20},{28,32},{32,28... | collective-permute-start | bytes 98312 | tf_op jit(solution)/shard_map/ppermute | solution.py:58
Sparse Core Ops, SparseCore 0:
  29.2 58.0 all-gather.1

commit v3 on v2

--- a/solution.py
+++ b/solution.py
@@ -24,7 +24,7 @@
 HALF = 256
 STEP = 512
 FC1, FC2, POOL, WROWS = 256, 1280, 2304, 2560
-MESSAGE = QUARTER + 3 * CELLS
+MESSAGE = QUARTER + CELLS
 VMEM_LIMIT = 48 * 1024 * 1024
 MOST_VMEM = 61 * 1024 * 1024 + 512 * 1024
 ALL_VMEM = 63 * 1024 * 1024 + 512 * 1024
@@ -160,7 +160,7 @@
 
 def pack_kernel(
     feats_ref, dest_ref, cell_ref, w_out_ref, w_fc1_ref, w_fc2_ref, w_pool_ref,
-    own_ref, up_ref, down_ref, swap_ref, far_ref, across_ref, weights_ref,
+    up_ref, down_ref, swap_ref, far_ref, across_ref, weights_ref,
     feats_here, dest_here, cell_here, sems,
 ):
     me = lax.axis_index("pts")
@@ -200,7 +200,7 @@
     rank = jnp.sum(ranks, axis=0, keepdims=True).astype(jnp.int32)
     slot = jnp.where(rank < 128, kind * 128 + rank, 1024 - 128 + kind * 64 + rank)
     homes = [
-        (own_ref, 0), (up_ref, 0), (up_ref, BLOCK), (down_ref, 0),
+        (swap_ref, BLOCK), (up_ref, 0), (up_ref, BLOCK), (down_ref, 0),
         (down_ref, BLOCK), (swap_ref, 0), (far_ref, 0), (across_ref, 0),
     ]
     blocks = [home + (offset,) for home, offset in zip(homes, offsets)]
@@ -211,10 +211,10 @@
     wait(weight_copies)
 
 
-def unpack_kernel(own_ref, up_ref, down_ref, far_ref, across_ref, swap_ref, out_ref, count_ref, held):
+def unpack_kernel(sent_ref, up_ref, down_ref, far_ref, across_ref, swap_ref, out_ref, count_ref, held):
     homes = [
-        (own_ref, 0), (up_ref, 0), (swap_ref, BLOCK), (down_ref, 0),
-        (swap_ref, 2 * BLOCK), (swap_ref, 0), (far_ref, 0), (across_ref, 0),
+        (sent_ref, BLOCK), (up_ref, 0), (swap_ref, 2 * BLOCK), (down_ref, 0),
+        (swap_ref, 3 * BLOCK), (swap_ref, 0), (far_ref, 0), (across_ref, 0),
     ]
     firsts, seconds = [], []
     count = jnp.zeros((1, 128), F32)
@@ -267,7 +267,8 @@
 
 
 def mlp_kernel(
-    attn_ref, x_ref, gain_ref, cell_ref, mine_ref, other_ref, out_ref, x_rows, held, sems,
+    attn_ref, x_ref, gain_ref, cell_ref, mine_ref, other_ref,
+    block_ref, own_ref, swap_ref, next_ref, x_rows, held, sems,
 ):
     chan = lax.axis_index("chan")
     me = lax.axis_index("pts")
@@ -314,20 +315,9 @@
         lin = term if lin is None else lin + term
     high = lin.astype(BF16)
     low = (lin - high.astype(F32)).astype(BF16)
-    member = one_hot(cell_ref[pl.ds(chan, 1), :] - (me - 1) * CELLS, 3 * CELLS)
-    sums = (matmul(member, high) + matmul(member, low)).astype(BF16)
-    for c in range(4):
-        cols = slice(c * 128, (c + 1) * 128)
-        out_ref[c * MESSAGE : c * MESSAGE + QUARTER, :] = block[:, cols]
-        out_ref[c * MESSAGE + QUARTER : (c + 1) * MESSAGE, :] = sums[:, cols]
-
-
-def gather_kernel(got_ref, block_ref, own_ref, swap_ref, next_ref):
-    core = lax.rem(lax.axis_index("pts"), 2)
-    sums = jnp.zeros((3 * CELLS, LANES), F32)
-    for c in range(4):
-        block_ref[c * QUARTER : (c + 1) * QUARTER, :] = got_ref[c * MESSAGE : c * MESSAGE + QUARTER, :]
-        sums = sums + got_ref[c * MESSAGE + QUARTER : (c + 1) * MESSAGE, :].astype(F32)
+    member = one_hot(cell_ref[:, pl.ds(row, QUARTER)] - (me - 1) * CELLS, 3 * CELLS)
+    sums = matmul(member, high) + matmul(member, low)
+    block_ref[...] = block
     own_ref[...] = sums[CELLS : 2 * CELLS]
     before = sums[:CELLS].astype(BF16)
     after = sums[2 * CELLS :].astype(BF16)
@@ -343,8 +333,20 @@
         next_ref[...] = after
 
 
-def pool_kernel(own_ref, swap_ref, next_ref, count_ref, out_ref):
-    total = own_ref[...] + swap_ref[...].astype(F32) + next_ref[...].astype(F32)
+def message_kernel(block_ref, own_ref, swap_ref, next_ref, out_ref):
+    sums = own_ref[...] + swap_ref[...].astype(F32) + next_ref[...].astype(F32)
+    sums = sums.astype(BF16)
+    for c in range(N_CHAN):
+        cols = slice(c * 128, (c + 1) * 128)
+        out_ref[c * MESSAGE : c * MESSAGE + QUARTER, :] = block_ref[:, cols]
+        out_ref[c * MESSAGE + QUARTER : (c + 1) * MESSAGE, :] = sums[:, cols]
+
+
+def pool_kernel(got_ref, count_ref, block_ref, out_ref):
+    total = jnp.zeros((CELLS, LANES), F32)
+    for c in range(N_CHAN):
+        block_ref[c * QUARTER : (c + 1) * QUARTER, :] = got_ref[c * MESSAGE : c * MESSAGE + QUARTER, :]
+        total = total + got_ref[c * MESSAGE + QUARTER : (c + 1) * MESSAGE, :].astype(F32)
     out_ref[...] = gelu(total / count_ref[...]).astype(BF16)
 
 
@@ -365,9 +367,9 @@
     def block(count=1):
         return ((count * BLOCK, LANES), BF16)
 
-    own, up, down, swap, far, over, weights = call(
+    up, down, swap, far, over, weights = call(
         pack_kernel,
-        [block(), block(2), block(2), block(), block(), block(), ((WROWS, LANES), BF16)],
+        [block(2), block(2), block(2), block(), block(), ((WROWS, LANES), BF16)],
         (feats, dest_pos.reshape(1, ROWS), cell_id.reshape(1, ROWS), w_out, w_fc1, w_fc2, w_pool),
         scratch=[
             pltpu.VMEM((ROWS, LANES), BF16),
@@ -377,7 +379,6 @@
         ],
         limit=ALL_VMEM,
         in_hbm=range(7),
-        out_hbm=(6,),
     )
     gathered = lax.all_gather(weights, "chan", axis=0, tiled=True)
     far = exchange(far, far_pair)
@@ -385,11 +386,12 @@
     up = exchange(up, chip_up)
     down = exchange(down, chip_down)
     swap, far, over = lax.optimization_barrier((swap, far, over))
-    swap = exchange(jnp.concatenate([swap, up[BLOCK:], down[BLOCK:]], axis=0), core_swap)
+    sent = jnp.concatenate([swap, up[BLOCK:], down[BLOCK:]], axis=0)
+    swap = exchange(sent, core_swap)
     ordered, count = call(
         unpack_kernel,
         [((N_CHAN * ROWS, LANES), BF16), ((128, 128), F32)],
-        (own, up, down, far, over, swap),
+        (sent, up, down, far, over, swap),
         scratch=[pltpu.VMEM((SLOTS, LANES), BF16)],
     )
     full = lax.all_to_all(ordered, "chan", split_axis=0, concat_axis=0, tiled=True)
@@ -407,10 +409,11 @@
     attn, gathered = lax.optimization_barrier((attn, gathered))
     others = exchange(gathered, core_swap)
     attn = lax.all_to_all(attn, "chan", split_axis=0, concat_axis=0, tiled=True)
-    (message,) = call(
+    cell_sum = ((CELLS, C), BF16)
+    rows, mine, for_swap, for_next = call(
         mlp_kernel,
-        [((N_CHAN * MESSAGE, LANES), BF16)],
-        (attn, full, ln2_gain.reshape(1, C), cell_id.reshape(N_CHAN, QUARTER), gathered, others),
+        [((QUARTER, C), BF16), ((CELLS, C), F32), cell_sum, cell_sum],
+        (attn, full, ln2_gain.reshape(1, C), cell_id.reshape(1, ROWS), gathered, others),
         limit=MOST_VMEM,
         in_hbm=(4, 5),
         scratch=[
@@ -419,16 +422,17 @@
             pltpu.SemaphoreType.DMA((20,)),
         ],
     )
-    got = lax.all_to_all(message, "chan", split_axis=0, concat_axis=0, tiled=True)
-    cell_sum = ((CELLS, LANES), BF16)
-    block_out, mine, for_swap, for_next = call(
-        gather_kernel,
-        [((ROWS, LANES), BF16), ((CELLS, LANES), F32), cell_sum, cell_sum],
-        (got,),
-    )
     from_swap = exchange(for_swap, core_swap)
     from_next = exchange(for_next, next_pair)
-    (pooled,) = call(pool_kernel, [cell_sum], (mine, from_swap, from_next, count))
+    (message,) = call(
+        message_kernel,
+        [((N_CHAN * MESSAGE, LANES), BF16)],
+        (rows, mine, from_swap, from_next),
+    )
+    got = lax.all_to_all(message, "chan", split_axis=0, concat_axis=0, tiled=True)
+    block_out, pooled = call(
+        pool_kernel, [((ROWS, LANES), BF16), ((CELLS, LANES), BF16)], (got, count)
+    )
     return (block_out, pooled)
 
 

time: 155 us -> 134 us (0.86)
  the two profiles are of different devices: /device:TPU:1 before, /device:TPU:8 now
where the time goes in v3:
time: 134 us; the launch traced here: 133 us
  blocking collectives  45.7 us (34%)
  starting transfers between devices  35.1 us (26%)
  Pallas kernels  25.4 us (19%)
  between operations  14.2 us (11%)
  waiting for transfers between devices  9.79 us (7%)
  local copies, waits for them, and re-layouts  1.92 us (1%)
    ppermute x8, starting transfers between devices, exchange(): return lax.ppermute(x, 'pts', [(i, partner(i)) for i in range(N_PTS)])  35.1 us
    all_to_all x1, blocking collectives, body(): lax.all_to_all(ordered, 'chan', split_axis=0, concat_axis=0, tiled=True)  25.7 us
    pallas_call x6, Pallas kernels, call(): pl.pallas_call(kernel, out_shape=[jax.ShapeDtypeStruct(shape, dtype) for...  25.4 us
    all_to_all x1, blocking collectives, body(): attn = lax.all_to_all(attn, 'chan', split_axis=0, concat_axis=0, tiled=True)  10.3 us
    all_to_all x1, blocking collectives, body(): lax.all_to_all(message, 'chan', split_axis=0, concat_axis=0, tiled=True)  9.77 us
    ppermute x8, waiting for transfers between devices, exchange(): return lax.ppermute(x, 'pts', [(i, partner(i)) for i in range(N_PTS)])  9.77 us
  transfers between devices with their start and end apart: 9, of which 4 were waited for; matrix products, arithmetic and copies ran while one was open for 1% of the time, Pallas kernels for 10%

profile of v3, /device:TPU:8, one launch (start us, length us, event | category | flops | bytes accessed | tf_op | source)
XLA Modules:
  0.0 133.1 jit_solution(11318651372940685207)
XLA Ops:
  7.2 4.4 %shard_map.113 = (bf16[416,128]{1,0:T(8,128)(2,1)}, bf16[416,128]{1,0:T(8,128)(2,1)}, bf16[416,128]{1,0:T(8,128)(2,1)}, bf16[208,128]{1,0:T(8,128)(2,1)}, bf16[2...) custom-call(bf16[1024,128]{1,0:T(8,128)(2,1)} %feats_ref.1, s32[1,1024]{1,0:T(1,128)} %bitcast.20, s32[1,1024]{1,0:T(1,128)} %bitcast.18, ...), custom_call_target="tpu_custom_call" | custom-call | tf_op jit(solution)/shard_map/pallas_call | solution.py:356
  11.7 3.8 %collective-permute-start.2 = (bf16[416,128]{1,0:T(8,128)(2,1)}, bf16[416,128]{1,0:T(8,128)(2,1)S(1)}, u32[]{:S(2)}, u32[]{:S(2)}) collective-permute-start(bf16[416,128]{1,0:T(8,128)(2,1)} %get-tuple-element.23), channel_id=1, source_target_pairs={{0,8},{4,12},{8,0},{12,4},{16,24},{20,28},{24,16},{28,20},{32,40},... | collective-permute-start | bytes 319496 | tf_op jit(solution)/shard_map/ppermute | solution.py:58
  15.5 12.7 %collective-permute-start.3 = (bf16[416,128]{1,0:T(8,128)(2,1)}, bf16[416,128]{1,0:T(8,128)(2,1)S(1)}, u32[]{:S(2)}, u32[]{:S(2)}) collective-permute-start(bf16[416,128]{1,0:T(8,128)(2,1)} %get-tuple-element.24), channel_id=1, source_target_pairs={{0,504},{4,508},{8,16},{12,20},{16,8},{20,12},{24,32},{28,36},{32,... | collective-permute-start | bytes 319496 | tf_op jit(solution)/shard_map/ppermute | solution.py:58
  28.2 2.2 %collective-permute-start = (bf16[208,128]{1,0:T(8,128)(2,1)}, bf16[208,128]{1,0:T(8,128)(2,1)S(1)}, u32[]{:S(2)}, u32[]{:S(2)}) collective-permute-start(bf16[208,128]{1,0:T(8,128)(2,1)} %get-tuple-element.20), channel_id=1, source_target_pairs={{0,500},{4,16},{8,508},{12,24},{16,4},{20,32},{24,12},{28,40},{32,... | collective-permute-start | bytes 159752 | tf_op jit(solution)/shard_map/ppermute | solution.py:58
  30.4 2.7 %collective-permute-start.1 = (bf16[208,128]{1,0:T(8,128)(2,1)}, bf16[208,128]{1,0:T(8,128)(2,1)S(1)}, u32[]{:S(2)}, u32[]{:S(2)}) collective-permute-start(bf16[208,128]{1,0:T(8,128)(2,1)} %get-tuple-element.21), channel_id=1, source_target_pairs={{0,256},{4,260},{8,264},{12,268},{16,272},{20,276},{24,280},{28,28... | collective-permute-start | bytes 159752 | tf_op jit(solution)/shard_map/ppermute | solution.py:58
  33.2 5.4 %collective-permute-done.far_ref = bf16[208,128]{1,0:T(8,128)(2,1)S(1)} collective-permute-done((bf16[208,128]{1,0:T(8,128)(2,1)}, bf16[208,128]{1,0:T(8,128)(2,1)S(1)}, u32[]{:S(2)}, u32[]{:S(2)}) %collective-permute-start) | collective-permute-done | bytes 53280 | tf_op jit(solution)/shard_map/ppermute | solution.py:58
  38.5 0.1 collective-permute-done.1.across_ref
  38.7 0.9 pad_maximum_fusion.sent_ref
  39.6 1.9 %collective-permute-start.4 = (bf16[832,128]{1,0:T(8,128)(2,1)S(1)}, bf16[832,128]{1,0:T(8,128)(2,1)S(1)}, u32[]{:S(2)}, u32[]{:S(2)}) collective-permute-start(bf16[832,128]{1,0:T(8,128)(2,1)S(1)} %pad_maximum_fusion.sent_ref), channel_id=1, source_target_pairs={{0,4},{4,0},{8,12},{12,8},{16,20},{20,16},{24,28},{28,24},{32,36},... | collective-permute-start | bytes 638984 | tf_op jit(solution)/shard_map/ppermute | solution.py:58
  41.5 1.4 %collective-permute-done.4.swap_ref = bf16[832,128]{1,0:T(8,128)(2,1)S(1)} collective-permute-done((bf16[832,128]{1,0:T(8,128)(2,1)S(1)}, bf16[832,128]{1,0:T(8,128)(2,1)S(1)}, u32[]{:S(2)}, u32[]{:S(2)}) %collective-permute-start.4) | collective-permute-done | bytes 213024 | tf_op jit(solution)/shard_map/ppermute | solution.py:58
  43.0 1.0 shard_map.114
  44.0 25.7 %all_to_all.33 = bf16[4,1024,128]{2,1,0:T(8,128)(2,1)S(1)} all-to-all(bf16[4,1024,128]{2,1,0:T(8,128)(2,1)S(1)} %bitcast.14), channel_id=1, replica_groups=mesh['pts'=128,'chan'=4] {'chan'}, dimensions={0} | all-to-all | bytes 2097152 | tf_op jit(solution)/shard_map/all_to_all | solution.py:397
  69.7 11.9 %shard_map.115 = bf16[512,256]{1,0:T(8,128)(2,1)S(1)} custom-call(bf16[4096,128]{1,0:T(8,128)(2,1)S(1)} %bitcast.10, f32[1,512]{1,0:T(1,128)S(1)} %bitcast.16, bf16[3,512,128]{2,1,0:T(8,128)(2,1)S(1)} %copy-done.1), custom_call_target="tpu_custom_call" | custom-call | tf_op jit(solution)/shard_map/pallas_call | solution.py:356
  81.6 1.9 %collective-permute-start.5 = (bf16[10240,128]{1,0:T(8,128)(2,1)}, bf16[10240,128]{1,0:T(8,128)(2,1)}, u32[]{:S(2)}, u32[]{:S(2)}) collective-permute-start(bf16[10240,128]{1,0:T(8,128)(2,1)} %all-gather.2.cloned.1.call-done.mine_ref), channel_id=1, source_target_pairs={{0,4},{4,0},{8,12},{12,8},{16,20},{20,16},{24,28},{28,24},{32,36},... | collective-permute-start | bytes 7864328 | tf_op jit(solution)/shard_map/ppermute | solution.py:58
  83.6 10.3 %all_to_all.34 = bf16[4,128,256]{2,1,0:T(8,128)(2,1)} all-to-all(bf16[4,128,256]{2,1,0:T(8,128)(2,1)S(1)} %bitcast.15), channel_id=1, replica_groups=mesh['pts'=128,'chan'=4] {'chan'}, dimensions={0} | all-to-all | bytes 524288 | tf_op jit(solution)/shard_map/all_to_all | solution.py:411
  93.8 7.3 %shard_map.116 = (bf16[256,512]{1,0:T(8,128)(2,1)}, f32[128,512]{1,0:T(8,128)}, bf16[128,512]{1,0:T(8,128)(2,1)}, bf16[128,512]{1,0:T(8,128)(2,1)}) custom-call(bf16[512,256]{1,0:T(8,128)(2,1)} %bitcast.17, bf16[4096,128]{1,0:T(8,128)(2,1)} %bitcast.11, f32[1,512]{1,0:T(1,128)} %bitcast.21, s32[1,1024]{1,0:T(1,128)} %bitcast.19, ...), custom_call_target="tpu_custom_call" | custom-call | tf_op jit(solution)/shard_map/pallas_call | solution.py:356
  101.1 1.9 %collective-permute-start.6 = (bf16[128,512]{1,0:T(8,128)(2,1)}, bf16[128,512]{1,0:T(8,128)(2,1)S(1)}, u32[]{:S(2)}, u32[]{:S(2)}) collective-permute-start(bf16[128,512]{1,0:T(8,128)(2,1)} %get-tuple-element.33), channel_id=1, source_target_pairs={{0,4},{4,0},{8,12},{12,8},{16,20},{20,16},{24,28},{28,24},{32,36},... | collective-permute-start | bytes 393224 | tf_op jit(solution)/shard_map/ppermute | solution.py:58
  103.0 7.9 %collective-permute-start.7 = (bf16[128,512]{1,0:T(8,128)(2,1)}, bf16[128,512]{1,0:T(8,128)(2,1)S(1)}, u32[]{:S(2)}, u32[]{:S(2)}) collective-permute-start(bf16[128,512]{1,0:T(8,128)(2,1)} %get-tuple-element.34), channel_id=1, source_target_pairs={{0,508},{4,8},{8,4},{12,16},{16,12},{20,24},{24,20},{28,32},{32,28... | collective-permute-start | bytes 393224 | tf_op jit(solution)/shard_map/ppermute | solution.py:58
  110.9 2.8 %collective-permute-done.7.next_ref = bf16[128,512]{1,0:T(8,128)(2,1)S(1)} collective-permute-done((bf16[128,512]{1,0:T(8,128)(2,1)}, bf16[128,512]{1,0:T(8,128)(2,1)S(1)}, u32[]{:S(2)}, u32[]{:S(2)}) %collective-permute-start.7) | collective-permute-done | bytes 131104 | tf_op jit(solution)/shard_map/ppermute | solution.py:58
  113.8 0.9 copy-done.2
  114.7 0.9 copy-done.3
  115.7 0.1 shard_map.117
  115.7 9.8 %all_to_all.35 = bf16[4,384,128]{2,1,0:T(8,128)(2,1)S(1)} all-to-all(bf16[4,384,128]{2,1,0:T(8,128)(2,1)S(1)} %bitcast.13), channel_id=1, replica_groups=mesh['pts'=128,'chan'=4] {'chan'}, dimensions={0} | all-to-all | bytes 786432 | tf_op jit(solution)/shard_map/all_to_all | solution.py:432
  125.5 0.7 shard_map.118
  (17 shorter events, 0.1 us)
Async XLA Ops:
  7.2 74.5 %all-gather.2.cloned.1.call-start = ((), (), s32[]{:S(2)}) async-start(), calls=%async_computation.3 | async-start | bytes 3276800 | tf_op jit(solution)/shard_map/all_gather | solution.py:383
  7.2 62.5 %copy-start.1 = (bf16[3,512,128]{2,1,0:T(8,128)(2,1)S(1)}, bf16[3,512,128]{2,1,0:T(8,128)(2,1)}, u32[]{:S(2)}) copy-start(bf16[3,512,128]{2,1,0:T(8,128)(2,1)} %w_ref.1) | copy-start | bytes 1179652
  7.2 62.5 %copy-start.4 = (f32[512]{0:T(512)S(1)}, f32[512]{0:T(512)}, u32[]{:S(2)}) copy-start(f32[512]{0:T(512)} %param.13) | copy-start | bytes 6148
  11.7 27.0 %collective-permute-start.2 = (bf16[416,128]{1,0:T(8,128)(2,1)}, bf16[416,128]{1,0:T(8,128)(2,1)S(1)}, u32[]{:S(2)}, u32[]{:S(2)}) collective-permute-start(bf16[416,128]{1,0:T(8,128)(2,1)} %get-tuple-element.23), channel_id=1, source_target_pairs={{0,8},{4,12},{8,0},{12,4},{16,24},{20,28},{24,16},{28,20},{32,40},... | collective-permute-start | bytes 319496 | tf_op jit(solution)/shard_map/ppermute | solution.py:58
  15.5 23.2 %collective-permute-start.3 = (bf16[416,128]{1,0:T(8,128)(2,1)}, bf16[416,128]{1,0:T(8,128)(2,1)S(1)}, u32[]{:S(2)}, u32[]{:S(2)}) collective-permute-start(bf16[416,128]{1,0:T(8,128)(2,1)} %get-tuple-element.24), channel_id=1, source_target_pairs={{0,504},{4,508},{8,16},{12,20},{16,8},{20,12},{24,32},{28,36},{32,... | collective-permute-start | bytes 319496 | tf_op jit(solution)/shard_map/ppermute | solution.py:58
  28.2 10.3 %collective-permute-start = (bf16[208,128]{1,0:T(8,128)(2,1)}, bf16[208,128]{1,0:T(8,128)(2,1)S(1)}, u32[]{:S(2)}, u32[]{:S(2)}) collective-permute-start(bf16[208,128]{1,0:T(8,128)(2,1)} %get-tuple-element.20), channel_id=1, source_target_pairs={{0,500},{4,16},{8,508},{12,24},{16,4},{20,32},{24,12},{28,40},{32,... | collective-permute-start | bytes 159752 | tf_op jit(solution)/shard_map/ppermute | solution.py:58
  30.4 8.2 %collective-permute-start.1 = (bf16[208,128]{1,0:T(8,128)(2,1)}, bf16[208,128]{1,0:T(8,128)(2,1)S(1)}, u32[]{:S(2)}, u32[]{:S(2)}) collective-permute-start(bf16[208,128]{1,0:T(8,128)(2,1)} %get-tuple-element.21), channel_id=1, source_target_pairs={{0,256},{4,260},{8,264},{12,268},{16,272},{20,276},{24,280},{28,28... | collective-permute-start | bytes 159752 | tf_op jit(solution)/shard_map/ppermute | solution.py:58
  39.6 3.4 %collective-permute-start.4 = (bf16[832,128]{1,0:T(8,128)(2,1)S(1)}, bf16[832,128]{1,0:T(8,128)(2,1)S(1)}, u32[]{:S(2)}, u32[]{:S(2)}) collective-permute-start(bf16[832,128]{1,0:T(8,128)(2,1)S(1)} %pad_maximum_fusion.sent_ref), channel_id=1, source_target_pairs={{0,4},{4,0},{8,12},{12,8},{16,20},{20,16},{24,28},{28,24},{32,36},... | collective-permute-start | bytes 638984 | tf_op jit(solution)/shard_map/ppermute | solution.py:58
  69.7 24.1 %copy-start = (bf16[4,1024,128]{2,1,0:T(8,128)(2,1)}, bf16[4,1024,128]{2,1,0:T(8,128)(2,1)S(1)}, u32[]{:S(2)}) copy-start(bf16[4,1024,128]{2,1,0:T(8,128)(2,1)S(1)} %all_to_all.33) | copy-start | bytes 3145732
  81.6 12.2 %collective-permute-start.5 = (bf16[10240,128]{1,0:T(8,128)(2,1)}, bf16[10240,128]{1,0:T(8,128)(2,1)}, u32[]{:S(2)}, u32[]{:S(2)}) collective-permute-start(bf16[10240,128]{1,0:T(8,128)(2,1)} %all-gather.2.cloned.1.call-done.mine_ref), channel_id=1, source_target_pairs={{0,4},{4,0},{8,12},{12,8},{16,20},{20,16},{24,28},{28,24},{32,36},... | collective-permute-start | bytes 7864328 | tf_op jit(solution)/shard_map/ppermute | solution.py:58
  101.1 9.8 %collective-permute-start.6 = (bf16[128,512]{1,0:T(8,128)(2,1)}, bf16[128,512]{1,0:T(8,128)(2,1)S(1)}, u32[]{:S(2)}, u32[]{:S(2)}) collective-permute-start(bf16[128,512]{1,0:T(8,128)(2,1)} %get-tuple-element.33), channel_id=1, source_target_pairs={{0,4},{4,0},{8,12},{12,8},{16,20},{20,16},{24,28},{28,24},{32,36},... | collective-permute-start | bytes 393224 | tf_op jit(solution)/shard_map/ppermute | solution.py:58
  103.0 10.7 %collective-permute-start.7 = (bf16[128,512]{1,0:T(8,128)(2,1)}, bf16[128,512]{1,0:T(8,128)(2,1)S(1)}, u32[]{:S(2)}, u32[]{:S(2)}) collective-permute-start(bf16[128,512]{1,0:T(8,128)(2,1)} %get-tuple-element.34), channel_id=1, source_target_pairs={{0,508},{4,8},{8,4},{12,16},{16,12},{20,24},{24,20},{28,32},{32,28... | collective-permute-start | bytes 393224 | tf_op jit(solution)/shard_map/ppermute | solution.py:58
  113.8 1.0 copy-start.2
  114.7 0.9 copy-start.3
Sparse Core Ops, SparseCore 0:
  11.8 56.6 all-gather.1

commit v4 on v3

--- a/solution.py
+++ b/solution.py
@@ -23,10 +23,11 @@
 SLOTS = KINDS * CAP
 HALF = 256
 STEP = 512
-FC1, FC2, POOL, WROWS = 256, 1280, 2304, 2560
+HALF_ROWS = 2048
+SQUARE_ROWS = 1024
 MESSAGE = QUARTER + CELLS
 VMEM_LIMIT = 48 * 1024 * 1024
-MOST_VMEM = 61 * 1024 * 1024 + 512 * 1024
+SOME_VMEM = 32 * 1024 * 1024
 ALL_VMEM = 63 * 1024 * 1024 + 512 * 1024
 
 
@@ -160,7 +161,7 @@
 
 def pack_kernel(
     feats_ref, dest_ref, cell_ref, w_out_ref, w_fc1_ref, w_fc2_ref, w_pool_ref,
-    up_ref, down_ref, swap_ref, far_ref, across_ref, weights_ref,
+    up_ref, down_ref, swap_ref, far_ref, across_ref, halves_ref, square_ref,
     feats_here, dest_here, cell_here, sems,
 ):
     me = lax.axis_index("pts")
@@ -171,18 +172,16 @@
     feats_copy = start(feats_ref, feats_here)
 
     half = pl.multiple_of(core * HALF, HALF)
-    quarter = pl.multiple_of(core * 64, 64)
     weight_copies = []
     for r in range(2):
         src = w_fc1_ref.at[:, pl.ds(pl.multiple_of(half + r * 128, 128), 128)]
-        weight_copies.append(start(src, weights_ref.at[FC1 + r * C : FC1 + (r + 1) * C, :]))
+        weight_copies.append(start(src, halves_ref.at[r * C : (r + 1) * C, :]))
     for r in range(4):
         cols = slice(r * 128, (r + 1) * 128)
-        dst = weights_ref.at[FC2 + r * HALF : FC2 + (r + 1) * HALF, :]
+        dst = halves_ref.at[2 * C + r * HALF : 2 * C + (r + 1) * HALF, :]
         weight_copies.append(start(w_fc2_ref.at[pl.ds(half, HALF), cols], dst))
-        dst = weights_ref.at[r * 64 : (r + 1) * 64, :]
-        weight_copies.append(start(w_out_ref.at[pl.ds(quarter, 64), cols], dst))
-    weight_copies.append(start(w_pool_ref.at[pl.ds(half, HALF), :], weights_ref.at[POOL:WROWS, :]))
+        weight_copies.append(start(w_out_ref.at[:, cols], square_ref.at[r * 128 : (r + 1) * 128, :]))
+    weight_copies.append(start(w_pool_ref, square_ref.at[C:, :]))
 
     before = lax.broadcasted_iota(jnp.int32, (ROWS, ROWS), 0)
     after = lax.broadcasted_iota(jnp.int32, (ROWS, ROWS), 1)
@@ -267,52 +266,36 @@
 
 
 def mlp_kernel(
-    attn_ref, x_ref, gain_ref, cell_ref, mine_ref, other_ref,
-    block_ref, own_ref, swap_ref, next_ref, x_rows, held, sems,
+    attn_ref, x_ref, gain_ref, cell_ref, mine_ref, other_ref, square_ref,
+    block_ref, own_ref, swap_ref, next_ref,
 ):
     chan = lax.axis_index("chan")
     me = lax.axis_index("pts")
     core = lax.rem(me, 2)
     row = pl.multiple_of(chan * QUARTER, QUARTER)
-    start = copier(sems)
-    sources = [(s, c) for s in range(2) for c in range(4)]
-    refs = (mine_ref, other_ref)
-    early, late = [], []
-    for c in range(4):
-        src = x_ref.at[pl.ds(c * ROWS + row, QUARTER), :]
-        early.append(start(src, x_rows.at[:, c * 128 : (c + 1) * 128]))
-    for s, c in sources:
-        early.append(start(refs[s].at[c * WROWS : c * WROWS + FC1, :], held.at[s, c, 0:FC1, :]))
-    for s, c in sources:
-        src = refs[s].at[c * WROWS + FC1 : (c + 1) * WROWS, :]
-        late.append(start(src, held.at[s, c, FC1:WROWS, :]))
-
-    def part(s, c, row, height, count):
-        pieces = [held[s, c, row + r * height : row + (r + 1) * height, :] for r in range(count)]
-        return jnp.concatenate(pieces, axis=1)
-
-    wait(early)
-    halves = (core, 1 - core)
-    attn = jnp.concatenate(
-        [attn_ref[pl.ds(pl.multiple_of(c * 128 + halves[s] * 64, 64), 64), :] for s, c in sources], axis=0
-    )
-    w_out = jnp.concatenate([part(s, c, 0, 64, 4) for s, c in sources], axis=0)
-    mid = (x_rows[...].astype(F32) + matmul_tn(attn, w_out)).astype(BF16).astype(F32)
+
+    def columns(ref, base, height, count):
+        return jnp.concatenate([ref[base + r * height : base + (r + 1) * height, :] for r in range(count)], axis=1)
+
+    def stacked(parts):
+        return jnp.concatenate(parts, axis=0)
+
+    x = jnp.concatenate([x_ref[pl.ds(c * ROWS + row, QUARTER), :] for c in range(4)], axis=1)
+    w_out = stacked([columns(square_ref, c * SQUARE_ROWS, 128, 4) for c in range(4)])
+    mid = (x.astype(F32) + matmul_tn(attn_ref[...], w_out)).astype(BF16).astype(F32)
     normed = normed_chunks([mid], [gain_ref[...]])[0]
     summed = None
-    for k, (s, c) in enumerate(sources):
-        wait([late[k]])
-        act = gelu(matmul(normed, part(s, c, FC1, C, 2))).astype(BF16)
-        term = matmul(act, part(s, c, FC2, HALF, 4))
-        summed = term if summed is None else summed + term
+    for ref in (mine_ref, other_ref):
+        for c in range(0, 4, 2):
+            bases = (c * HALF_ROWS, (c + 1) * HALF_ROWS)
+            w_fc1 = jnp.concatenate([columns(ref, base, C, 2) for base in bases], axis=1)
+            w_fc2 = stacked([columns(ref, base + 2 * C, HALF, 4) for base in bases])
+            act = gelu(matmul(normed, w_fc1)).astype(BF16)
+            term = matmul(act, w_fc2)
+            summed = term if summed is None else summed + term
     block = (mid + summed).astype(BF16)
-    left, right = block[:, :HALF].astype(F32), block[:, HALF:].astype(F32)
-    lin = None
-    for s in range(2):
-        mine = jnp.where(halves[s] == 0, left, right).astype(BF16)
-        w_pool = jnp.concatenate([held[s, c, POOL:WROWS, :] for c in range(4)], axis=1)
-        term = matmul(mine, w_pool)
-        lin = term if lin is None else lin + term
+    w_pool = jnp.concatenate([square_ref[c * SQUARE_ROWS + C : (c + 1) * SQUARE_ROWS, :] for c in range(4)], axis=1)
+    lin = matmul(block, w_pool)
     high = lin.astype(BF16)
     low = (lin - high.astype(F32)).astype(BF16)
     member = one_hot(cell_ref[:, pl.ds(row, QUARTER)] - (me - 1) * CELLS, 3 * CELLS)
@@ -367,9 +350,9 @@
     def block(count=1):
         return ((count * BLOCK, LANES), BF16)
 
-    up, down, swap, far, over, weights = call(
+    up, down, swap, far, over, halves, square = call(
         pack_kernel,
-        [block(2), block(2), block(2), block(), block(), ((WROWS, LANES), BF16)],
+        [block(2), block(2), block(2), block(), block(), ((HALF_ROWS, LANES), BF16), ((SQUARE_ROWS, LANES), BF16)],
         (feats, dest_pos.reshape(1, ROWS), cell_id.reshape(1, ROWS), w_out, w_fc1, w_fc2, w_pool),
         scratch=[
             pltpu.VMEM((ROWS, LANES), BF16),
@@ -380,7 +363,7 @@
         limit=ALL_VMEM,
         in_hbm=range(7),
     )
-    gathered = lax.all_gather(weights, "chan", axis=0, tiled=True)
+    halves = lax.all_gather(halves, "chan", axis=0, tiled=True)
     far = exchange(far, far_pair)
     over = exchange(over, across)
     up = exchange(up, chip_up)
@@ -395,6 +378,9 @@
         scratch=[pltpu.VMEM((SLOTS, LANES), BF16)],
     )
     full = lax.all_to_all(ordered, "chan", split_axis=0, concat_axis=0, tiled=True)
+    full, square, halves = lax.optimization_barrier((full, square, halves))
+    square = lax.all_gather(square, "chan", axis=0, tiled=True)
+    others = exchange(halves, core_swap)
     (attn,) = call(
         attention_kernel,
         [((N_CHAN * LANES, QUARTER), BF16)],
@@ -406,21 +392,13 @@
             pltpu.VMEM((LANES, ROWS), BF16),
         ],
     )
-    attn, gathered = lax.optimization_barrier((attn, gathered))
-    others = exchange(gathered, core_swap)
     attn = lax.all_to_all(attn, "chan", split_axis=0, concat_axis=0, tiled=True)
     cell_sum = ((CELLS, C), BF16)
     rows, mine, for_swap, for_next = call(
         mlp_kernel,
         [((QUARTER, C), BF16), ((CELLS, C), F32), cell_sum, cell_sum],
-        (attn, full, ln2_gain.reshape(1, C), cell_id.reshape(1, ROWS), gathered, others),
-        limit=MOST_VMEM,
-        in_hbm=(4, 5),
-        scratch=[
-            pltpu.VMEM((QUARTER, C), BF16),
-            pltpu.VMEM((2, N_CHAN, WROWS, LANES), BF16),
-            pltpu.SemaphoreType.DMA((20,)),
-        ],
+        (attn, full, ln2_gain.reshape(1, C), cell_id.reshape(1, ROWS), halves, others, square),
+        limit=SOME_VMEM,
     )
     from_swap = exchange(for_swap, core_swap)
     from_next = exchange(for_next, next_pair)

time: 134 us -> 136 us (1.015)
  waiting for transfers between devices: 9.79 us -> 19.3 us
  blocking collectives: 45.7 us -> 41.6 us
  Pallas kernels: 25.4 us -> 22.3 us
    all_gather x1 -> x2, waiting for transfers between devices: 0.01 us -> 9.69 us  [the longest x1 9.69 us: body(): square = lax.all_gather(square, 'chan', axis=0, tiled=True)]
    all_to_all x1, blocking collectives: 25.7 us -> 20.5 us  [body(): lax.all_to_all(ordered, 'chan', split_axis=0, concat_axis=0, tiled=True)]
    pallas_call x6, Pallas kernels: 25.4 us -> 22.3 us  [call(): pl.pallas_call(kernel, out_shape=[jax.ShapeDtypeStruct(shape, dtype) for...]
  transfers between devices with their start and end apart: 9 -> 10, of which waited for: 4 -> 5; matrix products, arithmetic and copies ran while one was open for 1% -> 1% of each run, Pallas kernels for 10% -> 10%
where the time goes in v4:
time: 136 us
  blocking collectives  41.6 us (31%)
  starting transfers between devices  35.5 us (26%)
  Pallas kernels  22.3 us (16%)
  waiting for transfers between devices  19.3 us (14%)
  between operations  14.2 us (10%)
  local copies, waits for them, and re-layouts  1.87 us (1%)
    ppermute x8, starting transfers between devices, exchange(): return lax.ppermute(x, 'pts', [(i, partner(i)) for i in range(N_PTS)])  35.4 us
    pallas_call x6, Pallas kernels, call(): pl.pallas_call(kernel, out_shape=[jax.ShapeDtypeStruct(shape, dtype) for...  22.3 us
    all_to_all x1, blocking collectives, body(): lax.all_to_all(ordered, 'chan', split_axis=0, concat_axis=0, tiled=True)  20.5 us
    all_to_all x1, blocking collectives, body(): lax.all_to_all(message, 'chan', split_axis=0, concat_axis=0, tiled=True)  10.9 us
    all_to_all x1, blocking collectives, body(): attn = lax.all_to_all(attn, 'chan', split_axis=0, concat_axis=0, tiled=True)  10.2 us
    all_gather x1, waiting for transfers between devices, body(): square = lax.all_gather(square, 'chan', axis=0, tiled=True)  9.69 us
    ppermute x8, waiting for transfers between devices, exchange(): return lax.ppermute(x, 'pts', [(i, partner(i)) for i in range(N_PTS)])  9.56 us
  transfers between devices with their start and end apart: 10, of which 5 were waited for; matrix products, arithmetic and copies ran while one was open for 1% of the time, Pallas kernels for 10%

profile of v4, /device:TPU:8, one launch (start us, length us, event | category | flops | bytes accessed | tf_op | source)
XLA Modules:
  0.0 135.8 jit_solution(5199959151097444148)
XLA Ops:
  7.2 4.4 %shard_map.113 = (bf16[416,128]{1,0:T(8,128)(2,1)}, bf16[416,128]{1,0:T(8,128)(2,1)}, bf16[416,128]{1,0:T(8,128)(2,1)}, bf16[208,128]{1,0:T(8,128)(2,1)}, bf16[2...) custom-call(bf16[1024,128]{1,0:T(8,128)(2,1)} %feats_ref.1, s32[1,1024]{1,0:T(1,128)} %bitcast.21, ...), custom_call_target="tpu_custom_call" | custom-call | tf_op jit(solution)/shard_map/pallas_call | solution.py:339
  11.7 4.0 %collective-permute-start.2 = (bf16[416,128]{1,0:T(8,128)(2,1)}, bf16[416,128]{1,0:T(8,128)(2,1)S(1)}, u32[]{:S(2)}, u32[]{:S(2)}) collective-permute-start(bf16[416,128]{1,0:T(8,128)(2,1)} %get-tuple-element.25), channel_id=1, source_target_pairs={{0,8},{4,12},{8,0},{12,4},{16,24},{20,28},{24,16},{28,20},{32,40},... | collective-permute-start | bytes 319496 | tf_op jit(solution)/shard_map/ppermute | solution.py:59
  15.7 12.7 %collective-permute-start.3 = (bf16[416,128]{1,0:T(8,128)(2,1)}, bf16[416,128]{1,0:T(8,128)(2,1)S(1)}, u32[]{:S(2)}, u32[]{:S(2)}) collective-permute-start(bf16[416,128]{1,0:T(8,128)(2,1)} %get-tuple-element.26), channel_id=1, source_target_pairs={{0,504},{4,508},{8,16},{12,20},{16,8},{20,12},{24,32},{28,36},{32,... | collective-permute-start | bytes 319496 | tf_op jit(solution)/shard_map/ppermute | solution.py:59
  28.4 2.2 %collective-permute-start = (bf16[208,128]{1,0:T(8,128)(2,1)}, bf16[208,128]{1,0:T(8,128)(2,1)S(1)}, u32[]{:S(2)}, u32[]{:S(2)}) collective-permute-start(bf16[208,128]{1,0:T(8,128)(2,1)} %get-tuple-element.22), channel_id=1, source_target_pairs={{0,500},{4,16},{8,508},{12,24},{16,4},{20,32},{24,12},{28,40},{32,... | collective-permute-start | bytes 159752 | tf_op jit(solution)/shard_map/ppermute | solution.py:59
  30.6 2.7 %collective-permute-start.1 = (bf16[208,128]{1,0:T(8,128)(2,1)}, bf16[208,128]{1,0:T(8,128)(2,1)S(1)}, u32[]{:S(2)}, u32[]{:S(2)}) collective-permute-start(bf16[208,128]{1,0:T(8,128)(2,1)} %get-tuple-element.23), channel_id=1, source_target_pairs={{0,256},{4,260},{8,264},{12,268},{16,272},{20,276},{24,280},{28,28... | collective-permute-start | bytes 159752 | tf_op jit(solution)/shard_map/ppermute | solution.py:59
  33.3 5.4 %collective-permute-done.far_ref = bf16[208,128]{1,0:T(8,128)(2,1)S(1)} collective-permute-done((bf16[208,128]{1,0:T(8,128)(2,1)}, bf16[208,128]{1,0:T(8,128)(2,1)S(1)}, u32[]{:S(2)}, u32[]{:S(2)}) %collective-permute-start) | collective-permute-done | bytes 53280 | tf_op jit(solution)/shard_map/ppermute | solution.py:59
  38.7 0.1 collective-permute-done.1.across_ref
  38.8 0.9 pad_maximum_fusion.sent_ref
  39.8 1.9 %collective-permute-start.4 = (bf16[832,128]{1,0:T(8,128)(2,1)S(1)}, bf16[832,128]{1,0:T(8,128)(2,1)S(1)}, u32[]{:S(2)}, u32[]{:S(2)}) collective-permute-start(bf16[832,128]{1,0:T(8,128)(2,1)S(1)} %pad_maximum_fusion.sent_ref), channel_id=1, source_target_pairs={{0,4},{4,0},{8,12},{12,8},{16,20},{20,16},{24,28},{28,24},{32,36},... | collective-permute-start | bytes 638984 | tf_op jit(solution)/shard_map/ppermute | solution.py:59
  41.7 1.4 %collective-permute-done.4.swap_ref = bf16[832,128]{1,0:T(8,128)(2,1)S(1)} collective-permute-done((bf16[832,128]{1,0:T(8,128)(2,1)S(1)}, bf16[832,128]{1,0:T(8,128)(2,1)S(1)}, u32[]{:S(2)}, u32[]{:S(2)}) %collective-permute-start.4) | collective-permute-done | bytes 213024 | tf_op jit(solution)/shard_map/ppermute | solution.py:59
  43.1 1.0 shard_map.114
  44.2 0.6 copy-done.3
  44.8 20.5 %all_to_all.34 = bf16[4,1024,128]{2,1,0:T(8,128)(2,1)S(1)} all-to-all(bf16[4,1024,128]{2,1,0:T(8,128)(2,1)S(1)} %bitcast.14), channel_id=1, replica_groups=mesh['pts'=128,'chan'=4] {'chan'}, dimensions={0} | all-to-all | bytes 2097152 | tf_op jit(solution)/shard_map/all_to_all | solution.py:380
  65.2 2.2 %collective-permute-start.5 = (bf16[8192,128]{1,0:T(8,128)(2,1)}, bf16[8192,128]{1,0:T(8,128)(2,1)}, u32[]{:S(2)}, u32[]{:S(2)}) collective-permute-start(bf16[8192,128]{1,0:T(8,128)(2,1)} %all-gather.3.cloned.1.call-done.mine_ref), channel_id=1, source_target_pairs={{0,4},{4,0},{8,12},{12,8},{16,20},{20,16},{24,28},{28,24},{32,36},... | collective-permute-start | bytes 6291464 | tf_op jit(solution)/shard_map/ppermute | solution.py:59
  67.5 11.9 %shard_map.115 = bf16[512,256]{1,0:T(8,128)(2,1)S(1)} custom-call(bf16[4096,128]{1,0:T(8,128)(2,1)S(1)} %bitcast.10, f32[1,512]{1,0:T(1,128)S(1)} %bitcast.19, bf16[3,512,128]{2,1,0:T(8,128)(2,1)S(1)} %copy-done.2), custom_call_target="tpu_custom_call" | custom-call | tf_op jit(solution)/shard_map/pallas_call | solution.py:339
  79.4 10.2 %all_to_all.35 = bf16[4,128,256]{2,1,0:T(8,128)(2,1)S(1)} all-to-all(bf16[4,128,256]{2,1,0:T(8,128)(2,1)S(1)} %bitcast.15), channel_id=1, replica_groups=mesh['pts'=128,'chan'=4] {'chan'}, dimensions={0} | all-to-all | bytes 524288 | tf_op jit(solution)/shard_map/all_to_all | solution.py:395
  89.7 9.7 %all-gather.5.cloned.1.call-done.square_ref = bf16[4096,128]{1,0:T(8,128)(2,1)} async-done(((bf16[1024,128]{1,0:T(8,128)(2,1)}), bf16[4096,128]{1,0:T(8,128)(2,1)}) %all-gather.5.cloned.1.call-update) | async-done | bytes 1048592 | tf_op jit(solution)/shard_map/all_gather | solution.py:382
  99.4 1.2 copy-done.1
  100.6 4.2 %shard_map.116 = (bf16[256,512]{1,0:T(8,128)(2,1)S(1)}, f32[128,512]{1,0:T(8,128)S(1)}, bf16[128,512]{1,0:T(8,128)(2,1)S(1)}, bf16[128,512]{1,0:T(8,128)(2,1)S(1)}) custom-call(bf16[512,256]{1,0:T(8,128)(2,1)S(1)} %bitcast.16, bf16[4096,128]{1,0:T(8,128)(2,1)S(1)} %bitcast.11, f32[1,512]{1,0:T(1,128)S(1)} %bitcast.20, s32[1,1024]{1,0:T(1,128)S(1)} %bitcast.18, ...), custom_call_target="tpu_custom_call" | custom-call | tf_op jit(solution)/shard_map/pallas_call | solution.py:339
  104.8 1.9 %collective-permute-start.6 = (bf16[128,512]{1,0:T(8,128)(2,1)S(1)}, bf16[128,512]{1,0:T(8,128)(2,1)S(1)}, u32[]{:S(2)}, u32[]{:S(2)}) collective-permute-start(bf16[128,512]{1,0:T(8,128)(2,1)S(1)} %get-tuple-element.37), channel_id=1, source_target_pairs={{0,4},{4,0},{8,12},{12,8},{16,20},{20,16},{24,28},{28,24},{32,36},... | collective-permute-start | bytes 393224 | tf_op jit(solution)/shard_map/ppermute | solution.py:59
  106.8 7.8 %collective-permute-start.7 = (bf16[128,512]{1,0:T(8,128)(2,1)S(1)}, bf16[128,512]{1,0:T(8,128)(2,1)S(1)}, u32[]{:S(2)}, u32[]{:S(2)}) collective-permute-start(bf16[128,512]{1,0:T(8,128)(2,1)S(1)} %get-tuple-element.38), channel_id=1, source_target_pairs={{0,508},{4,8},{8,4},{12,16},{16,12},{20,24},{24,20},{28,32},{32,28... | collective-permute-start | bytes 393224 | tf_op jit(solution)/shard_map/ppermute | solution.py:59
  114.5 2.6 %collective-permute-done.7.next_ref = bf16[128,512]{1,0:T(8,128)(2,1)S(1)} collective-permute-done((bf16[128,512]{1,0:T(8,128)(2,1)S(1)}, bf16[128,512]{1,0:T(8,128)(2,1)S(1)}, u32[]{:S(2)}, u32[]{:S(2)}) %collective-permute-start.7) | collective-permute-done | bytes 131104 | tf_op jit(solution)/shard_map/ppermute | solution.py:59
  117.3 10.9 %all_to_all.36 = bf16[4,384,128]{2,1,0:T(8,128)(2,1)S(1)} all-to-all(bf16[4,384,128]{2,1,0:T(8,128)(2,1)S(1)} %bitcast.13), channel_id=1, replica_groups=mesh['pts'=128,'chan'=4] {'chan'}, dimensions={0} | all-to-all | bytes 786432 | tf_op jit(solution)/shard_map/all_to_all | solution.py:410
  128.2 0.7 shard_map.118
  (26 shorter events, 0.2 us)
Async XLA Ops:
  7.2 58.1 %all-gather.3.cloned.1.call-start = ((), (), s32[]{:S(2)}) async-start(), calls=%async_computation.3 | async-start | bytes 2621440 | tf_op jit(solution)/shard_map/all_gather | solution.py:366
  11.6 55.9 %copy-start.2 = (bf16[3,512,128]{2,1,0:T(8,128)(2,1)S(1)}, bf16[3,512,128]{2,1,0:T(8,128)(2,1)}, u32[]{:S(2)}) copy-start(bf16[3,512,128]{2,1,0:T(8,128)(2,1)} %w_ref.1) | copy-start | bytes 1179652
  11.6 55.9 %copy-start.6 = (f32[512]{0:T(512)S(1)}, f32[512]{0:T(512)}, u32[]{:S(2)}) copy-start(f32[512]{0:T(512)} %param.13) | copy-start | bytes 6148
  11.6 87.7 %all-gather.5.cloned.1.call-start = ((), (), s32[]{:S(2)}) async-start(), calls=%async_computation.4 | async-start | bytes 1310720 | tf_op jit(solution)/shard_map/all_gather | solution.py:382
  11.7 27.1 %collective-permute-start.2 = (bf16[416,128]{1,0:T(8,128)(2,1)}, bf16[416,128]{1,0:T(8,128)(2,1)S(1)}, u32[]{:S(2)}, u32[]{:S(2)}) collective-permute-start(bf16[416,128]{1,0:T(8,128)(2,1)} %get-tuple-element.25), channel_id=1, source_target_pairs={{0,8},{4,12},{8,0},{12,4},{16,24},{20,28},{24,16},{28,20},{32,40},... | collective-permute-start | bytes 319496 | tf_op jit(solution)/shard_map/ppermute | solution.py:59
  15.7 23.2 %collective-permute-start.3 = (bf16[416,128]{1,0:T(8,128)(2,1)}, bf16[416,128]{1,0:T(8,128)(2,1)S(1)}, u32[]{:S(2)}, u32[]{:S(2)}) collective-permute-start(bf16[416,128]{1,0:T(8,128)(2,1)} %get-tuple-element.26), channel_id=1, source_target_pairs={{0,504},{4,508},{8,16},{12,20},{16,8},{20,12},{24,32},{28,36},{32,... | collective-permute-start | bytes 319496 | tf_op jit(solution)/shard_map/ppermute | solution.py:59
  28.4 10.3 %collective-permute-start = (bf16[208,128]{1,0:T(8,128)(2,1)}, bf16[208,128]{1,0:T(8,128)(2,1)S(1)}, u32[]{:S(2)}, u32[]{:S(2)}) collective-permute-start(bf16[208,128]{1,0:T(8,128)(2,1)} %get-tuple-element.22), channel_id=1, source_target_pairs={{0,500},{4,16},{8,508},{12,24},{16,4},{20,32},{24,12},{28,40},{32,... | collective-permute-start | bytes 159752 | tf_op jit(solution)/shard_map/ppermute | solution.py:59
  30.6 8.2 %collective-permute-start.1 = (bf16[208,128]{1,0:T(8,128)(2,1)}, bf16[208,128]{1,0:T(8,128)(2,1)S(1)}, u32[]{:S(2)}, u32[]{:S(2)}) collective-permute-start(bf16[208,128]{1,0:T(8,128)(2,1)} %get-tuple-element.23), channel_id=1, source_target_pairs={{0,256},{4,260},{8,264},{12,268},{16,272},{20,276},{24,280},{28,28... | collective-permute-start | bytes 159752 | tf_op jit(solution)/shard_map/ppermute | solution.py:59
  39.8 3.4 %collective-permute-start.4 = (bf16[832,128]{1,0:T(8,128)(2,1)S(1)}, bf16[832,128]{1,0:T(8,128)(2,1)S(1)}, u32[]{:S(2)}, u32[]{:S(2)}) collective-permute-start(bf16[832,128]{1,0:T(8,128)(2,1)S(1)} %pad_maximum_fusion.sent_ref), channel_id=1, source_target_pairs={{0,4},{4,0},{8,12},{12,8},{16,20},{20,16},{24,28},{28,24},{32,36},... | collective-permute-start | bytes 638984 | tf_op jit(solution)/shard_map/ppermute | solution.py:59
  44.2 0.6 copy-start.3
  44.8 54.6 %copy-start.5 = (s32[1024]{0:T(1024)S(1)}, s32[1024]{0:T(1024)}, u32[]{:S(2)}) copy-start(s32[1024]{0:T(1024)} %param.12) | copy-start | bytes 12292
  44.8 54.6 %copy-start.7 = (f32[512]{0:T(512)S(1)}, f32[512]{0:T(512)}, u32[]{:S(2)}) copy-start(f32[512]{0:T(512)} %param.16) | copy-start | bytes 6148
  65.2 34.1 %copy-start = (bf16[8192,128]{1,0:T(8,128)(2,1)S(1)}, bf16[8192,128]{1,0:T(8,128)(2,1)}, u32[]{:S(2)}) copy-start(bf16[8192,128]{1,0:T(8,128)(2,1)} %all-gather.3.cloned.1.call-done.mine_ref) | copy-start | bytes 6291460
  65.2 34.1 %collective-permute-start.5 = (bf16[8192,128]{1,0:T(8,128)(2,1)}, bf16[8192,128]{1,0:T(8,128)(2,1)}, u32[]{:S(2)}, u32[]{:S(2)}) collective-permute-start(bf16[8192,128]{1,0:T(8,128)(2,1)} %all-gather.3.cloned.1.call-done.mine_ref), channel_id=1, source_target_pairs={{0,4},{4,0},{8,12},{12,8},{16,20},{20,16},{24,28},{28,24},{32,36},... | collective-permute-start | bytes 6291464 | tf_op jit(solution)/shard_map/ppermute | solution.py:59
  99.4 1.2 copy-start.1
  100.6 27.6 %copy-start.4 = (f32[128,128]{1,0:T(8,128)S(1)}, f32[128,128]{1,0:T(8,128)}, u32[]{:S(2)}) copy-start(f32[128,128]{1,0:T(8,128)} %copy-done.3) | copy-start | bytes 196612
  104.8 9.7 %collective-permute-start.6 = (bf16[128,512]{1,0:T(8,128)(2,1)S(1)}, bf16[128,512]{1,0:T(8,128)(2,1)S(1)}, u32[]{:S(2)}, u32[]{:S(2)}) collective-permute-start(bf16[128,512]{1,0:T(8,128)(2,1)S(1)} %get-tuple-element.37), channel_id=1, source_target_pairs={{0,4},{4,0},{8,12},{12,8},{16,20},{20,16},{24,28},{28,24},{32,36},... | collective-permute-start | bytes 393224 | tf_op jit(solution)/shard_map/ppermute | solution.py:59
  106.8 10.4 %collective-permute-start.7 = (bf16[128,512]{1,0:T(8,128)(2,1)S(1)}, bf16[128,512]{1,0:T(8,128)(2,1)S(1)}, u32[]{:S(2)}, u32[]{:S(2)}) collective-permute-start(bf16[128,512]{1,0:T(8,128)(2,1)S(1)} %get-tuple-element.38), channel_id=1, source_target_pairs={{0,508},{4,8},{8,4},{12,16},{16,12},{20,24},{24,20},{28,32},{32,28... | collective-permute-start | bytes 393224 | tf_op jit(solution)/shard_map/ppermute | solution.py:59
Sparse Core Ops, SparseCore 0:
  11.8 44.0 all-gather.2
  67.6 31.7 all-gather.4

commit v5 on v4

--- a/solution.py
+++ b/solution.py
@@ -23,10 +23,9 @@
 SLOTS = KINDS * CAP
 HALF = 256
 STEP = 512
-HALF_ROWS = 2048
-SQUARE_ROWS = 1024
+FC1, FC2, POOL, WROWS = 256, 1280, 2304, 2560
 MESSAGE = QUARTER + CELLS
-VMEM_LIMIT = 48 * 1024 * 1024
+VMEM_LIMIT = 32 * 1024 * 1024
 SOME_VMEM = 32 * 1024 * 1024
 ALL_VMEM = 63 * 1024 * 1024 + 512 * 1024
 
@@ -161,7 +160,7 @@
 
 def pack_kernel(
     feats_ref, dest_ref, cell_ref, w_out_ref, w_fc1_ref, w_fc2_ref, w_pool_ref,
-    up_ref, down_ref, swap_ref, far_ref, across_ref, halves_ref, square_ref,
+    up_ref, down_ref, swap_ref, far_ref, across_ref, weights_ref,
     feats_here, dest_here, cell_here, sems,
 ):
     me = lax.axis_index("pts")
@@ -172,16 +171,18 @@
     feats_copy = start(feats_ref, feats_here)
 
     half = pl.multiple_of(core * HALF, HALF)
+    quarter = pl.multiple_of(core * 64, 64)
     weight_copies = []
     for r in range(2):
         src = w_fc1_ref.at[:, pl.ds(pl.multiple_of(half + r * 128, 128), 128)]
-        weight_copies.append(start(src, halves_ref.at[r * C : (r + 1) * C, :]))
+        weight_copies.append(start(src, weights_ref.at[FC1 + r * C : FC1 + (r + 1) * C, :]))
     for r in range(4):
         cols = slice(r * 128, (r + 1) * 128)
-        dst = halves_ref.at[2 * C + r * HALF : 2 * C + (r + 1) * HALF, :]
+        dst = weights_ref.at[FC2 + r * HALF : FC2 + (r + 1) * HALF, :]
         weight_copies.append(start(w_fc2_ref.at[pl.ds(half, HALF), cols], dst))
-        weight_copies.append(start(w_out_ref.at[:, cols], square_ref.at[r * 128 : (r + 1) * 128, :]))
-    weight_copies.append(start(w_pool_ref, square_ref.at[C:, :]))
+        dst = weights_ref.at[r * 64 : (r + 1) * 64, :]
+        weight_copies.append(start(w_out_ref.at[pl.ds(quarter, 64), cols], dst))
+    weight_copies.append(start(w_pool_ref.at[pl.ds(half, HALF), :], weights_ref.at[POOL:WROWS, :]))
 
     before = lax.broadcasted_iota(jnp.int32, (ROWS, ROWS), 0)
     after = lax.broadcasted_iota(jnp.int32, (ROWS, ROWS), 1)
@@ -210,7 +211,7 @@
     wait(weight_copies)
 
 
-def unpack_kernel(sent_ref, up_ref, down_ref, far_ref, across_ref, swap_ref, out_ref, count_ref, held):
+def unpack_kernel(sent_ref, down_ref, up_ref, across_ref, far_ref, swap_ref, out_ref, count_ref, held):
     homes = [
         (sent_ref, BLOCK), (up_ref, 0), (swap_ref, 2 * BLOCK), (down_ref, 0),
         (swap_ref, 3 * BLOCK), (swap_ref, 0), (far_ref, 0), (across_ref, 0),
@@ -266,7 +267,7 @@
 
 
 def mlp_kernel(
-    attn_ref, x_ref, gain_ref, cell_ref, mine_ref, other_ref, square_ref,
+    attn_ref, x_ref, gain_ref, cell_ref, mine_ref, other_ref,
     block_ref, own_ref, swap_ref, next_ref,
 ):
     chan = lax.axis_index("chan")
@@ -281,21 +282,31 @@
         return jnp.concatenate(parts, axis=0)
 
     x = jnp.concatenate([x_ref[pl.ds(c * ROWS + row, QUARTER), :] for c in range(4)], axis=1)
-    w_out = stacked([columns(square_ref, c * SQUARE_ROWS, 128, 4) for c in range(4)])
-    mid = (x.astype(F32) + matmul_tn(attn_ref[...], w_out)).astype(BF16).astype(F32)
+    halves = ((core, mine_ref), (1 - core, other_ref))
+    rows, w_out = [], []
+    for which, ref in halves:
+        for c in range(4):
+            rows.append(attn_ref[pl.ds(pl.multiple_of(c * 128 + which * 64, 64), 64), :])
+            w_out.append(columns(ref, c * WROWS, 64, 4))
+    mid = (x.astype(F32) + matmul_tn(stacked(rows), stacked(w_out))).astype(BF16).astype(F32)
     normed = normed_chunks([mid], [gain_ref[...]])[0]
     summed = None
-    for ref in (mine_ref, other_ref):
+    for _, ref in halves:
         for c in range(0, 4, 2):
-            bases = (c * HALF_ROWS, (c + 1) * HALF_ROWS)
-            w_fc1 = jnp.concatenate([columns(ref, base, C, 2) for base in bases], axis=1)
-            w_fc2 = stacked([columns(ref, base + 2 * C, HALF, 4) for base in bases])
+            bases = (c * WROWS, (c + 1) * WROWS)
+            w_fc1 = jnp.concatenate([columns(ref, base + FC1, C, 2) for base in bases], axis=1)
+            w_fc2 = stacked([columns(ref, base + FC2, HALF, 4) for base in bases])
             act = gelu(matmul(normed, w_fc1)).astype(BF16)
             term = matmul(act, w_fc2)
             summed = term if summed is None else summed + term
     block = (mid + summed).astype(BF16)
-    w_pool = jnp.concatenate([square_ref[c * SQUARE_ROWS + C : (c + 1) * SQUARE_ROWS, :] for c in range(4)], axis=1)
-    lin = matmul(block, w_pool)
+    left, right = block[:, :HALF].astype(F32), block[:, HALF:].astype(F32)
+    lin = None
+    for which, ref in halves:
+        mine = jnp.where(which == 0, left, right).astype(BF16)
+        w_pool = jnp.concatenate([ref[c * WROWS + POOL : (c + 1) * WROWS, :] for c in range(4)], axis=1)
+        term = matmul(mine, w_pool)
+        lin = term if lin is None else lin + term
     high = lin.astype(BF16)
     low = (lin - high.astype(F32)).astype(BF16)
     member = one_hot(cell_ref[:, pl.ds(row, QUARTER)] - (me - 1) * CELLS, 3 * CELLS)
@@ -316,7 +327,7 @@
         next_ref[...] = after
 
 
-def message_kernel(block_ref, own_ref, swap_ref, next_ref, out_ref):
+def message_kernel(block_ref, own_ref, next_ref, swap_ref, out_ref):
     sums = own_ref[...] + swap_ref[...].astype(F32) + next_ref[...].astype(F32)
     sums = sums.astype(BF16)
     for c in range(N_CHAN):
@@ -333,16 +344,17 @@
     out_ref[...] = gelu(total / count_ref[...]).astype(BF16)
 
 
-def call(kernel, outs, args, scratch=(), in_hbm=(), out_hbm=(), limit=VMEM_LIMIT):
+def call(kernel, outs, args, scratch=(), in_hbm=(), limit=VMEM_LIMIT, cost=None):
     vmem = pl.BlockSpec(memory_space=pltpu.VMEM)
     hbm = pl.BlockSpec(memory_space=pltpu.HBM)
     return pl.pallas_call(
         kernel,
         out_shape=[jax.ShapeDtypeStruct(shape, dtype) for shape, dtype in outs],
         in_specs=[hbm if i in in_hbm else vmem for i in range(len(args))],
-        out_specs=[hbm if i in out_hbm else vmem for i in range(len(outs))],
+        out_specs=[vmem] * len(outs),
         scratch_shapes=list(scratch),
         compiler_params=pltpu.CompilerParams(vmem_limit_bytes=limit),
+        cost_estimate=cost,
     )(*args)
 
 
@@ -350,9 +362,9 @@
     def block(count=1):
         return ((count * BLOCK, LANES), BF16)
 
-    up, down, swap, far, over, halves, square = call(
+    up, down, swap, far, over, weights = call(
         pack_kernel,
-        [block(2), block(2), block(2), block(), block(), ((HALF_ROWS, LANES), BF16), ((SQUARE_ROWS, LANES), BF16)],
+        [block(2), block(2), block(2), block(), block(), ((WROWS, LANES), BF16)],
         (feats, dest_pos.reshape(1, ROWS), cell_id.reshape(1, ROWS), w_out, w_fc1, w_fc2, w_pool),
         scratch=[
             pltpu.VMEM((ROWS, LANES), BF16),
@@ -363,28 +375,28 @@
         limit=ALL_VMEM,
         in_hbm=range(7),
     )
-    halves = lax.all_gather(halves, "chan", axis=0, tiled=True)
+    weights = lax.all_gather(weights, "chan", axis=0, tiled=True)
+    down = exchange(down, chip_down)
+    up = exchange(up, chip_up)
+    over = exchange(over, across)
     far = exchange(far, far_pair)
-    over = exchange(over, across)
-    up = exchange(up, chip_up)
-    down = exchange(down, chip_down)
-    swap, far, over = lax.optimization_barrier((swap, far, over))
+    swap, over, far = lax.optimization_barrier((swap, over, far))
     sent = jnp.concatenate([swap, up[BLOCK:], down[BLOCK:]], axis=0)
     swap = exchange(sent, core_swap)
     ordered, count = call(
         unpack_kernel,
         [((N_CHAN * ROWS, LANES), BF16), ((128, 128), F32)],
-        (sent, up, down, far, over, swap),
+        (sent, down, up, over, far, swap),
         scratch=[pltpu.VMEM((SLOTS, LANES), BF16)],
     )
     full = lax.all_to_all(ordered, "chan", split_axis=0, concat_axis=0, tiled=True)
-    full, square, halves = lax.optimization_barrier((full, square, halves))
-    square = lax.all_gather(square, "chan", axis=0, tiled=True)
-    others = exchange(halves, core_swap)
+    full, weights = lax.optimization_barrier((full, weights))
+    others = exchange(weights, core_swap)
     (attn,) = call(
         attention_kernel,
         [((N_CHAN * LANES, QUARTER), BF16)],
         (full, ln1_gain.reshape(1, C), w_qkv),
+        cost=pl.CostEstimate(flops=9_000_000_000, bytes_accessed=2_000_000, transcendentals=8_400_000),
         scratch=[
             pltpu.VMEM((ROWS, C), BF16),
             pltpu.VMEM((ROWS, LANES), BF16),
@@ -397,15 +409,15 @@
     rows, mine, for_swap, for_next = call(
         mlp_kernel,
         [((QUARTER, C), BF16), ((CELLS, C), F32), cell_sum, cell_sum],
-        (attn, full, ln2_gain.reshape(1, C), cell_id.reshape(1, ROWS), halves, others, square),
+        (attn, full, ln2_gain.reshape(1, C), cell_id.reshape(1, ROWS), weights, others),
         limit=SOME_VMEM,
     )
+    from_next = exchange(for_next, next_pair)
     from_swap = exchange(for_swap, core_swap)
-    from_next = exchange(for_next, next_pair)
     (message,) = call(
         message_kernel,
         [((N_CHAN * MESSAGE, LANES), BF16)],
-        (rows, mine, from_swap, from_next),
+        (rows, mine, from_next, from_swap),
     )
     got = lax.all_to_all(message, "chan", split_axis=0, concat_axis=0, tiled=True)
     block_out, pooled = call(

time: 136 us -> 127 us (0.934)
  the two profiles are of different devices: /device:TPU:8 before, /device:TPU:1 now
where the time goes in v5:
time: 127 us
  blocking collectives  42.6 us (34%)
  starting transfers between devices  41.4 us (33%)
  Pallas kernels  20.8 us (16%)
  between operations  14.2 us (11%)
  waiting for transfers between devices  6.69 us (5%)
    ppermute x8, starting transfers between devices, exchange(): return lax.ppermute(x, 'pts', [(i, partner(i)) for i in range(N_PTS)])  41.4 us
    all_to_all x1, blocking collectives, body(): lax.all_to_all(ordered, 'chan', split_axis=0, concat_axis=0, tiled=True)  23.5 us
    pallas_call x6, Pallas kernels, call(): pl.pallas_call(kernel, out_shape=[jax.ShapeDtypeStruct(shape, dtype) for...  20.8 us
    all_to_all x1, blocking collectives, body(): lax.all_to_all(message, 'chan', split_axis=0, concat_axis=0, tiled=True)  10.2 us
    all_to_all x1, blocking collectives, body(): attn = lax.all_to_all(attn, 'chan', split_axis=0, concat_axis=0, tiled=True)  8.86 us
    ppermute x8, waiting for transfers between devices, exchange(): return lax.ppermute(x, 'pts', [(i, partner(i)) for i in range(N_PTS)])  6.67 us
  transfers between devices with their start and end apart: 9, of which 4 were waited for; matrix products, arithmetic and copies ran while one was open for 1% of the time, Pallas kernels for 10%

profile of v5, /device:TPU:1, one launch (start us, length us, event | category | flops | bytes accessed | tf_op | source)
XLA Modules:
  0.0 126.6 jit_solution(7807018198081667052)
XLA Ops:
  7.2 0.0 all-gather.2.cloned.1.call-start
  7.2 4.4 %shard_map.113 = (bf16[416,128]{1,0:T(8,128)(2,1)}, bf16[416,128]{1,0:T(8,128)(2,1)}, bf16[416,128]{1,0:T(8,128)(2,1)}, bf16[208,128]{1,0:T(8,128)(2,1)}, bf16[2...) custom-call(bf16[1024,128]{1,0:T(8,128)(2,1)} %feats_ref.1, s32[1,1024]{1,0:T(1,128)} %bitcast.21, s32[1,1024]{1,0:T(1,128)} %bitcast.17, ...), custom_call_target="tpu_custom_call" | custom-call | tf_op jit(solution)/shard_map/pallas_call | solution.py:350
  11.6 0.0 all-gather.2.cloned.1.call-update
  11.7 4.4 %collective-permute-start.2 = (bf16[416,128]{1,0:T(8,128)(2,1)}, bf16[416,128]{1,0:T(8,128)(2,1)S(1)}, u32[]{:S(2)}, u32[]{:S(2)}) collective-permute-start(bf16[416,128]{1,0:T(8,128)(2,1)} %get-tuple-element.23), channel_id=1, source_target_pairs={{0,8},{4,12},{8,0},{12,4},{16,24},{20,28},{24,16},{28,20},{32,40},... | collective-permute-start | bytes 319496 | tf_op jit(solution)/shard_map/ppermute | solution.py:58
  16.1 12.4 %collective-permute-start.3 = (bf16[416,128]{1,0:T(8,128)(2,1)}, bf16[416,128]{1,0:T(8,128)(2,1)S(1)}, u32[]{:S(2)}, u32[]{:S(2)}) collective-permute-start(bf16[416,128]{1,0:T(8,128)(2,1)} %get-tuple-element.24), channel_id=1, source_target_pairs={{0,504},{4,508},{8,16},{12,20},{16,8},{20,12},{24,32},{28,36},{32,... | collective-permute-start | bytes 319496 | tf_op jit(solution)/shard_map/ppermute | solution.py:58
  28.5 2.4 %collective-permute-start = (bf16[208,128]{1,0:T(8,128)(2,1)}, bf16[208,128]{1,0:T(8,128)(2,1)S(1)}, u32[]{:S(2)}, u32[]{:S(2)}) collective-permute-start(bf16[208,128]{1,0:T(8,128)(2,1)} %get-tuple-element.20), channel_id=1, source_target_pairs={{0,256},{4,260},{8,264},{12,268},{16,272},{20,276},{24,280},{28,28... | collective-permute-start | bytes 159752 | tf_op jit(solution)/shard_map/ppermute | solution.py:58
  30.9 1.9 %collective-permute-start.1 = (bf16[208,128]{1,0:T(8,128)(2,1)}, bf16[208,128]{1,0:T(8,128)(2,1)S(1)}, u32[]{:S(2)}, u32[]{:S(2)}) collective-permute-start(bf16[208,128]{1,0:T(8,128)(2,1)} %get-tuple-element.21), channel_id=1, source_target_pairs={{0,500},{4,16},{8,508},{12,24},{16,4},{20,32},{24,12},{28,40},{32,... | collective-permute-start | bytes 159752 | tf_op jit(solution)/shard_map/ppermute | solution.py:58
  32.8 2.2 %collective-permute-done.across_ref = bf16[208,128]{1,0:T(8,128)(2,1)S(1)} collective-permute-done((bf16[208,128]{1,0:T(8,128)(2,1)}, bf16[208,128]{1,0:T(8,128)(2,1)S(1)}, u32[]{:S(2)}, u32[]{:S(2)}) %collective-permute-start) | collective-permute-done | bytes 53280 | tf_op jit(solution)/shard_map/ppermute | solution.py:58
  35.1 2.4 %collective-permute-done.1.far_ref = bf16[208,128]{1,0:T(8,128)(2,1)S(1)} collective-permute-done((bf16[208,128]{1,0:T(8,128)(2,1)}, bf16[208,128]{1,0:T(8,128)(2,1)S(1)}, u32[]{:S(2)}, u32[]{:S(2)}) %collective-permute-start.1) | collective-permute-done | bytes 53280 | tf_op jit(solution)/shard_map/ppermute | solution.py:58
  37.5 0.9 pad_maximum_fusion.sent_ref
  38.4 6.7 %collective-permute-start.4 = (bf16[832,128]{1,0:T(8,128)(2,1)S(1)}, bf16[832,128]{1,0:T(8,128)(2,1)S(1)}, u32[]{:S(2)}, u32[]{:S(2)}) collective-permute-start(bf16[832,128]{1,0:T(8,128)(2,1)S(1)} %pad_maximum_fusion.sent_ref), channel_id=1, source_target_pairs={{0,4},{4,0},{8,12},{12,8},{16,20},{20,16},{24,28},{28,24},{32,36},... | collective-permute-start | bytes 638984 | tf_op jit(solution)/shard_map/ppermute | solution.py:58
  45.2 1.1 collective-permute-done.4.swap_ref
  46.2 1.0 shard_map.114
  47.3 23.5 %all_to_all.34 = bf16[4,1024,128]{2,1,0:T(8,128)(2,1)S(1)} all-to-all(bf16[4,1024,128]{2,1,0:T(8,128)(2,1)S(1)} %bitcast.14), channel_id=1, replica_groups=mesh['pts'=128,'chan'=4] {'chan'}, dimensions={0} | all-to-all | bytes 2097152 | tf_op jit(solution)/shard_map/all_to_all | solution.py:392
  70.7 3.1 %collective-permute-start.5 = (bf16[10240,128]{1,0:T(8,128)(2,1)}, bf16[10240,128]{1,0:T(8,128)(2,1)S(1)}, u32[]{:S(2)}, u32[]{:S(2)}) collective-permute-start(bf16[10240,128]{1,0:T(8,128)(2,1)} %all-gather.2.cloned.1.call-done.mine_ref), channel_id=1, source_target_pairs={{0,4},{4,0},{8,12},{12,8},{16,20},{20,16},{24,28},{28,24},{32,36},... | collective-permute-start | bytes 7864328 | tf_op jit(solution)/shard_map/ppermute | solution.py:58
  73.9 11.9 %shard_map.115 = bf16[512,256]{1,0:T(8,128)(2,1)S(1)} custom-call(bf16[4096,128]{1,0:T(8,128)(2,1)S(1)} %bitcast.10, f32[1,512]{1,0:T(1,128)S(1)} %bitcast.20, bf16[3,512,128]{2,1,0:T(8,128)(2,1)S(1)} %copy-done.3), custom_call_target="tpu_custom_call" | custom-call | flops 8999999488 | bytes 2000000 | tf_op jit(solution)/shard_map/pallas_call | solution.py:350
  85.9 8.9 %all_to_all.35 = bf16[4,128,256]{2,1,0:T(8,128)(2,1)S(1)} all-to-all(bf16[4,128,256]{2,1,0:T(8,128)(2,1)S(1)} %bitcast.16), channel_id=1, replica_groups=mesh['pts'=128,'chan'=4] {'chan'}, dimensions={0} | all-to-all | bytes 524288 | tf_op jit(solution)/shard_map/all_to_all | solution.py:407
  94.8 2.6 %shard_map.116 = (bf16[256,512]{1,0:T(8,128)(2,1)S(1)}, f32[128,512]{1,0:T(8,128)S(1)}, bf16[128,512]{1,0:T(8,128)(2,1)S(1)}, bf16[128,512]{1,0:T(8,128)(2,1)S(1)}) custom-call(bf16[512,256]{1,0:T(8,128)(2,1)S(1)} %bitcast.15, bf16[4096,128]{1,0:T(8,128)(2,1)S(1)} %bitcast.11, f32[1,512]{1,0:T(1,128)S(1)} %bitcast.19, s32[1,1024]{1,0:T(1,128)S(1)} %bitcast.18, ...), custom_call_target="tpu_custom_call" | custom-call | tf_op jit(solution)/shard_map/pallas_call | solution.py:350
  97.4 4.3 %collective-permute-start.6 = (bf16[128,512]{1,0:T(8,128)(2,1)S(1)}, bf16[128,512]{1,0:T(8,128)(2,1)S(1)}, u32[]{:S(2)}, u32[]{:S(2)}) collective-permute-start(bf16[128,512]{1,0:T(8,128)(2,1)S(1)} %get-tuple-element.33), channel_id=1, source_target_pairs={{0,508},{4,8},{8,4},{12,16},{16,12},{20,24},{24,20},{28,32},{32,28... | collective-permute-start | bytes 393224 | tf_op jit(solution)/shard_map/ppermute | solution.py:58
  101.6 6.1 %collective-permute-start.7 = (bf16[128,512]{1,0:T(8,128)(2,1)S(1)}, bf16[128,512]{1,0:T(8,128)(2,1)S(1)}, u32[]{:S(2)}, u32[]{:S(2)}) collective-permute-start(bf16[128,512]{1,0:T(8,128)(2,1)S(1)} %get-tuple-element.34), channel_id=1, source_target_pairs={{0,4},{4,0},{8,12},{12,8},{16,20},{20,16},{24,28},{28,24},{32,36},... | collective-permute-start | bytes 393224 | tf_op jit(solution)/shard_map/ppermute | solution.py:58
  107.8 1.0 collective-permute-done.7.swap_ref
  108.7 0.1 shard_map.117
  108.8 10.2 %all_to_all.36 = bf16[4,384,128]{2,1,0:T(8,128)(2,1)S(1)} all-to-all(bf16[4,384,128]{2,1,0:T(8,128)(2,1)S(1)} %bitcast.13), channel_id=1, replica_groups=mesh['pts'=128,'chan'=4] {'chan'}, dimensions={0} | all-to-all | bytes 786432 | tf_op jit(solution)/shard_map/all_to_all | solution.py:422
  119.0 0.7 shard_map.118
  (17 shorter events, 0.0 us)
Async XLA Ops:
  7.2 63.6 %all-gather.2.cloned.1.call-start = ((), (), s32[]{:S(2)}) async-start(), calls=%async_computation.3 | async-start | bytes 3276800 | tf_op jit(solution)/shard_map/all_gather | solution.py:378
  7.2 66.7 %copy-start.3 = (bf16[3,512,128]{2,1,0:T(8,128)(2,1)S(1)}, bf16[3,512,128]{2,1,0:T(8,128)(2,1)}, u32[]{:S(2)}) copy-start(bf16[3,512,128]{2,1,0:T(8,128)(2,1)} %w_ref.1) | copy-start | bytes 1179652
  7.2 66.7 %copy-start.4 = (f32[512]{0:T(512)S(1)}, f32[512]{0:T(512)}, u32[]{:S(2)}) copy-start(f32[512]{0:T(512)} %param.13) | copy-start | bytes 6148
  11.7 25.8 %collective-permute-start.2 = (bf16[416,128]{1,0:T(8,128)(2,1)}, bf16[416,128]{1,0:T(8,128)(2,1)S(1)}, u32[]{:S(2)}, u32[]{:S(2)}) collective-permute-start(bf16[416,128]{1,0:T(8,128)(2,1)} %get-tuple-element.23), channel_id=1, source_target_pairs={{0,8},{4,12},{8,0},{12,4},{16,24},{20,28},{24,16},{28,20},{32,40},... | collective-permute-start | bytes 319496 | tf_op jit(solution)/shard_map/ppermute | solution.py:58
  16.1 21.4 %collective-permute-start.3 = (bf16[416,128]{1,0:T(8,128)(2,1)}, bf16[416,128]{1,0:T(8,128)(2,1)S(1)}, u32[]{:S(2)}, u32[]{:S(2)}) collective-permute-start(bf16[416,128]{1,0:T(8,128)(2,1)} %get-tuple-element.24), channel_id=1, source_target_pairs={{0,504},{4,508},{8,16},{12,20},{16,8},{20,12},{24,32},{28,36},{32,... | collective-permute-start | bytes 319496 | tf_op jit(solution)/shard_map/ppermute | solution.py:58
  28.5 6.6 %collective-permute-start = (bf16[208,128]{1,0:T(8,128)(2,1)}, bf16[208,128]{1,0:T(8,128)(2,1)S(1)}, u32[]{:S(2)}, u32[]{:S(2)}) collective-permute-start(bf16[208,128]{1,0:T(8,128)(2,1)} %get-tuple-element.20), channel_id=1, source_target_pairs={{0,256},{4,260},{8,264},{12,268},{16,272},{20,276},{24,280},{28,28... | collective-permute-start | bytes 159752 | tf_op jit(solution)/shard_map/ppermute | solution.py:58
  30.9 6.6 %collective-permute-start.1 = (bf16[208,128]{1,0:T(8,128)(2,1)}, bf16[208,128]{1,0:T(8,128)(2,1)S(1)}, u32[]{:S(2)}, u32[]{:S(2)}) collective-permute-start(bf16[208,128]{1,0:T(8,128)(2,1)} %get-tuple-element.21), channel_id=1, source_target_pairs={{0,500},{4,16},{8,508},{12,24},{16,4},{20,32},{24,12},{28,40},{32,... | collective-permute-start | bytes 159752 | tf_op jit(solution)/shard_map/ppermute | solution.py:58
  38.4 7.8 %collective-permute-start.4 = (bf16[832,128]{1,0:T(8,128)(2,1)S(1)}, bf16[832,128]{1,0:T(8,128)(2,1)S(1)}, u32[]{:S(2)}, u32[]{:S(2)}) collective-permute-start(bf16[832,128]{1,0:T(8,128)(2,1)S(1)} %pad_maximum_fusion.sent_ref), channel_id=1, source_target_pairs={{0,4},{4,0},{8,12},{12,8},{16,20},{20,16},{24,28},{28,24},{32,36},... | collective-permute-start | bytes 638984 | tf_op jit(solution)/shard_map/ppermute | solution.py:58
  70.7 24.0 %collective-permute-start.5 = (bf16[10240,128]{1,0:T(8,128)(2,1)}, bf16[10240,128]{1,0:T(8,128)(2,1)S(1)}, u32[]{:S(2)}, u32[]{:S(2)}) collective-permute-start(bf16[10240,128]{1,0:T(8,128)(2,1)} %all-gather.2.cloned.1.call-done.mine_ref), channel_id=1, source_target_pairs={{0,4},{4,0},{8,12},{12,8},{16,20},{20,16},{24,28},{28,24},{32,36},... | collective-permute-start | bytes 7864328 | tf_op jit(solution)/shard_map/ppermute | solution.py:58
  73.9 20.8 %copy-start = (bf16[10240,128]{1,0:T(8,128)(2,1)S(1)}, bf16[10240,128]{1,0:T(8,128)(2,1)}, u32[]{:S(2)}) copy-start(bf16[10240,128]{1,0:T(8,128)(2,1)} %all-gather.2.cloned.1.call-done.mine_ref) | copy-start | bytes 7864324
  73.9 20.8 %copy-start.1 = (s32[1024]{0:T(1024)S(1)}, s32[1024]{0:T(1024)}, u32[]{:S(2)}) copy-start(s32[1024]{0:T(1024)} %param.12) | copy-start | bytes 12292
  73.9 20.8 %copy-start.2 = (f32[512]{0:T(512)S(1)}, f32[512]{0:T(512)}, u32[]{:S(2)}) copy-start(f32[512]{0:T(512)} %param.16) | copy-start | bytes 6148
  97.4 10.4 %collective-permute-start.6 = (bf16[128,512]{1,0:T(8,128)(2,1)S(1)}, bf16[128,512]{1,0:T(8,128)(2,1)S(1)}, u32[]{:S(2)}, u32[]{:S(2)}) collective-permute-start(bf16[128,512]{1,0:T(8,128)(2,1)S(1)} %get-tuple-element.33), channel_id=1, source_target_pairs={{0,508},{4,8},{8,4},{12,16},{16,12},{20,24},{24,20},{28,32},{32,28... | collective-permute-start | bytes 393224 | tf_op jit(solution)/shard_map/ppermute | solution.py:58
  101.6 7.1 %collective-permute-start.7 = (bf16[128,512]{1,0:T(8,128)(2,1)S(1)}, bf16[128,512]{1,0:T(8,128)(2,1)S(1)}, u32[]{:S(2)}, u32[]{:S(2)}) collective-permute-start(bf16[128,512]{1,0:T(8,128)(2,1)S(1)} %get-tuple-element.34), channel_id=1, source_target_pairs={{0,4},{4,0},{8,12},{12,8},{16,20},{20,16},{24,28},{28,24},{32,36},... | collective-permute-start | bytes 393224 | tf_op jit(solution)/shard_map/ppermute | solution.py:58
Sparse Core Ops, SparseCore 0:
  11.8 55.2 all-gather.1

commit v6 on v5

--- a/solution.py
+++ b/solution.py
@@ -158,32 +158,34 @@
         ref[base + CAP : base + BLOCK, :] = notes.astype(BF16)
 
 
+def weights_kernel(w_out_ref, w_fc1_ref, w_fc2_ref, w_pool_ref, out_ref, sems):
+    core = lax.rem(lax.axis_index("pts"), 2)
+    start = copier(sems)
+    half = pl.multiple_of(core * HALF, HALF)
+    quarter = pl.multiple_of(core * 64, 64)
+    copies = []
+    for r in range(2):
+        src = w_fc1_ref.at[:, pl.ds(pl.multiple_of(half + r * 128, 128), 128)]
+        copies.append(start(src, out_ref.at[FC1 + r * C : FC1 + (r + 1) * C, :]))
+    for r in range(4):
+        cols = slice(r * 128, (r + 1) * 128)
+        dst = out_ref.at[FC2 + r * HALF : FC2 + (r + 1) * HALF, :]
+        copies.append(start(w_fc2_ref.at[pl.ds(half, HALF), cols], dst))
+        dst = out_ref.at[r * 64 : (r + 1) * 64, :]
+        copies.append(start(w_out_ref.at[pl.ds(quarter, 64), cols], dst))
+    copies.append(start(w_pool_ref.at[pl.ds(half, HALF), :], out_ref.at[POOL:WROWS, :]))
+    wait(copies)
+
+
 def pack_kernel(
-    feats_ref, dest_ref, cell_ref, w_out_ref, w_fc1_ref, w_fc2_ref, w_pool_ref,
-    up_ref, down_ref, swap_ref, far_ref, across_ref, weights_ref,
+    feats_ref, dest_ref, cell_ref, up_ref, down_ref, swap_ref, far_ref, across_ref,
     feats_here, dest_here, cell_here, sems,
 ):
     me = lax.axis_index("pts")
-    core = lax.rem(me, 2)
     start = copier(sems)
     dest_copy = start(dest_ref, dest_here)
     cell_copy = start(cell_ref, cell_here)
     feats_copy = start(feats_ref, feats_here)
-
-    half = pl.multiple_of(core * HALF, HALF)
-    quarter = pl.multiple_of(core * 64, 64)
-    weight_copies = []
-    for r in range(2):
-        src = w_fc1_ref.at[:, pl.ds(pl.multiple_of(half + r * 128, 128), 128)]
-        weight_copies.append(start(src, weights_ref.at[FC1 + r * C : FC1 + (r + 1) * C, :]))
-    for r in range(4):
-        cols = slice(r * 128, (r + 1) * 128)
-        dst = weights_ref.at[FC2 + r * HALF : FC2 + (r + 1) * HALF, :]
-        weight_copies.append(start(w_fc2_ref.at[pl.ds(half, HALF), cols], dst))
-        dst = weights_ref.at[r * 64 : (r + 1) * 64, :]
-        weight_copies.append(start(w_out_ref.at[pl.ds(quarter, 64), cols], dst))
-    weight_copies.append(start(w_pool_ref.at[pl.ds(half, HALF), :], weights_ref.at[POOL:WROWS, :]))
-
     before = lax.broadcasted_iota(jnp.int32, (ROWS, ROWS), 0)
     after = lax.broadcasted_iota(jnp.int32, (ROWS, ROWS), 1)
     earlier = jnp.where(before < after, 1.0, 0.0).astype(BF16)
@@ -208,7 +210,6 @@
     counts = cell_counts(cell_here[...], me)
     wait([feats_copy])
     write_blocks(slot, dest, feats_here[...], blocks, counts)
-    wait(weight_copies)
 
 
 def unpack_kernel(sent_ref, down_ref, up_ref, across_ref, far_ref, swap_ref, out_ref, count_ref, held):
@@ -362,25 +363,33 @@
     def block(count=1):
         return ((count * BLOCK, LANES), BF16)
 
-    up, down, swap, far, over, weights = call(
+    (weights,) = call(
+        weights_kernel,
+        [((WROWS, LANES), BF16)],
+        (w_out, w_fc1, w_fc2, w_pool),
+        scratch=[pltpu.SemaphoreType.DMA((11,))],
+        limit=ALL_VMEM,
+        in_hbm=range(4),
+    )
+    weights = lax.all_gather(weights, "chan", axis=0, tiled=True)
+    up, down, swap, far, over = call(
         pack_kernel,
-        [block(2), block(2), block(2), block(), block(), ((WROWS, LANES), BF16)],
-        (feats, dest_pos.reshape(1, ROWS), cell_id.reshape(1, ROWS), w_out, w_fc1, w_fc2, w_pool),
+        [block(2), block(2), block(2), block(), block()],
+        (feats, dest_pos.reshape(1, ROWS), cell_id.reshape(1, ROWS)),
         scratch=[
             pltpu.VMEM((ROWS, LANES), BF16),
             pltpu.VMEM((1, ROWS), jnp.int32),
             pltpu.VMEM((1, ROWS), jnp.int32),
-            pltpu.SemaphoreType.DMA((14,)),
+            pltpu.SemaphoreType.DMA((3,)),
         ],
         limit=ALL_VMEM,
-        in_hbm=range(7),
-    )
-    weights = lax.all_gather(weights, "chan", axis=0, tiled=True)
+        in_hbm=range(3),
+    )
+    far = exchange(far, far_pair)
+    over = exchange(over, across)
     down = exchange(down, chip_down)
+    up, far, over = lax.optimization_barrier((up, far, over))
     up = exchange(up, chip_up)
-    over = exchange(over, across)
-    far = exchange(far, far_pair)
-    swap, over, far = lax.optimization_barrier((swap, over, far))
     sent = jnp.concatenate([swap, up[BLOCK:], down[BLOCK:]], axis=0)
     swap = exchange(sent, core_swap)
     ordered, count = call(

time: 127 us -> 125 us (0.984)
  blocking collectives: 42.6 us -> 40.3 us
  Pallas kernels: 20.8 us -> 22.5 us
    all_to_all x1, blocking collectives: 23.5 us -> 21.2 us  [body(): lax.all_to_all(ordered, 'chan', split_axis=0, concat_axis=0, tiled=True)]
    pallas_call x6 -> x7, Pallas kernels: 20.8 us -> 22.5 us  [call(): pl.pallas_call(kernel, out_shape=[jax.ShapeDtypeStruct(shape, dtype) for...]
  transfers between devices with their start and end apart: 9 -> 9, of which waited for: 4 -> 4; matrix products, arithmetic and copies ran while one was open for 1% -> 1% of each run, Pallas kernels for 10% -> 14%
where the time goes in v6:
time: 125 us
  starting transfers between devices  40.5 us (32%)
  blocking collectives  40.3 us (32%)
  Pallas kernels  22.5 us (18%)
  between operations  14.2 us (11%)
  waiting for transfers between devices  6.18 us (5%)
    ppermute x8, starting transfers between devices, exchange(): return lax.ppermute(x, 'pts', [(i, partner(i)) for i in range(N_PTS)])  40.5 us
    pallas_call x7, Pallas kernels, call(): pl.pallas_call(kernel, out_shape=[jax.ShapeDtypeStruct(shape, dtype) for...  22.5 us
    all_to_all x1, blocking collectives, body(): lax.all_to_all(ordered, 'chan', split_axis=0, concat_axis=0, tiled=True)  21.2 us
    all_to_all x1, blocking collectives, body(): lax.all_to_all(message, 'chan', split_axis=0, concat_axis=0, tiled=True)  10.2 us
    all_to_all x1, blocking collectives, body(): attn = lax.all_to_all(attn, 'chan', split_axis=0, concat_axis=0, tiled=True)  8.86 us
    ppermute x8, waiting for transfers between devices, exchange(): return lax.ppermute(x, 'pts', [(i, partner(i)) for i in range(N_PTS)])  6.16 us
  transfers between devices with their start and end apart: 9, of which 4 were waited for; matrix products, arithmetic and copies ran while one was open for 1% of the time, Pallas kernels for 14%

profile of v6, /device:TPU:1, one launch (start us, length us, event | category | flops | bytes accessed | tf_op | source)
XLA Modules:
  0.0 124.7 jit_solution(14402187098054968315)
XLA Ops:
  7.2 0.0 all-gather.2.cloned.1.call-start
  7.2 2.1 %shard_map.115 = bf16[2560,128]{1,0:T(8,128)(2,1)} custom-call(bf16[128,512]{1,0:T(8,128)(2,1)} %w_out_ref.1, bf16[512,512]{1,0:T(8,128)(2,1)} %w_fc1_ref.1, bf16[512,512]{1,0:T(8,128)(2,1)} %w_fc2_ref.1, bf16[512,128]{1,0:T(8,128)(2,1)} %w_pool_ref.1), custom_call_target="tpu_custom_call" | custom-call | tf_op jit(solution)/shard_map/pallas_call | solution.py:351
  9.4 4.0 %shard_map.113 = (bf16[416,128]{1,0:T(8,128)(2,1)}, bf16[416,128]{1,0:T(8,128)(2,1)}, bf16[416,128]{1,0:T(8,128)(2,1)}, bf16[208,128]{1,0:T(8,128)(2,1)}, bf16[208,128]{1,0:T(8,128)(2,1)}) custom-call(bf16[1024,128]{1,0:T(8,128)(2,1)} %feats_ref.1, s32[1,1024]{1,0:T(1,128)} %bitcast.21, s32[1,1024]{1,0:T(1,128)} %bitcast.17), custom_call_target="tpu_custom_call" | custom-call | tf_op jit(solution)/shard_map/pallas_call | solution.py:351
  13.4 6.3 %collective-permute-start = (bf16[208,128]{1,0:T(8,128)(2,1)}, bf16[208,128]{1,0:T(8,128)(2,1)S(1)}, u32[]{:S(2)}, u32[]{:S(2)}) collective-permute-start(bf16[208,128]{1,0:T(8,128)(2,1)} %get-tuple-element.20), channel_id=1, source_target_pairs={{0,500},{4,16},{8,508},{12,24},{16,4},{20,32},{24,12},{28,40},{32,... | collective-permute-start | bytes 159752 | tf_op jit(solution)/shard_map/ppermute | solution.py:58
  19.7 4.7 %collective-permute-start.1 = (bf16[208,128]{1,0:T(8,128)(2,1)}, bf16[208,128]{1,0:T(8,128)(2,1)S(1)}, u32[]{:S(2)}, u32[]{:S(2)}) collective-permute-start(bf16[208,128]{1,0:T(8,128)(2,1)} %get-tuple-element.21), channel_id=1, source_target_pairs={{0,256},{4,260},{8,264},{12,268},{16,272},{20,276},{24,280},{28,28... | collective-permute-start | bytes 159752 | tf_op jit(solution)/shard_map/ppermute | solution.py:58
  24.3 8.2 %collective-permute-start.3 = (bf16[416,128]{1,0:T(8,128)(2,1)}, bf16[416,128]{1,0:T(8,128)(2,1)S(1)}, u32[]{:S(2)}, u32[]{:S(2)}) collective-permute-start(bf16[416,128]{1,0:T(8,128)(2,1)} %get-tuple-element.23), channel_id=1, source_target_pairs={{0,504},{4,508},{8,16},{12,20},{16,8},{20,12},{24,32},{28,36},{32,... | collective-permute-start | bytes 319496 | tf_op jit(solution)/shard_map/ppermute | solution.py:58
  32.5 1.9 %collective-permute-start.2 = (bf16[416,128]{1,0:T(8,128)(2,1)}, bf16[416,128]{1,0:T(8,128)(2,1)S(1)}, u32[]{:S(2)}, u32[]{:S(2)}) collective-permute-start(bf16[416,128]{1,0:T(8,128)(2,1)} %get-tuple-element.22), channel_id=1, source_target_pairs={{0,8},{4,12},{8,0},{12,4},{16,24},{20,28},{24,16},{28,20},{32,40},... | collective-permute-start | bytes 319496 | tf_op jit(solution)/shard_map/ppermute | solution.py:58
  34.4 0.3 collective-permute-done.3.down_ref
  34.8 3.8 %collective-permute-done.2.up_ref = bf16[416,128]{1,0:T(8,128)(2,1)S(1)} collective-permute-done((bf16[416,128]{1,0:T(8,128)(2,1)}, bf16[416,128]{1,0:T(8,128)(2,1)S(1)}, u32[]{:S(2)}, u32[]{:S(2)}) %collective-permute-start.2) | collective-permute-done | bytes 106528 | tf_op jit(solution)/shard_map/ppermute | solution.py:58
  38.6 0.9 pad_maximum_fusion.sent_ref
  39.5 6.2 %collective-permute-start.4 = (bf16[832,128]{1,0:T(8,128)(2,1)S(1)}, bf16[832,128]{1,0:T(8,128)(2,1)S(1)}, u32[]{:S(2)}, u32[]{:S(2)}) collective-permute-start(bf16[832,128]{1,0:T(8,128)(2,1)S(1)} %pad_maximum_fusion.sent_ref), channel_id=1, source_target_pairs={{0,4},{4,0},{8,12},{12,8},{16,20},{20,16},{24,28},{28,24},{32,36},... | collective-permute-start | bytes 638984 | tf_op jit(solution)/shard_map/ppermute | solution.py:58
  45.7 1.1 collective-permute-done.4.swap_ref
  46.8 1.0 shard_map.114
  47.8 21.2 %all_to_all.34 = bf16[4,1024,128]{2,1,0:T(8,128)(2,1)S(1)} all-to-all(bf16[4,1024,128]{2,1,0:T(8,128)(2,1)S(1)} %bitcast.14), channel_id=1, replica_groups=mesh['pts'=128,'chan'=4] {'chan'}, dimensions={0} | all-to-all | bytes 2097152 | tf_op jit(solution)/shard_map/all_to_all | solution.py:401
  69.1 3.1 %collective-permute-start.5 = (bf16[10240,128]{1,0:T(8,128)(2,1)}, bf16[10240,128]{1,0:T(8,128)(2,1)S(1)}, u32[]{:S(2)}, u32[]{:S(2)}) collective-permute-start(bf16[10240,128]{1,0:T(8,128)(2,1)} %all-gather.2.cloned.1.call-done.mine_ref), channel_id=1, source_target_pairs={{0,4},{4,0},{8,12},{12,8},{16,20},{20,16},{24,28},{28,24},{32,36},... | collective-permute-start | bytes 7864328 | tf_op jit(solution)/shard_map/ppermute | solution.py:58
  72.3 11.9 %shard_map.116 = bf16[512,256]{1,0:T(8,128)(2,1)S(1)} custom-call(bf16[4096,128]{1,0:T(8,128)(2,1)S(1)} %bitcast.10, f32[1,512]{1,0:T(1,128)S(1)} %bitcast.20, bf16[3,512,128]{2,1,0:T(8,128)(2,1)S(1)} %copy-done.3), custom_call_target="tpu_custom_call" | custom-call | flops 8999999488 | bytes 2000000 | tf_op jit(solution)/shard_map/pallas_call | solution.py:351
  84.2 8.9 %all_to_all.35 = bf16[4,128,256]{2,1,0:T(8,128)(2,1)S(1)} all-to-all(bf16[4,128,256]{2,1,0:T(8,128)(2,1)S(1)} %bitcast.16), channel_id=1, replica_groups=mesh['pts'=128,'chan'=4] {'chan'}, dimensions={0} | all-to-all | bytes 524288 | tf_op jit(solution)/shard_map/all_to_all | solution.py:416
  93.1 2.6 %shard_map.117 = (bf16[256,512]{1,0:T(8,128)(2,1)S(1)}, f32[128,512]{1,0:T(8,128)S(1)}, bf16[128,512]{1,0:T(8,128)(2,1)S(1)}, bf16[128,512]{1,0:T(8,128)(2,1)S(1)}) custom-call(bf16[512,256]{1,0:T(8,128)(2,1)S(1)} %bitcast.15, bf16[4096,128]{1,0:T(8,128)(2,1)S(1)} %bitcast.11, f32[1,512]{1,0:T(1,128)S(1)} %bitcast.19, s32[1,1024]{1,0:T(1,128)S(1)} %bitcast.18, ...), custom_call_target="tpu_custom_call" | custom-call | tf_op jit(solution)/shard_map/pallas_call | solution.py:351
  95.7 4.2 %collective-permute-start.6 = (bf16[128,512]{1,0:T(8,128)(2,1)S(1)}, bf16[128,512]{1,0:T(8,128)(2,1)S(1)}, u32[]{:S(2)}, u32[]{:S(2)}) collective-permute-start(bf16[128,512]{1,0:T(8,128)(2,1)S(1)} %get-tuple-element.31), channel_id=1, source_target_pairs={{0,508},{4,8},{8,4},{12,16},{16,12},{20,24},{24,20},{28,32},{32,28... | collective-permute-start | bytes 393224 | tf_op jit(solution)/shard_map/ppermute | solution.py:58
  99.9 5.9 %collective-permute-start.7 = (bf16[128,512]{1,0:T(8,128)(2,1)S(1)}, bf16[128,512]{1,0:T(8,128)(2,1)S(1)}, u32[]{:S(2)}, u32[]{:S(2)}) collective-permute-start(bf16[128,512]{1,0:T(8,128)(2,1)S(1)} %get-tuple-element.32), channel_id=1, source_target_pairs={{0,4},{4,0},{8,12},{12,8},{16,20},{20,16},{24,28},{28,24},{32,36},... | collective-permute-start | bytes 393224 | tf_op jit(solution)/shard_map/ppermute | solution.py:58
  105.8 1.0 collective-permute-done.7.swap_ref
  106.8 0.1 shard_map.118
  106.9 10.2 %all_to_all.36 = bf16[4,384,128]{2,1,0:T(8,128)(2,1)S(1)} all-to-all(bf16[4,384,128]{2,1,0:T(8,128)(2,1)S(1)} %bitcast.13), channel_id=1, replica_groups=mesh['pts'=128,'chan'=4] {'chan'}, dimensions={0} | all-to-all | bytes 786432 | tf_op jit(solution)/shard_map/all_to_all | solution.py:431
  117.1 0.7 shard_map.119
  (18 shorter events, 0.1 us)
Async XLA Ops:
  7.2 61.9 %all-gather.2.cloned.1.call-start = ((), (), s32[]{:S(2)}) async-start(), calls=%async_computation.3 | async-start | bytes 3276800 | tf_op jit(solution)/shard_map/all_gather | solution.py:374
  9.3 62.9 %copy-start.3 = (bf16[3,512,128]{2,1,0:T(8,128)(2,1)S(1)}, bf16[3,512,128]{2,1,0:T(8,128)(2,1)}, u32[]{:S(2)}) copy-start(bf16[3,512,128]{2,1,0:T(8,128)(2,1)} %w_ref.1) | copy-start | bytes 1179652
  9.3 62.9 %copy-start.4 = (f32[512]{0:T(512)S(1)}, f32[512]{0:T(512)}, u32[]{:S(2)}) copy-start(f32[512]{0:T(512)} %param.13) | copy-start | bytes 6148
  13.4 19.1 %collective-permute-start = (bf16[208,128]{1,0:T(8,128)(2,1)}, bf16[208,128]{1,0:T(8,128)(2,1)S(1)}, u32[]{:S(2)}, u32[]{:S(2)}) collective-permute-start(bf16[208,128]{1,0:T(8,128)(2,1)} %get-tuple-element.20), channel_id=1, source_target_pairs={{0,500},{4,16},{8,508},{12,24},{16,4},{20,32},{24,12},{28,40},{32,... | collective-permute-start | bytes 159752 | tf_op jit(solution)/shard_map/ppermute | solution.py:58
  19.7 12.8 %collective-permute-start.1 = (bf16[208,128]{1,0:T(8,128)(2,1)}, bf16[208,128]{1,0:T(8,128)(2,1)S(1)}, u32[]{:S(2)}, u32[]{:S(2)}) collective-permute-start(bf16[208,128]{1,0:T(8,128)(2,1)} %get-tuple-element.21), channel_id=1, source_target_pairs={{0,256},{4,260},{8,264},{12,268},{16,272},{20,276},{24,280},{28,28... | collective-permute-start | bytes 159752 | tf_op jit(solution)/shard_map/ppermute | solution.py:58
  24.3 10.5 %collective-permute-start.3 = (bf16[416,128]{1,0:T(8,128)(2,1)}, bf16[416,128]{1,0:T(8,128)(2,1)S(1)}, u32[]{:S(2)}, u32[]{:S(2)}) collective-permute-start(bf16[416,128]{1,0:T(8,128)(2,1)} %get-tuple-element.23), channel_id=1, source_target_pairs={{0,504},{4,508},{8,16},{12,20},{16,8},{20,12},{24,32},{28,36},{32,... | collective-permute-start | bytes 319496 | tf_op jit(solution)/shard_map/ppermute | solution.py:58
  32.5 6.1 %collective-permute-start.2 = (bf16[416,128]{1,0:T(8,128)(2,1)}, bf16[416,128]{1,0:T(8,128)(2,1)S(1)}, u32[]{:S(2)}, u32[]{:S(2)}) collective-permute-start(bf16[416,128]{1,0:T(8,128)(2,1)} %get-tuple-element.22), channel_id=1, source_target_pairs={{0,8},{4,12},{8,0},{12,4},{16,24},{20,28},{24,16},{28,20},{32,40},... | collective-permute-start | bytes 319496 | tf_op jit(solution)/shard_map/ppermute | solution.py:58
  39.5 7.3 %collective-permute-start.4 = (bf16[832,128]{1,0:T(8,128)(2,1)S(1)}, bf16[832,128]{1,0:T(8,128)(2,1)S(1)}, u32[]{:S(2)}, u32[]{:S(2)}) collective-permute-start(bf16[832,128]{1,0:T(8,128)(2,1)S(1)} %pad_maximum_fusion.sent_ref), channel_id=1, source_target_pairs={{0,4},{4,0},{8,12},{12,8},{16,20},{20,16},{24,28},{28,24},{32,36},... | collective-permute-start | bytes 638984 | tf_op jit(solution)/shard_map/ppermute | solution.py:58
  69.1 24.0 %collective-permute-start.5 = (bf16[10240,128]{1,0:T(8,128)(2,1)}, bf16[10240,128]{1,0:T(8,128)(2,1)S(1)}, u32[]{:S(2)}, u32[]{:S(2)}) collective-permute-start(bf16[10240,128]{1,0:T(8,128)(2,1)} %all-gather.2.cloned.1.call-done.mine_ref), channel_id=1, source_target_pairs={{0,4},{4,0},{8,12},{12,8},{16,20},{20,16},{24,28},{28,24},{32,36},... | collective-permute-start | bytes 7864328 | tf_op jit(solution)/shard_map/ppermute | solution.py:58
  72.2 20.8 %copy-start = (bf16[10240,128]{1,0:T(8,128)(2,1)S(1)}, bf16[10240,128]{1,0:T(8,128)(2,1)}, u32[]{:S(2)}) copy-start(bf16[10240,128]{1,0:T(8,128)(2,1)} %all-gather.2.cloned.1.call-done.mine_ref) | copy-start | bytes 7864324
  72.2 20.8 %copy-start.1 = (s32[1024]{0:T(1024)S(1)}, s32[1024]{0:T(1024)}, u32[]{:S(2)}) copy-start(s32[1024]{0:T(1024)} %param.12) | copy-start | bytes 12292
  72.2 20.8 %copy-start.2 = (f32[512]{0:T(512)S(1)}, f32[512]{0:T(512)}, u32[]{:S(2)}) copy-start(f32[512]{0:T(512)} %param.16) | copy-start | bytes 6148
  95.7 10.1 %collective-permute-start.6 = (bf16[128,512]{1,0:T(8,128)(2,1)S(1)}, bf16[128,512]{1,0:T(8,128)(2,1)S(1)}, u32[]{:S(2)}, u32[]{:S(2)}) collective-permute-start(bf16[128,512]{1,0:T(8,128)(2,1)S(1)} %get-tuple-element.31), channel_id=1, source_target_pairs={{0,508},{4,8},{8,4},{12,16},{16,12},{20,24},{24,20},{28,32},{32,28... | collective-permute-start | bytes 393224 | tf_op jit(solution)/shard_map/ppermute | solution.py:58
  99.9 6.8 %collective-permute-start.7 = (bf16[128,512]{1,0:T(8,128)(2,1)S(1)}, bf16[128,512]{1,0:T(8,128)(2,1)S(1)}, u32[]{:S(2)}, u32[]{:S(2)}) collective-permute-start(bf16[128,512]{1,0:T(8,128)(2,1)S(1)} %get-tuple-element.32), channel_id=1, source_target_pairs={{0,4},{4,0},{8,12},{12,8},{16,20},{20,16},{24,28},{28,24},{32,36},... | collective-permute-start | bytes 393224 | tf_op jit(solution)/shard_map/ppermute | solution.py:58
Sparse Core Ops, SparseCore 0:
  10.1 50.7 all-gather.1

commit v7 on v6

--- a/solution.py
+++ b/solution.py
@@ -21,9 +21,9 @@
 BLOCK = CAP + 16
 KINDS = 8
 SLOTS = KINDS * CAP
-HALF = 256
+SHARE = 128
 STEP = 512
-FC1, FC2, POOL, WROWS = 256, 1280, 2304, 2560
+FC1, FC2, POOL, WROWS = 128, 640, 1152, 1280
 MESSAGE = QUARTER + CELLS
 VMEM_LIMIT = 32 * 1024 * 1024
 SOME_VMEM = 32 * 1024 * 1024
@@ -158,22 +158,23 @@
         ref[base + CAP : base + BLOCK, :] = notes.astype(BF16)
 
 
+def quarter_of(me):
+    return lax.rem(me, 4)
+
+
 def weights_kernel(w_out_ref, w_fc1_ref, w_fc2_ref, w_pool_ref, out_ref, sems):
-    core = lax.rem(lax.axis_index("pts"), 2)
+    mine = quarter_of(lax.axis_index("pts"))
     start = copier(sems)
-    half = pl.multiple_of(core * HALF, HALF)
-    quarter = pl.multiple_of(core * 64, 64)
-    copies = []
-    for r in range(2):
-        src = w_fc1_ref.at[:, pl.ds(pl.multiple_of(half + r * 128, 128), 128)]
-        copies.append(start(src, out_ref.at[FC1 + r * C : FC1 + (r + 1) * C, :]))
+    share = pl.multiple_of(mine * SHARE, SHARE)
+    few = pl.multiple_of(mine * 32, 32)
+    copies = [start(w_fc1_ref.at[:, pl.ds(share, SHARE)], out_ref.at[FC1 : FC1 + C, :])]
     for r in range(4):
         cols = slice(r * 128, (r + 1) * 128)
-        dst = out_ref.at[FC2 + r * HALF : FC2 + (r + 1) * HALF, :]
-        copies.append(start(w_fc2_ref.at[pl.ds(half, HALF), cols], dst))
-        dst = out_ref.at[r * 64 : (r + 1) * 64, :]
-        copies.append(start(w_out_ref.at[pl.ds(quarter, 64), cols], dst))
-    copies.append(start(w_pool_ref.at[pl.ds(half, HALF), :], out_ref.at[POOL:WROWS, :]))
+        dst = out_ref.at[FC2 + r * SHARE : FC2 + (r + 1) * SHARE, :]
+        copies.append(start(w_fc2_ref.at[pl.ds(share, SHARE), cols], dst))
+        dst = out_ref.at[r * 32 : (r + 1) * 32, :]
+        copies.append(start(w_out_ref.at[pl.ds(few, 32), cols], dst))
+    copies.append(start(w_pool_ref.at[pl.ds(share, SHARE), :], out_ref.at[POOL:WROWS, :]))
     wait(copies)
 
 
@@ -268,7 +269,7 @@
 
 
 def mlp_kernel(
-    attn_ref, x_ref, gain_ref, cell_ref, mine_ref, other_ref,
+    attn_ref, x_ref, gain_ref, cell_ref, mine_ref, chip_ref, core_ref, both_ref,
     block_ref, own_ref, swap_ref, next_ref,
 ):
     chan = lax.axis_index("chan")
@@ -283,36 +284,38 @@
         return jnp.concatenate(parts, axis=0)
 
     x = jnp.concatenate([x_ref[pl.ds(c * ROWS + row, QUARTER), :] for c in range(4)], axis=1)
-    halves = ((core, mine_ref), (1 - core, other_ref))
+    q = quarter_of(me)
+    other_core = q + 1 - 2 * core
+    quarters = [
+        (q, mine_ref), (lax.rem(q + 2, 4), chip_ref),
+        (other_core, core_ref), (lax.rem(other_core + 2, 4), both_ref),
+    ]
     rows, w_out = [], []
-    for which, ref in halves:
+    for which, ref in quarters:
         for c in range(4):
-            rows.append(attn_ref[pl.ds(pl.multiple_of(c * 128 + which * 64, 64), 64), :])
-            w_out.append(columns(ref, c * WROWS, 64, 4))
+            rows.append(attn_ref[pl.ds(pl.multiple_of(c * 128 + which * 32, 32), 32), :])
+            w_out.append(columns(ref, c * WROWS, 32, 4))
     mid = (x.astype(F32) + matmul_tn(stacked(rows), stacked(w_out))).astype(BF16).astype(F32)
     normed = normed_chunks([mid], [gain_ref[...]])[0]
     summed = None
-    for _, ref in halves:
-        for c in range(0, 4, 2):
-            bases = (c * WROWS, (c + 1) * WROWS)
-            w_fc1 = jnp.concatenate([columns(ref, base + FC1, C, 2) for base in bases], axis=1)
-            w_fc2 = stacked([columns(ref, base + FC2, HALF, 4) for base in bases])
-            act = gelu(matmul(normed, w_fc1)).astype(BF16)
-            term = matmul(act, w_fc2)
-            summed = term if summed is None else summed + term
+    for _, ref in quarters:
+        bases = [c * WROWS for c in range(4)]
+        w_fc1 = jnp.concatenate([ref[base + FC1 : base + FC1 + C, :] for base in bases], axis=1)
+        w_fc2 = stacked([columns(ref, base + FC2, SHARE, 4) for base in bases])
+        act = gelu(matmul(normed, w_fc1)).astype(BF16)
+        term = matmul(act, w_fc2)
+        summed = term if summed is None else summed + term
     block = (mid + summed).astype(BF16)
-    left, right = block[:, :HALF].astype(F32), block[:, HALF:].astype(F32)
-    lin = None
-    for which, ref in halves:
-        mine = jnp.where(which == 0, left, right).astype(BF16)
-        w_pool = jnp.concatenate([ref[c * WROWS + POOL : (c + 1) * WROWS, :] for c in range(4)], axis=1)
-        term = matmul(mine, w_pool)
-        lin = term if lin is None else lin + term
+    block_ref[...] = block
+    parts, w_pool = [], []
+    for which, ref in quarters:
+        parts.append(block_ref[:, pl.ds(pl.multiple_of(which * 128, 128), 128)])
+        w_pool.append(jnp.concatenate([ref[c * WROWS + POOL : (c + 1) * WROWS, :] for c in range(4)], axis=1))
+    lin = matmul(jnp.concatenate(parts, axis=1), stacked(w_pool))
     high = lin.astype(BF16)
     low = (lin - high.astype(F32)).astype(BF16)
     member = one_hot(cell_ref[:, pl.ds(row, QUARTER)] - (me - 1) * CELLS, 3 * CELLS)
     sums = matmul(member, high) + matmul(member, low)
-    block_ref[...] = block
     own_ref[...] = sums[CELLS : 2 * CELLS]
     before = sums[:CELLS].astype(BF16)
     after = sums[2 * CELLS :].astype(BF16)
@@ -367,7 +370,7 @@
         weights_kernel,
         [((WROWS, LANES), BF16)],
         (w_out, w_fc1, w_fc2, w_pool),
-        scratch=[pltpu.SemaphoreType.DMA((11,))],
+        scratch=[pltpu.SemaphoreType.DMA((10,))],
         limit=ALL_VMEM,
         in_hbm=range(4),
     )
@@ -398,9 +401,11 @@
         (sent, down, up, over, far, swap),
         scratch=[pltpu.VMEM((SLOTS, LANES), BF16)],
     )
+    ordered, weights = lax.optimization_barrier((ordered, weights))
+    from_chip = exchange(weights, chip_up)
     full = lax.all_to_all(ordered, "chan", split_axis=0, concat_axis=0, tiled=True)
     full, weights = lax.optimization_barrier((full, weights))
-    others = exchange(weights, core_swap)
+    from_core = exchange(weights, core_swap)
     (attn,) = call(
         attention_kernel,
         [((N_CHAN * LANES, QUARTER), BF16)],
@@ -413,12 +418,14 @@
             pltpu.VMEM((LANES, ROWS), BF16),
         ],
     )
+    attn, from_chip = lax.optimization_barrier((attn, from_chip))
+    from_both = exchange(from_chip, core_swap)
     attn = lax.all_to_all(attn, "chan", split_axis=0, concat_axis=0, tiled=True)
     cell_sum = ((CELLS, C), BF16)
     rows, mine, for_swap, for_next = call(
         mlp_kernel,
         [((QUARTER, C), BF16), ((CELLS, C), F32), cell_sum, cell_sum],
-        (attn, full, ln2_gain.reshape(1, C), cell_id.reshape(1, ROWS), weights, others),
+        (attn, full, ln2_gain.reshape(1, C), cell_id.reshape(1, ROWS), weights, from_chip, from_core, from_both),
         limit=SOME_VMEM,
     )
     from_next = exchange(for_next, next_pair)

time: 125 us -> 129 us (1.032)
  blocking collectives: 40.3 us -> 19.2 us
  waiting for transfers between devices: 6.18 us -> 19.6 us
  starting transfers between devices: 40.5 us -> 49.2 us
  Pallas kernels: 22.5 us -> 24.4 us
    all_to_all x1 -> x0, blocking collectives: 21.2 us -> none  [body(): lax.all_to_all(ordered, 'chan', split_axis=0, concat_axis=0, tiled=True)]
    all_to_all x0 -> x1, waiting for transfers between devices: none -> 11.9 us  [body(): lax.all_to_all(ordered, 'chan', split_axis=0, concat_axis=0, tiled=True)]
    ppermute x8 -> x10, starting transfers between devices: 40.5 us -> 44.8 us  [exchange(): return lax.ppermute(x, 'pts', [(i, partner(i)) for i in range(N_PTS)])]
    all_to_all x0 -> x1, starting transfers between devices: none -> 4.31 us  [body(): lax.all_to_all(ordered, 'chan', split_axis=0, concat_axis=0, tiled=True)]
    pallas_call x7, Pallas kernels: 22.5 us -> 24.4 us  [call(): pl.pallas_call(kernel, out_shape=[jax.ShapeDtypeStruct(shape, dtype) for...]
    all_to_all x1, blocking collectives: 8.86 us -> 10.5 us  [body(): attn = lax.all_to_all(attn, 'chan', split_axis=0, concat_axis=0, tiled=True)]
    all_to_all x1, blocking collectives: 10.2 us -> 8.62 us  [body(): lax.all_to_all(message, 'chan', split_axis=0, concat_axis=0, tiled=True)]
    ppermute x8 -> x10, waiting for transfers between devices: 6.16 us -> 7.71 us  [exchange(): return lax.ppermute(x, 'pts', [(i, partner(i)) for i in range(N_PTS)])]
  transfers between devices with their start and end apart: 9 -> 12, of which waited for: 4 -> 6; matrix products, arithmetic and copies ran while one was open for 1% -> 1% of each run, Pallas kernels for 14% -> 14%
where the time goes in v7:
time: 129 us; the launch traced here: 128 us
  starting transfers between devices  49.2 us (38%)
  Pallas kernels  24.4 us (19%)
  waiting for transfers between devices  19.6 us (15%)
  blocking collectives  19.2 us (15%)
  between operations  14.2 us (11%)
    ppermute x10, starting transfers between devices, exchange(): return lax.ppermute(x, 'pts', [(i, partner(i)) for i in range(N_PTS)])  44.8 us
    pallas_call x7, Pallas kernels, call(): pl.pallas_call(kernel, out_shape=[jax.ShapeDtypeStruct(shape, dtype) for...  24.4 us
    all_to_all x1, waiting for transfers between devices, body(): lax.all_to_all(ordered, 'chan', split_axis=0, concat_axis=0, tiled=True)  11.9 us
    all_to_all x1, blocking collectives, body(): attn = lax.all_to_all(attn, 'chan', split_axis=0, concat_axis=0, tiled=True)  10.5 us
    all_to_all x1, blocking collectives, body(): lax.all_to_all(message, 'chan', split_axis=0, concat_axis=0, tiled=True)  8.62 us
    ppermute x10, waiting for transfers between devices, exchange(): return lax.ppermute(x, 'pts', [(i, partner(i)) for i in range(N_PTS)])  7.71 us
    all_to_all x1, starting transfers between devices, body(): lax.all_to_all(ordered, 'chan', split_axis=0, concat_axis=0, tiled=True)  4.31 us
  transfers between devices with their start and end apart: 12, of which 6 were waited for; matrix products, arithmetic and copies ran while one was open for 1% of the time, Pallas kernels for 14%

profile of v7, /device:TPU:1, one launch (start us, length us, event | category | flops | bytes accessed | tf_op | source)
XLA Modules:
  0.0 127.6 jit_solution(6642371018549428202)
XLA Ops:
  7.2 1.8 %shard_map.115 = bf16[1280,128]{1,0:T(8,128)(2,1)} custom-call(bf16[128,512]{1,0:T(8,128)(2,1)} %w_out_ref.1, bf16[512,512]{1,0:T(8,128)(2,1)} %w_fc1_ref.1, bf16[512,512]{1,0:T(8,128)(2,1)} %w_fc2_ref.1, bf16[512,128]{1,0:T(8,128)(2,1)} %w_pool_ref.1), custom_call_target="tpu_custom_call" | custom-call | tf_op jit(solution)/shard_map/pallas_call | solution.py:354
  9.0 3.9 %shard_map.113 = (bf16[416,128]{1,0:T(8,128)(2,1)}, bf16[416,128]{1,0:T(8,128)(2,1)}, bf16[416,128]{1,0:T(8,128)(2,1)}, bf16[208,128]{1,0:T(8,128)(2,1)}, bf16[208,128]{1,0:T(8,128)(2,1)}) custom-call(bf16[1024,128]{1,0:T(8,128)(2,1)} %feats_ref.1, s32[1,1024]{1,0:T(1,128)} %bitcast.20, s32[1,1024]{1,0:T(1,128)} %bitcast.16), custom_call_target="tpu_custom_call" | custom-call | tf_op jit(solution)/shard_map/pallas_call | solution.py:354
  13.0 6.3 %collective-permute-start = (bf16[208,128]{1,0:T(8,128)(2,1)}, bf16[208,128]{1,0:T(8,128)(2,1)S(1)}, u32[]{:S(2)}, u32[]{:S(2)}) collective-permute-start(bf16[208,128]{1,0:T(8,128)(2,1)} %get-tuple-element.24), channel_id=1, source_target_pairs={{0,500},{4,16},{8,508},{12,24},{16,4},{20,32},{24,12},{28,40},{32,... | collective-permute-start | bytes 159752 | tf_op jit(solution)/shard_map/ppermute | solution.py:58
  19.3 4.7 %collective-permute-start.1 = (bf16[208,128]{1,0:T(8,128)(2,1)}, bf16[208,128]{1,0:T(8,128)(2,1)S(1)}, u32[]{:S(2)}, u32[]{:S(2)}) collective-permute-start(bf16[208,128]{1,0:T(8,128)(2,1)} %get-tuple-element.25), channel_id=1, source_target_pairs={{0,256},{4,260},{8,264},{12,268},{16,272},{20,276},{24,280},{28,28... | collective-permute-start | bytes 159752 | tf_op jit(solution)/shard_map/ppermute | solution.py:58
  23.9 8.2 %collective-permute-start.3 = (bf16[416,128]{1,0:T(8,128)(2,1)}, bf16[416,128]{1,0:T(8,128)(2,1)S(1)}, u32[]{:S(2)}, u32[]{:S(2)}) collective-permute-start(bf16[416,128]{1,0:T(8,128)(2,1)} %get-tuple-element.27), channel_id=1, source_target_pairs={{0,504},{4,508},{8,16},{12,20},{16,8},{20,12},{24,32},{28,36},{32,... | collective-permute-start | bytes 319496 | tf_op jit(solution)/shard_map/ppermute | solution.py:58
  32.1 1.9 %collective-permute-start.2 = (bf16[416,128]{1,0:T(8,128)(2,1)}, bf16[416,128]{1,0:T(8,128)(2,1)S(1)}, u32[]{:S(2)}, u32[]{:S(2)}) collective-permute-start(bf16[416,128]{1,0:T(8,128)(2,1)} %get-tuple-element.26), channel_id=1, source_target_pairs={{0,8},{4,12},{8,0},{12,4},{16,24},{20,28},{24,16},{28,20},{32,40},... | collective-permute-start | bytes 319496 | tf_op jit(solution)/shard_map/ppermute | solution.py:58
  34.4 3.8 %collective-permute-done.2.up_ref = bf16[416,128]{1,0:T(8,128)(2,1)S(1)} collective-permute-done((bf16[416,128]{1,0:T(8,128)(2,1)}, bf16[416,128]{1,0:T(8,128)(2,1)S(1)}, u32[]{:S(2)}, u32[]{:S(2)}) %collective-permute-start.2) | collective-permute-done | bytes 106528 | tf_op jit(solution)/shard_map/ppermute | solution.py:58
  38.2 0.9 pad_maximum_fusion.sent_ref
  39.1 6.4 %collective-permute-start.4 = (bf16[832,128]{1,0:T(8,128)(2,1)S(1)}, bf16[832,128]{1,0:T(8,128)(2,1)S(1)}, u32[]{:S(2)}, u32[]{:S(2)}) collective-permute-start(bf16[832,128]{1,0:T(8,128)(2,1)S(1)} %pad_maximum_fusion.sent_ref), channel_id=1, source_target_pairs={{0,4},{4,0},{8,12},{12,8},{16,20},{20,16},{24,28},{28,24},{32,36},... | collective-permute-start | bytes 638984 | tf_op jit(solution)/shard_map/ppermute | solution.py:58
  45.5 1.1 collective-permute-done.4.swap_ref
  46.6 2.0 %shard_map.114 = (bf16[4096,128]{1,0:T(8,128)(2,1)}, f32[128,128]{1,0:T(8,128)S(1)}) custom-call(bf16[832,128]{1,0:T(8,128)(2,1)S(1)} %pad_maximum_fusion.sent_ref, bf16[416,128]{1,0:T(8,128)(2,1)S(1)} %collective-permute-done.3.down_ref, bf16[416,128]{1,0:T(8,128)(2,1)S(1)} %collective-permute-done.2.up_ref, ...), custom_call_target="tpu_custom_call" | custom-call | tf_op jit(solution)/shard_map/pallas_call | solution.py:354
  48.6 4.3 %all-to-all-start = ((bf16[4,1024,128]{2,1,0:T(8,128)(2,1)}), bf16[4,1024,128]{2,1,0:T(8,128)(2,1)S(1)}, u32[]{:S(2)}, u32[]{:S(2)}) async-start(bf16[4,1024,128]{2,1,0:T(8,128)(2,1)} %bitcast.2), calls=%async_computation | async-start | bytes 2097152 | tf_op jit(solution)/shard_map/all_to_all | solution.py:406
  52.9 2.6 %collective-permute-start.5 = (bf16[5120,128]{1,0:T(8,128)(2,1)S(1)}, bf16[5120,128]{1,0:T(8,128)(2,1)}, u32[]{:S(2)}, u32[]{:S(2)}) collective-permute-start(bf16[5120,128]{1,0:T(8,128)(2,1)S(1)} %copy-done), channel_id=1, source_target_pairs={{0,8},{4,12},{8,0},{12,4},{16,24},{20,28},{24,16},{28,20},{32,40},... | collective-permute-start | bytes 3932168 | tf_op jit(solution)/shard_map/ppermute | solution.py:58
  55.5 11.9 %all-to-all-done = bf16[4,1024,128]{2,1,0:T(8,128)(2,1)S(1)} async-done(((bf16[4,1024,128]{2,1,0:T(8,128)(2,1)}), bf16[4,1024,128]{2,1,0:T(8,128)(2,1)S(1)}, u32[]{:S(2)}, u32[]{:S(2)}) %all-to-all-start) | async-done | bytes 1048608 | tf_op jit(solution)/shard_map/all_to_all | solution.py:406
  67.4 3.6 %collective-permute-start.6 = (bf16[5120,128]{1,0:T(8,128)(2,1)S(1)}, bf16[5120,128]{1,0:T(8,128)(2,1)S(1)}, u32[]{:S(2)}, u32[]{:S(2)}) collective-permute-start(bf16[5120,128]{1,0:T(8,128)(2,1)S(1)} %copy-done), channel_id=1, source_target_pairs={{0,4},{4,0},{8,12},{12,8},{16,20},{20,16},{24,28},{28,24},{32,36},... | collective-permute-start | bytes 3932168 | tf_op jit(solution)/shard_map/ppermute | solution.py:58
  71.1 11.9 %shard_map.116 = bf16[512,256]{1,0:T(8,128)(2,1)S(1)} custom-call(bf16[4096,128]{1,0:T(8,128)(2,1)S(1)} %bitcast.10, f32[1,512]{1,0:T(1,128)S(1)} %bitcast.19, bf16[3,512,128]{2,1,0:T(8,128)(2,1)S(1)} %copy-done.3), custom_call_target="tpu_custom_call" | custom-call | flops 8999999488 | bytes 2000000 | tf_op jit(solution)/shard_map/pallas_call | solution.py:354
  83.0 1.5 %collective-permute-done.5.chip_ref = bf16[5120,128]{1,0:T(8,128)(2,1)} collective-permute-done((bf16[5120,128]{1,0:T(8,128)(2,1)S(1)}, bf16[5120,128]{1,0:T(8,128)(2,1)}, u32[]{:S(2)}, u32[]{:S(2)}) %collective-permute-start.5) | collective-permute-done | bytes 1310752 | tf_op jit(solution)/shard_map/ppermute | solution.py:58
  84.5 3.4 %collective-permute-start.7 = (bf16[5120,128]{1,0:T(8,128)(2,1)}, bf16[5120,128]{1,0:T(8,128)(2,1)S(1)}, u32[]{:S(2)}, u32[]{:S(2)}) collective-permute-start(bf16[5120,128]{1,0:T(8,128)(2,1)} %collective-permute-done.5.chip_ref), channel_id=1, source_target_pairs={{0,4},{4,0},{8,12},{12,8},{16,20},{20,16},{24,28},{28,24},{32,36},... | collective-permute-start | bytes 3932168 | tf_op jit(solution)/shard_map/ppermute | solution.py:58
  88.0 10.5 %all_to_all.34 = bf16[4,128,256]{2,1,0:T(8,128)(2,1)S(1)} all-to-all(bf16[4,128,256]{2,1,0:T(8,128)(2,1)S(1)} %bitcast.15), channel_id=1, replica_groups=mesh['pts'=128,'chan'=4] {'chan'}, dimensions={0} | all-to-all | bytes 524288 | tf_op jit(solution)/shard_map/all_to_all | solution.py:423
  98.5 4.0 %shard_map.117 = (bf16[256,512]{1,0:T(8,128)(2,1)S(1)}, f32[128,512]{1,0:T(8,128)S(1)}, bf16[128,512]{1,0:T(8,128)(2,1)S(1)}, bf16[128,512]{1,0:T(8,128)(2,1)S(1)}) custom-call(bf16[512,256]{1,0:T(8,128)(2,1)S(1)} %bitcast.14, bf16[4096,128]{1,0:T(8,128)(2,1)S(1)} %bitcast.11, f32[1,512]{1,0:T(1,128)S(1)} %bitcast.18, s32[1,1024]{1,0:T(1,128)S(1)} %bitcast.17, ...), custom_call_target="tpu_custom_call" | custom-call | tf_op jit(solution)/shard_map/pallas_call | solution.py:354
  102.5 3.7 %collective-permute-start.8 = (bf16[128,512]{1,0:T(8,128)(2,1)S(1)}, bf16[128,512]{1,0:T(8,128)(2,1)S(1)}, u32[]{:S(2)}, u32[]{:S(2)}) collective-permute-start(bf16[128,512]{1,0:T(8,128)(2,1)S(1)} %get-tuple-element.39), channel_id=1, source_target_pairs={{0,508},{4,8},{8,4},{12,16},{16,12},{20,24},{24,20},{28,32},{32,28... | collective-permute-start | bytes 393224 | tf_op jit(solution)/shard_map/ppermute | solution.py:58
  106.2 4.1 %collective-permute-start.9 = (bf16[128,512]{1,0:T(8,128)(2,1)S(1)}, bf16[128,512]{1,0:T(8,128)(2,1)S(1)}, u32[]{:S(2)}, u32[]{:S(2)}) collective-permute-start(bf16[128,512]{1,0:T(8,128)(2,1)S(1)} %get-tuple-element.40), channel_id=1, source_target_pairs={{0,4},{4,0},{8,12},{12,8},{16,20},{20,16},{24,28},{28,24},{32,36},... | collective-permute-start | bytes 393224 | tf_op jit(solution)/shard_map/ppermute | solution.py:58
  110.3 1.0 collective-permute-done.9.swap_ref
  111.4 8.6 %all_to_all.35 = bf16[4,384,128]{2,1,0:T(8,128)(2,1)S(1)} all-to-all(bf16[4,384,128]{2,1,0:T(8,128)(2,1)S(1)} %bitcast.13), channel_id=1, replica_groups=mesh['pts'=128,'chan'=4] {'chan'}, dimensions={0} | all-to-all | bytes 786432 | tf_op jit(solution)/shard_map/all_to_all | solution.py:438
  (23 shorter events, 1.3 us)
Async XLA Ops:
  7.2 41.4 %all-gather.2.cloned.1.call-start = ((), (), s32[]{:S(2)}) async-start(), calls=%async_computation.3 | async-start | bytes 1638400 | tf_op jit(solution)/shard_map/all_gather | solution.py:377
  13.0 19.1 %collective-permute-start = (bf16[208,128]{1,0:T(8,128)(2,1)}, bf16[208,128]{1,0:T(8,128)(2,1)S(1)}, u32[]{:S(2)}, u32[]{:S(2)}) collective-permute-start(bf16[208,128]{1,0:T(8,128)(2,1)} %get-tuple-element.24), channel_id=1, source_target_pairs={{0,500},{4,16},{8,508},{12,24},{16,4},{20,32},{24,12},{28,40},{32,... | collective-permute-start | bytes 159752 | tf_op jit(solution)/shard_map/ppermute | solution.py:58
  19.3 12.8 %collective-permute-start.1 = (bf16[208,128]{1,0:T(8,128)(2,1)}, bf16[208,128]{1,0:T(8,128)(2,1)S(1)}, u32[]{:S(2)}, u32[]{:S(2)}) collective-permute-start(bf16[208,128]{1,0:T(8,128)(2,1)} %get-tuple-element.25), channel_id=1, source_target_pairs={{0,256},{4,260},{8,264},{12,268},{16,272},{20,276},{24,280},{28,28... | collective-permute-start | bytes 159752 | tf_op jit(solution)/shard_map/ppermute | solution.py:58
  23.9 10.5 %collective-permute-start.3 = (bf16[416,128]{1,0:T(8,128)(2,1)}, bf16[416,128]{1,0:T(8,128)(2,1)S(1)}, u32[]{:S(2)}, u32[]{:S(2)}) collective-permute-start(bf16[416,128]{1,0:T(8,128)(2,1)} %get-tuple-element.27), channel_id=1, source_target_pairs={{0,504},{4,508},{8,16},{12,20},{16,8},{20,12},{24,32},{28,36},{32,... | collective-permute-start | bytes 319496 | tf_op jit(solution)/shard_map/ppermute | solution.py:58
  32.1 6.1 %collective-permute-start.2 = (bf16[416,128]{1,0:T(8,128)(2,1)}, bf16[416,128]{1,0:T(8,128)(2,1)S(1)}, u32[]{:S(2)}, u32[]{:S(2)}) collective-permute-start(bf16[416,128]{1,0:T(8,128)(2,1)} %get-tuple-element.26), channel_id=1, source_target_pairs={{0,8},{4,12},{8,0},{12,4},{16,24},{20,28},{24,16},{28,20},{32,40},... | collective-permute-start | bytes 319496 | tf_op jit(solution)/shard_map/ppermute | solution.py:58
  39.1 31.9 %copy-start.3 = (bf16[3,512,128]{2,1,0:T(8,128)(2,1)S(1)}, bf16[3,512,128]{2,1,0:T(8,128)(2,1)}, u32[]{:S(2)}) copy-start(bf16[3,512,128]{2,1,0:T(8,128)(2,1)} %w_ref.1) | copy-start | bytes 1179652
  39.1 31.9 %copy-start.4 = (f32[512]{0:T(512)S(1)}, f32[512]{0:T(512)}, u32[]{:S(2)}) copy-start(f32[512]{0:T(512)} %param.13) | copy-start | bytes 6148
  39.1 7.4 %collective-permute-start.4 = (bf16[832,128]{1,0:T(8,128)(2,1)S(1)}, bf16[832,128]{1,0:T(8,128)(2,1)S(1)}, u32[]{:S(2)}, u32[]{:S(2)}) collective-permute-start(bf16[832,128]{1,0:T(8,128)(2,1)S(1)} %pad_maximum_fusion.sent_ref), channel_id=1, source_target_pairs={{0,4},{4,0},{8,12},{12,8},{16,20},{20,16},{24,28},{28,24},{32,36},... | collective-permute-start | bytes 638984 | tf_op jit(solution)/shard_map/ppermute | solution.py:58
  48.6 4.3 %copy-start = (bf16[5120,128]{1,0:T(8,128)(2,1)S(1)}, bf16[5120,128]{1,0:T(8,128)(2,1)}, u32[]{:S(2)}) copy-start(bf16[5120,128]{1,0:T(8,128)(2,1)} %all-gather.2.cloned.1.call-done.mine_ref) | copy-start | bytes 3932164
  48.6 18.8 %all-to-all-start = ((bf16[4,1024,128]{2,1,0:T(8,128)(2,1)}), bf16[4,1024,128]{2,1,0:T(8,128)(2,1)S(1)}, u32[]{:S(2)}, u32[]{:S(2)}) async-start(bf16[4,1024,128]{2,1,0:T(8,128)(2,1)} %bitcast.2), calls=%async_computation | async-start | bytes 2097152 | tf_op jit(solution)/shard_map/all_to_all | solution.py:406
  52.9 31.7 %collective-permute-start.5 = (bf16[5120,128]{1,0:T(8,128)(2,1)S(1)}, bf16[5120,128]{1,0:T(8,128)(2,1)}, u32[]{:S(2)}, u32[]{:S(2)}) collective-permute-start(bf16[5120,128]{1,0:T(8,128)(2,1)S(1)} %copy-done), channel_id=1, source_target_pairs={{0,8},{4,12},{8,0},{12,4},{16,24},{20,28},{24,16},{28,20},{32,40},... | collective-permute-start | bytes 3932168 | tf_op jit(solution)/shard_map/ppermute | solution.py:58
  67.4 31.1 %collective-permute-start.6 = (bf16[5120,128]{1,0:T(8,128)(2,1)S(1)}, bf16[5120,128]{1,0:T(8,128)(2,1)S(1)}, u32[]{:S(2)}, u32[]{:S(2)}) collective-permute-start(bf16[5120,128]{1,0:T(8,128)(2,1)S(1)} %copy-done), channel_id=1, source_target_pairs={{0,4},{4,0},{8,12},{12,8},{16,20},{20,16},{24,28},{28,24},{32,36},... | collective-permute-start | bytes 3932168 | tf_op jit(solution)/shard_map/ppermute | solution.py:58
  71.0 27.5 %copy-start.1 = (s32[1024]{0:T(1024)S(1)}, s32[1024]{0:T(1024)}, u32[]{:S(2)}) copy-start(s32[1024]{0:T(1024)} %param.12) | copy-start | bytes 12292
  71.1 27.5 %copy-start.2 = (f32[512]{0:T(512)S(1)}, f32[512]{0:T(512)}, u32[]{:S(2)}) copy-start(f32[512]{0:T(512)} %param.16) | copy-start | bytes 6148
  84.5 14.0 %collective-permute-start.7 = (bf16[5120,128]{1,0:T(8,128)(2,1)}, bf16[5120,128]{1,0:T(8,128)(2,1)S(1)}, u32[]{:S(2)}, u32[]{:S(2)}) collective-permute-start(bf16[5120,128]{1,0:T(8,128)(2,1)} %collective-permute-done.5.chip_ref), channel_id=1, source_target_pairs={{0,4},{4,0},{8,12},{12,8},{16,20},{20,16},{24,28},{28,24},{32,36},... | collective-permute-start | bytes 3932168 | tf_op jit(solution)/shard_map/ppermute | solution.py:58
  102.5 7.8 %collective-permute-start.8 = (bf16[128,512]{1,0:T(8,128)(2,1)S(1)}, bf16[128,512]{1,0:T(8,128)(2,1)S(1)}, u32[]{:S(2)}, u32[]{:S(2)}) collective-permute-start(bf16[128,512]{1,0:T(8,128)(2,1)S(1)} %get-tuple-element.39), channel_id=1, source_target_pairs={{0,508},{4,8},{8,4},{12,16},{16,12},{20,24},{24,20},{28,32},{32,28... | collective-permute-start | bytes 393224 | tf_op jit(solution)/shard_map/ppermute | solution.py:58
  106.2 5.1 %collective-permute-start.9 = (bf16[128,512]{1,0:T(8,128)(2,1)S(1)}, bf16[128,512]{1,0:T(8,128)(2,1)S(1)}, u32[]{:S(2)}, u32[]{:S(2)}) collective-permute-start(bf16[128,512]{1,0:T(8,128)(2,1)S(1)} %get-tuple-element.40), channel_id=1, source_target_pairs={{0,4},{4,0},{8,12},{12,8},{16,20},{20,16},{24,28},{28,24},{32,36},... | collective-permute-start | bytes 393224 | tf_op jit(solution)/shard_map/ppermute | solution.py:58
Sparse Core Ops, SparseCore 0:
  10.1 36.7 all-gather.1

commit v8 on v6

--- a/solution.py
+++ b/solution.py
@@ -135,8 +135,13 @@
     small = lax.broadcasted_iota(jnp.int32, (16, 128), 0)
     lane = lax.broadcasted_iota(jnp.int32, (1, 128), 1)
     chosen = one_hot(slot, SLOTS)
-    packed = matmul(chosen, feats).astype(BF16)
-    places = matmul_nt(digits_of(dest), chosen)
+    eye_row = lax.broadcasted_iota(jnp.int32, (16, LANES), 0)
+    eye_col = lax.broadcasted_iota(jnp.int32, (16, LANES), 1)
+    eye = jnp.where(eye_row == eye_col, 1.0, 0.0).astype(BF16)
+    columns = matmul_tn(digits_of(dest), eye).astype(BF16)
+    picked = matmul(chosen, jnp.concatenate([feats, columns], axis=1)).astype(BF16)
+    packed = picked[:, :LANES]
+    places = matmul_nt(eye, picked[:, LANES:])
     for m, (ref, base, offset) in enumerate(blocks):
         ref[base : base + 128, :] = packed[m * 128 : (m + 1) * 128, :]
         ref[base + 128 : base + CAP, :] = packed[1024 + m * 64 : 1024 + (m + 1) * 64, :]
@@ -242,9 +247,10 @@
         for c, part in enumerate(normed_chunks(chunks, gains)):
             normed[rows, c * 128 : (c + 1) * 128] = part
     everything = normed[...]
-    q_ref[...] = (matmul(everything, w_ref[0]).astype(BF16).astype(F32) * 0.25).astype(BF16)
-    k_ref[...] = matmul(everything, w_ref[1]).astype(BF16)
-    v_ref[...] = matmul(everything, w_ref[2]).T.astype(BF16)
+    qkv = matmul(everything, jnp.concatenate([w_ref[t] for t in range(3)], axis=1))
+    q_ref[...] = (qkv[:, :LANES].astype(BF16).astype(F32) * 0.25).astype(BF16)
+    k_ref[...] = qkv[:, LANES : 2 * LANES].astype(BF16)
+    v_ref[...] = qkv[:, 2 * LANES :].T.astype(BF16)
     head_of = lax.broadcasted_iota(jnp.int32, (STEP, LANES), 1) // HEAD_DIM
     work = [(h, part) for h in range(HEADS_HERE) for part in range(ROWS // STEP)]
 
@@ -363,15 +369,6 @@
     def block(count=1):
         return ((count * BLOCK, LANES), BF16)
 
-    (weights,) = call(
-        weights_kernel,
-        [((WROWS, LANES), BF16)],
-        (w_out, w_fc1, w_fc2, w_pool),
-        scratch=[pltpu.SemaphoreType.DMA((11,))],
-        limit=ALL_VMEM,
-        in_hbm=range(4),
-    )
-    weights = lax.all_gather(weights, "chan", axis=0, tiled=True)
     up, down, swap, far, over = call(
         pack_kernel,
         [block(2), block(2), block(2), block(), block()],
@@ -390,6 +387,17 @@
     down = exchange(down, chip_down)
     up, far, over = lax.optimization_barrier((up, far, over))
     up = exchange(up, chip_up)
+    w_fc1, far = lax.optimization_barrier((w_fc1, far))
+    (weights,) = call(
+        weights_kernel,
+        [((WROWS, LANES), BF16)],
+        (w_out, w_fc1, w_fc2, w_pool),
+        scratch=[pltpu.SemaphoreType.DMA((11,))],
+        limit=ALL_VMEM,
+        in_hbm=range(4),
+        cost=pl.CostEstimate(flops=0, bytes_accessed=6_000_000, transcendentals=0),
+    )
+    weights = lax.all_gather(weights, "chan", axis=0, tiled=True)
     sent = jnp.concatenate([swap, up[BLOCK:], down[BLOCK:]], axis=0)
     swap = exchange(sent, core_swap)
     ordered, count = call(
@@ -399,8 +407,6 @@
         scratch=[pltpu.VMEM((SLOTS, LANES), BF16)],
     )
     full = lax.all_to_all(ordered, "chan", split_axis=0, concat_axis=0, tiled=True)
-    full, weights = lax.optimization_barrier((full, weights))
-    others = exchange(weights, core_swap)
     (attn,) = call(
         attention_kernel,
         [((N_CHAN * LANES, QUARTER), BF16)],
@@ -413,6 +419,8 @@
             pltpu.VMEM((LANES, ROWS), BF16),
         ],
     )
+    attn, weights = lax.optimization_barrier((attn, weights))
+    others = exchange(weights, core_swap)
     attn = lax.all_to_all(attn, "chan", split_axis=0, concat_axis=0, tiled=True)
     cell_sum = ((CELLS, C), BF16)
     rows, mine, for_swap, for_next = call(

time: 125 us -> 135 us (1.080)
  blocking collectives: 40.3 us -> 47.8 us
  local copies, waits for them, and re-layouts: 0.04 us -> 1.77 us
    all_to_all x1, blocking collectives: 21.2 us -> 30.2 us  [body(): lax.all_to_all(ordered, 'chan', split_axis=0, concat_axis=0, tiled=True)]
    unnamed x10 -> x16, local copies, waits for them, and re-layouts: 0.03 us -> 1.77 us
    all_to_all x1, blocking collectives: 10.2 us -> 8.63 us  [body(): lax.all_to_all(message, 'chan', split_axis=0, concat_axis=0, tiled=True)]
  transfers between devices with their start and end apart: 9 -> 9, of which waited for: 4 -> 5; matrix products, arithmetic and copies ran while one was open for 1% -> 0% of each run, Pallas kernels for 14% -> 10%
where the time goes in v8:
time: 135 us; the launch traced here: 134 us
  blocking collectives  47.8 us (35%)
  starting transfers between devices  40.9 us (30%)
  Pallas kernels  21.9 us (16%)
  between operations  14.2 us (11%)
  waiting for transfers between devices  7.49 us (6%)
  local copies, waits for them, and re-layouts  1.77 us (1%)
    ppermute x8, starting transfers between devices, exchange(): return lax.ppermute(x, 'pts', [(i, partner(i)) for i in range(N_PTS)])  40.9 us
    all_to_all x1, blocking collectives, body(): lax.all_to_all(ordered, 'chan', split_axis=0, concat_axis=0, tiled=True)  30.2 us
    pallas_call x7, Pallas kernels, call(): pl.pallas_call(kernel, out_shape=[jax.ShapeDtypeStruct(shape, dtype) for...  21.9 us
    all_to_all x1, blocking collectives, body(): attn = lax.all_to_all(attn, 'chan', split_axis=0, concat_axis=0, tiled=True)  8.92 us
    all_to_all x1, blocking collectives, body(): lax.all_to_all(message, 'chan', split_axis=0, concat_axis=0, tiled=True)  8.63 us
    ppermute x8, waiting for transfers between devices, exchange(): return lax.ppermute(x, 'pts', [(i, partner(i)) for i in range(N_PTS)])  7.47 us
  transfers between devices with their start and end apart: 9, of which 5 were waited for; matrix products, arithmetic and copies ran while one was open for 0% of the time, Pallas kernels for 10%

profile of v8, /device:TPU:1, one launch (start us, length us, event | category | flops | bytes accessed | tf_op | source)
XLA Modules:
  0.0 134.1 jit_solution(2386534380220101095)
XLA Ops:
  7.2 3.6 %shard_map.113 = (bf16[416,128]{1,0:T(8,128)(2,1)}, bf16[416,128]{1,0:T(8,128)(2,1)}, bf16[416,128]{1,0:T(8,128)(2,1)}, bf16[208,128]{1,0:T(8,128)(2,1)}, bf16[208,128]{1,0:T(8,128)(2,1)}) custom-call(bf16[1024,128]{1,0:T(8,128)(2,1)} %feats_ref.1, s32[1,1024]{1,0:T(1,128)} %bitcast.21, s32[1,1024]{1,0:T(1,128)} %bitcast.17), custom_call_target="tpu_custom_call" | custom-call | tf_op jit(solution)/shard_map/pallas_call | solution.py:357
  10.8 6.4 %collective-permute-start = (bf16[208,128]{1,0:T(8,128)(2,1)}, bf16[208,128]{1,0:T(8,128)(2,1)S(1)}, u32[]{:S(2)}, u32[]{:S(2)}) collective-permute-start(bf16[208,128]{1,0:T(8,128)(2,1)} %get-tuple-element.22), channel_id=1, source_target_pairs={{0,500},{4,16},{8,508},{12,24},{16,4},{20,32},{24,12},{28,40},{32,... | collective-permute-start | bytes 159752 | tf_op jit(solution)/shard_map/ppermute | solution.py:58
  17.3 4.7 %collective-permute-start.1 = (bf16[208,128]{1,0:T(8,128)(2,1)}, bf16[208,128]{1,0:T(8,128)(2,1)S(1)}, u32[]{:S(2)}, u32[]{:S(2)}) collective-permute-start(bf16[208,128]{1,0:T(8,128)(2,1)} %get-tuple-element.23), channel_id=1, source_target_pairs={{0,256},{4,260},{8,264},{12,268},{16,272},{20,276},{24,280},{28,28... | collective-permute-start | bytes 159752 | tf_op jit(solution)/shard_map/ppermute | solution.py:58
  21.9 1.9 %collective-permute-done.1.across_ref = bf16[208,128]{1,0:T(8,128)(2,1)S(1)} collective-permute-done((bf16[208,128]{1,0:T(8,128)(2,1)}, bf16[208,128]{1,0:T(8,128)(2,1)S(1)}, u32[]{:S(2)}, u32[]{:S(2)}) %collective-permute-start.1) | collective-permute-done | bytes 53280 | tf_op jit(solution)/shard_map/ppermute | solution.py:58
  23.9 2.1 %shard_map.116 = bf16[2560,128]{1,0:T(8,128)(2,1)} custom-call(bf16[128,512]{1,0:T(8,128)(2,1)} %w_out_ref.1, bf16[512,512]{1,0:T(8,128)(2,1)} %w_fc1_ref, bf16[512,512]{1,0:T(8,128)(2,1)} %w_fc2_ref.1, bf16[512,128]{1,0:T(8,128)(2,1)} %w_pool_ref.1), custom_call_target="tpu_custom_call" | custom-call | bytes 6000000 | tf_op jit(solution)/shard_map/pallas_call | solution.py:357
  26.0 11.4 %collective-permute-start.3 = (bf16[416,128]{1,0:T(8,128)(2,1)S(1)}, bf16[416,128]{1,0:T(8,128)(2,1)S(1)}, u32[]{:S(2)}, u32[]{:S(2)}) collective-permute-start(bf16[416,128]{1,0:T(8,128)(2,1)S(1)} %copy-done.7), channel_id=1, source_target_pairs={{0,504},{4,508},{8,16},{12,20},{16,8},{20,12},{24,32},{28,36},{32,... | collective-permute-start | bytes 319496 | tf_op jit(solution)/shard_map/ppermute | solution.py:58
  37.4 1.9 %collective-permute-start.2 = (bf16[416,128]{1,0:T(8,128)(2,1)S(1)}, bf16[416,128]{1,0:T(8,128)(2,1)S(1)}, u32[]{:S(2)}, u32[]{:S(2)}) collective-permute-start(bf16[416,128]{1,0:T(8,128)(2,1)S(1)} %copy-done.6), channel_id=1, source_target_pairs={{0,8},{4,12},{8,0},{12,4},{16,24},{20,28},{24,16},{28,20},{32,40},... | collective-permute-start | bytes 319496 | tf_op jit(solution)/shard_map/ppermute | solution.py:58
  39.3 0.1 collective-permute-done.3.down_ref
  39.5 3.4 %collective-permute-done.2.up_ref = bf16[416,128]{1,0:T(8,128)(2,1)S(1)} collective-permute-done((bf16[416,128]{1,0:T(8,128)(2,1)S(1)}, bf16[416,128]{1,0:T(8,128)(2,1)S(1)}, u32[]{:S(2)}, u32[]{:S(2)}) %collective-permute-start.2) | collective-permute-done | bytes 106528 | tf_op jit(solution)/shard_map/ppermute | solution.py:58
  42.9 5.0 %collective-permute-start.4 = (bf16[832,128]{1,0:T(8,128)(2,1)S(1)}, bf16[832,128]{1,0:T(8,128)(2,1)S(1)}, u32[]{:S(2)}, u32[]{:S(2)}) collective-permute-start(bf16[832,128]{1,0:T(8,128)(2,1)S(1)} %pad_maximum_fusion.sent_ref), channel_id=1, source_target_pairs={{0,4},{4,0},{8,12},{12,8},{16,20},{20,16},{24,28},{28,24},{32,36},... | collective-permute-start | bytes 638984 | tf_op jit(solution)/shard_map/ppermute | solution.py:58
  47.9 1.1 collective-permute-done.4.swap_ref
  48.9 1.0 shard_map.114
  50.0 30.2 %all_to_all.33 = bf16[4,1024,128]{2,1,0:T(8,128)(2,1)S(1)} all-to-all(bf16[4,1024,128]{2,1,0:T(8,128)(2,1)S(1)} %bitcast.14), channel_id=1, replica_groups=mesh['pts'=128,'chan'=4] {'chan'}, dimensions={0} | all-to-all | bytes 2097152 | tf_op jit(solution)/shard_map/all_to_all | solution.py:409
  80.2 11.8 %shard_map.115 = bf16[512,256]{1,0:T(8,128)(2,1)S(1)} custom-call(bf16[4096,128]{1,0:T(8,128)(2,1)S(1)} %bitcast.10, f32[1,512]{1,0:T(1,128)S(1)} %bitcast.20, bf16[3,512,128]{2,1,0:T(8,128)(2,1)S(1)} %copy-done.3), custom_call_target="tpu_custom_call" | custom-call | flops 8999999488 | bytes 2000000 | tf_op jit(solution)/shard_map/pallas_call | solution.py:357
  92.1 3.7 %collective-permute-start.5 = (bf16[10240,128]{1,0:T(8,128)(2,1)}, bf16[10240,128]{1,0:T(8,128)(2,1)S(1)}, u32[]{:S(2)}, u32[]{:S(2)}) collective-permute-start(bf16[10240,128]{1,0:T(8,128)(2,1)} %all-gather.2.cloned.1.call-done.mine_ref), channel_id=1, source_target_pairs={{0,4},{4,0},{8,12},{12,8},{16,20},{20,16},{24,28},{28,24},{32,36},... | collective-permute-start | bytes 7864328 | tf_op jit(solution)/shard_map/ppermute | solution.py:58
  95.7 8.9 %all_to_all.34 = bf16[4,128,256]{2,1,0:T(8,128)(2,1)S(1)} all-to-all(bf16[4,128,256]{2,1,0:T(8,128)(2,1)S(1)} %bitcast.16), channel_id=1, replica_groups=mesh['pts'=128,'chan'=4] {'chan'}, dimensions={0} | all-to-all | bytes 524288 | tf_op jit(solution)/shard_map/all_to_all | solution.py:424
  104.7 1.7 %copy-done = bf16[10240,128]{1,0:T(8,128)(2,1)S(1)} copy-done((bf16[10240,128]{1,0:T(8,128)(2,1)S(1)}, bf16[10240,128]{1,0:T(8,128)(2,1)}, u32[]{:S(2)}) %copy-start) | copy-done | bytes 2621464
  106.4 2.6 %shard_map.117 = (bf16[256,512]{1,0:T(8,128)(2,1)S(1)}, f32[128,512]{1,0:T(8,128)S(1)}, bf16[128,512]{1,0:T(8,128)(2,1)S(1)}, bf16[128,512]{1,0:T(8,128)(2,1)S(1)}) custom-call(bf16[512,256]{1,0:T(8,128)(2,1)S(1)} %bitcast.15, bf16[4096,128]{1,0:T(8,128)(2,1)S(1)} %bitcast.11, f32[1,512]{1,0:T(1,128)S(1)} %bitcast.19, s32[1,1024]{1,0:T(1,128)S(1)} %bitcast.18, ...), custom_call_target="tpu_custom_call" | custom-call | tf_op jit(solution)/shard_map/pallas_call | solution.py:357
  109.0 2.2 %collective-permute-start.6 = (bf16[128,512]{1,0:T(8,128)(2,1)S(1)}, bf16[128,512]{1,0:T(8,128)(2,1)S(1)}, u32[]{:S(2)}, u32[]{:S(2)}) collective-permute-start(bf16[128,512]{1,0:T(8,128)(2,1)S(1)} %get-tuple-element.35), channel_id=1, source_target_pairs={{0,508},{4,8},{8,4},{12,16},{16,12},{20,24},{24,20},{28,32},{32,28... | collective-permute-start | bytes 393224 | tf_op jit(solution)/shard_map/ppermute | solution.py:58
  111.2 5.7 %collective-permute-start.7 = (bf16[128,512]{1,0:T(8,128)(2,1)S(1)}, bf16[128,512]{1,0:T(8,128)(2,1)S(1)}, u32[]{:S(2)}, u32[]{:S(2)}) collective-permute-start(bf16[128,512]{1,0:T(8,128)(2,1)S(1)} %get-tuple-element.36), channel_id=1, source_target_pairs={{0,4},{4,0},{8,12},{12,8},{16,20},{20,16},{24,28},{28,24},{32,36},... | collective-permute-start | bytes 393224 | tf_op jit(solution)/shard_map/ppermute | solution.py:58
  116.9 1.0 collective-permute-done.7.swap_ref
  117.8 0.1 shard_map.118
  117.9 8.6 %all_to_all.35 = bf16[4,384,128]{2,1,0:T(8,128)(2,1)S(1)} all-to-all(bf16[4,384,128]{2,1,0:T(8,128)(2,1)S(1)} %bitcast.13), channel_id=1, replica_groups=mesh['pts'=128,'chan'=4] {'chan'}, dimensions={0} | all-to-all | bytes 786432 | tf_op jit(solution)/shard_map/all_to_all | solution.py:439
  126.6 0.7 shard_map.119
  (24 shorter events, 0.1 us)
Async XLA Ops:
  7.2 84.9 %all-gather.2.cloned.1.call-start = ((), (), s32[]{:S(2)}) async-start(), calls=%async_computation.3 | async-start | bytes 3276800 | tf_op jit(solution)/shard_map/all_gather | solution.py:400
  10.8 15.2 %copy-start.7 = (bf16[416,128]{1,0:T(8,128)(2,1)S(1)}, bf16[416,128]{1,0:T(8,128)(2,1)}, u32[]{:S(2)}) copy-start(bf16[416,128]{1,0:T(8,128)(2,1)} %get-tuple-element.25) | copy-start | bytes 319492
  10.8 26.6 %copy-start.6 = (bf16[416,128]{1,0:T(8,128)(2,1)S(1)}, bf16[416,128]{1,0:T(8,128)(2,1)}, u32[]{:S(2)}) copy-start(bf16[416,128]{1,0:T(8,128)(2,1)} %get-tuple-element.24) | copy-start | bytes 319492
  10.8 32.1 %copy-start.5 = (bf16[416,128]{1,0:T(8,128)(2,1)S(1)}, bf16[416,128]{1,0:T(8,128)(2,1)}, u32[]{:S(2)}) copy-start(bf16[416,128]{1,0:T(8,128)(2,1)} %get-tuple-element.20) | copy-start | bytes 319492
  10.8 11.1 %collective-permute-start = (bf16[208,128]{1,0:T(8,128)(2,1)}, bf16[208,128]{1,0:T(8,128)(2,1)S(1)}, u32[]{:S(2)}, u32[]{:S(2)}) collective-permute-start(bf16[208,128]{1,0:T(8,128)(2,1)} %get-tuple-element.22), channel_id=1, source_target_pairs={{0,500},{4,16},{8,508},{12,24},{16,4},{20,32},{24,12},{28,40},{32,... | collective-permute-start | bytes 159752 | tf_op jit(solution)/shard_map/ppermute | solution.py:58
  17.3 6.6 %collective-permute-start.1 = (bf16[208,128]{1,0:T(8,128)(2,1)}, bf16[208,128]{1,0:T(8,128)(2,1)S(1)}, u32[]{:S(2)}, u32[]{:S(2)}) collective-permute-start(bf16[208,128]{1,0:T(8,128)(2,1)} %get-tuple-element.23), channel_id=1, source_target_pairs={{0,256},{4,260},{8,264},{12,268},{16,272},{20,276},{24,280},{28,28... | collective-permute-start | bytes 159752 | tf_op jit(solution)/shard_map/ppermute | solution.py:58
  23.9 56.4 %copy-start.4 = (f32[512]{0:T(512)S(1)}, f32[512]{0:T(512)}, u32[]{:S(2)}) copy-start(f32[512]{0:T(512)} %param.13) | copy-start | bytes 6148
  26.0 54.3 %copy-start.3 = (bf16[3,512,128]{2,1,0:T(8,128)(2,1)S(1)}, bf16[3,512,128]{2,1,0:T(8,128)(2,1)}, u32[]{:S(2)}) copy-start(bf16[3,512,128]{2,1,0:T(8,128)(2,1)} %w_ref.1) | copy-start | bytes 1179652
  26.0 13.5 %collective-permute-start.3 = (bf16[416,128]{1,0:T(8,128)(2,1)S(1)}, bf16[416,128]{1,0:T(8,128)(2,1)S(1)}, u32[]{:S(2)}, u32[]{:S(2)}) collective-permute-start(bf16[416,128]{1,0:T(8,128)(2,1)S(1)} %copy-done.7), channel_id=1, source_target_pairs={{0,504},{4,508},{8,16},{12,20},{16,8},{20,12},{24,32},{28,36},{32,... | collective-permute-start | bytes 319496 | tf_op jit(solution)/shard_map/ppermute | solution.py:58
  37.4 5.4 %collective-permute-start.2 = (bf16[416,128]{1,0:T(8,128)(2,1)S(1)}, bf16[416,128]{1,0:T(8,128)(2,1)S(1)}, u32[]{:S(2)}, u32[]{:S(2)}) collective-permute-start(bf16[416,128]{1,0:T(8,128)(2,1)S(1)} %copy-done.6), channel_id=1, source_target_pairs={{0,8},{4,12},{8,0},{12,4},{16,24},{20,28},{24,16},{28,20},{32,40},... | collective-permute-start | bytes 319496 | tf_op jit(solution)/shard_map/ppermute | solution.py:58
  42.9 6.0 %collective-permute-start.4 = (bf16[832,128]{1,0:T(8,128)(2,1)S(1)}, bf16[832,128]{1,0:T(8,128)(2,1)S(1)}, u32[]{:S(2)}, u32[]{:S(2)}) collective-permute-start(bf16[832,128]{1,0:T(8,128)(2,1)S(1)} %pad_maximum_fusion.sent_ref), channel_id=1, source_target_pairs={{0,4},{4,0},{8,12},{12,8},{16,20},{20,16},{24,28},{28,24},{32,36},... | collective-permute-start | bytes 638984 | tf_op jit(solution)/shard_map/ppermute | solution.py:58
  80.2 24.4 %copy-start.1 = (s32[1024]{0:T(1024)S(1)}, s32[1024]{0:T(1024)}, u32[]{:S(2)}) copy-start(s32[1024]{0:T(1024)} %param.12) | copy-start | bytes 12292
  80.2 24.4 %copy-start.2 = (f32[512]{0:T(512)S(1)}, f32[512]{0:T(512)}, u32[]{:S(2)}) copy-start(f32[512]{0:T(512)} %param.16) | copy-start | bytes 6148
  92.1 12.6 %collective-permute-start.5 = (bf16[10240,128]{1,0:T(8,128)(2,1)}, bf16[10240,128]{1,0:T(8,128)(2,1)S(1)}, u32[]{:S(2)}, u32[]{:S(2)}) collective-permute-start(bf16[10240,128]{1,0:T(8,128)(2,1)} %all-gather.2.cloned.1.call-done.mine_ref), channel_id=1, source_target_pairs={{0,4},{4,0},{8,12},{12,8},{16,20},{20,16},{24,28},{28,24},{32,36},... | collective-permute-start | bytes 7864328 | tf_op jit(solution)/shard_map/ppermute | solution.py:58
  104.7 1.7 %copy-start = (bf16[10240,128]{1,0:T(8,128)(2,1)S(1)}, bf16[10240,128]{1,0:T(8,128)(2,1)}, u32[]{:S(2)}) copy-start(bf16[10240,128]{1,0:T(8,128)(2,1)} %all-gather.2.cloned.1.call-done.mine_ref) | copy-start | bytes 7864324
  109.0 7.9 %collective-permute-start.6 = (bf16[128,512]{1,0:T(8,128)(2,1)S(1)}, bf16[128,512]{1,0:T(8,128)(2,1)S(1)}, u32[]{:S(2)}, u32[]{:S(2)}) collective-permute-start(bf16[128,512]{1,0:T(8,128)(2,1)S(1)} %get-tuple-element.35), channel_id=1, source_target_pairs={{0,508},{4,8},{8,4},{12,16},{16,12},{20,24},{24,20},{28,32},{32,28... | collective-permute-start | bytes 393224 | tf_op jit(solution)/shard_map/ppermute | solution.py:58
  111.2 6.6 %collective-permute-start.7 = (bf16[128,512]{1,0:T(8,128)(2,1)S(1)}, bf16[128,512]{1,0:T(8,128)(2,1)S(1)}, u32[]{:S(2)}, u32[]{:S(2)}) collective-permute-start(bf16[128,512]{1,0:T(8,128)(2,1)S(1)} %get-tuple-element.36), channel_id=1, source_target_pairs={{0,4},{4,0},{8,12},{12,8},{16,20},{20,16},{24,28},{28,24},{32,36},... | collective-permute-start | bytes 393224 | tf_op jit(solution)/shard_map/ppermute | solution.py:58
Sparse Core Ops, SparseCore 0:
  26.1 56.4 all-gather.1

commit v9 on v6

--- a/solution.py
+++ b/solution.py
@@ -135,8 +135,13 @@
     small = lax.broadcasted_iota(jnp.int32, (16, 128), 0)
     lane = lax.broadcasted_iota(jnp.int32, (1, 128), 1)
     chosen = one_hot(slot, SLOTS)
-    packed = matmul(chosen, feats).astype(BF16)
-    places = matmul_nt(digits_of(dest), chosen)
+    eye_row = lax.broadcasted_iota(jnp.int32, (16, LANES), 0)
+    eye_col = lax.broadcasted_iota(jnp.int32, (16, LANES), 1)
+    eye = jnp.where(eye_row == eye_col, 1.0, 0.0).astype(BF16)
+    columns = matmul_tn(digits_of(dest), eye).astype(BF16)
+    picked = matmul(chosen, jnp.concatenate([feats, columns], axis=1)).astype(BF16)
+    packed = picked[:, :LANES]
+    places = matmul_nt(eye, picked[:, LANES:])
     for m, (ref, base, offset) in enumerate(blocks):
         ref[base : base + 128, :] = packed[m * 128 : (m + 1) * 128, :]
         ref[base + 128 : base + CAP, :] = packed[1024 + m * 64 : 1024 + (m + 1) * 64, :]
@@ -242,9 +247,10 @@
         for c, part in enumerate(normed_chunks(chunks, gains)):
             normed[rows, c * 128 : (c + 1) * 128] = part
     everything = normed[...]
-    q_ref[...] = (matmul(everything, w_ref[0]).astype(BF16).astype(F32) * 0.25).astype(BF16)
-    k_ref[...] = matmul(everything, w_ref[1]).astype(BF16)
-    v_ref[...] = matmul(everything, w_ref[2]).T.astype(BF16)
+    qkv = matmul(everything, jnp.concatenate([w_ref[t] for t in range(3)], axis=1))
+    q_ref[...] = (qkv[:, :LANES].astype(BF16).astype(F32) * 0.25).astype(BF16)
+    k_ref[...] = qkv[:, LANES : 2 * LANES].astype(BF16)
+    v_ref[...] = qkv[:, 2 * LANES :].T.astype(BF16)
     head_of = lax.broadcasted_iota(jnp.int32, (STEP, LANES), 1) // HEAD_DIM
     work = [(h, part) for h in range(HEADS_HERE) for part in range(ROWS // STEP)]
 

time: 125 us -> 125 us (level)
  transfers between devices with their start and end apart: 9 -> 9, of which waited for: 4 -> 4; matrix products, arithmetic and copies ran while one was open for 1% -> 1% of each run, Pallas kernels for 14% -> 13%
where the time goes in v9:
time: 125 us
  blocking collectives  40.7 us (33%)
  starting transfers between devices  40.6 us (32%)
  Pallas kernels  22 us (18%)
  between operations  14.2 us (11%)
  waiting for transfers between devices  6.18 us (5%)
    ppermute x8, starting transfers between devices, exchange(): return lax.ppermute(x, 'pts', [(i, partner(i)) for i in range(N_PTS)])  40.5 us
    pallas_call x7, Pallas kernels, call(): pl.pallas_call(kernel, out_shape=[jax.ShapeDtypeStruct(shape, dtype) for...  22 us
    all_to_all x1, blocking collectives, body(): lax.all_to_all(ordered, 'chan', split_axis=0, concat_axis=0, tiled=True)  21.6 us
    all_to_all x1, blocking collectives, body(): lax.all_to_all(message, 'chan', split_axis=0, concat_axis=0, tiled=True)  10.2 us
    all_to_all x1, blocking collectives, body(): attn = lax.all_to_all(attn, 'chan', split_axis=0, concat_axis=0, tiled=True)  8.86 us
    ppermute x8, waiting for transfers between devices, exchange(): return lax.ppermute(x, 'pts', [(i, partner(i)) for i in range(N_PTS)])  6.16 us
  transfers between devices with their start and end apart: 9, of which 4 were waited for; matrix products, arithmetic and copies ran while one was open for 1% of the time, Pallas kernels for 13%

profile of v9, /device:TPU:1, one launch (start us, length us, event | category | flops | bytes accessed | tf_op | source)
XLA Modules:
  0.0 124.6 jit_solution(2453128831419940014)
XLA Ops:
  7.2 0.0 all-gather.2.cloned.1.call-start
  7.2 2.1 %shard_map.115 = bf16[2560,128]{1,0:T(8,128)(2,1)} custom-call(bf16[128,512]{1,0:T(8,128)(2,1)} %w_out_ref.1, bf16[512,512]{1,0:T(8,128)(2,1)} %w_fc1_ref.1, bf16[512,512]{1,0:T(8,128)(2,1)} %w_fc2_ref.1, bf16[512,128]{1,0:T(8,128)(2,1)} %w_pool_ref.1), custom_call_target="tpu_custom_call" | custom-call | tf_op jit(solution)/shard_map/pallas_call | solution.py:357
  9.4 3.6 %shard_map.113 = (bf16[416,128]{1,0:T(8,128)(2,1)}, bf16[416,128]{1,0:T(8,128)(2,1)}, bf16[416,128]{1,0:T(8,128)(2,1)}, bf16[208,128]{1,0:T(8,128)(2,1)}, bf16[208,128]{1,0:T(8,128)(2,1)}) custom-call(bf16[1024,128]{1,0:T(8,128)(2,1)} %feats_ref.1, s32[1,1024]{1,0:T(1,128)} %bitcast.21, s32[1,1024]{1,0:T(1,128)} %bitcast.17), custom_call_target="tpu_custom_call" | custom-call | tf_op jit(solution)/shard_map/pallas_call | solution.py:357
  13.0 6.3 %collective-permute-start = (bf16[208,128]{1,0:T(8,128)(2,1)}, bf16[208,128]{1,0:T(8,128)(2,1)S(1)}, u32[]{:S(2)}, u32[]{:S(2)}) collective-permute-start(bf16[208,128]{1,0:T(8,128)(2,1)} %get-tuple-element.20), channel_id=1, source_target_pairs={{0,500},{4,16},{8,508},{12,24},{16,4},{20,32},{24,12},{28,40},{32,... | collective-permute-start | bytes 159752 | tf_op jit(solution)/shard_map/ppermute | solution.py:58
  19.3 4.7 %collective-permute-start.1 = (bf16[208,128]{1,0:T(8,128)(2,1)}, bf16[208,128]{1,0:T(8,128)(2,1)S(1)}, u32[]{:S(2)}, u32[]{:S(2)}) collective-permute-start(bf16[208,128]{1,0:T(8,128)(2,1)} %get-tuple-element.21), channel_id=1, source_target_pairs={{0,256},{4,260},{8,264},{12,268},{16,272},{20,276},{24,280},{28,28... | collective-permute-start | bytes 159752 | tf_op jit(solution)/shard_map/ppermute | solution.py:58
  24.0 8.2 %collective-permute-start.3 = (bf16[416,128]{1,0:T(8,128)(2,1)}, bf16[416,128]{1,0:T(8,128)(2,1)S(1)}, u32[]{:S(2)}, u32[]{:S(2)}) collective-permute-start(bf16[416,128]{1,0:T(8,128)(2,1)} %get-tuple-element.23), channel_id=1, source_target_pairs={{0,504},{4,508},{8,16},{12,20},{16,8},{20,12},{24,32},{28,36},{32,... | collective-permute-start | bytes 319496 | tf_op jit(solution)/shard_map/ppermute | solution.py:58
  32.2 1.9 %collective-permute-start.2 = (bf16[416,128]{1,0:T(8,128)(2,1)}, bf16[416,128]{1,0:T(8,128)(2,1)S(1)}, u32[]{:S(2)}, u32[]{:S(2)}) collective-permute-start(bf16[416,128]{1,0:T(8,128)(2,1)} %get-tuple-element.22), channel_id=1, source_target_pairs={{0,8},{4,12},{8,0},{12,4},{16,24},{20,28},{24,16},{28,20},{32,40},... | collective-permute-start | bytes 319496 | tf_op jit(solution)/shard_map/ppermute | solution.py:58
  34.1 0.3 collective-permute-done.3.down_ref
  34.4 3.8 %collective-permute-done.2.up_ref = bf16[416,128]{1,0:T(8,128)(2,1)S(1)} collective-permute-done((bf16[416,128]{1,0:T(8,128)(2,1)}, bf16[416,128]{1,0:T(8,128)(2,1)S(1)}, u32[]{:S(2)}, u32[]{:S(2)}) %collective-permute-start.2) | collective-permute-done | bytes 106528 | tf_op jit(solution)/shard_map/ppermute | solution.py:58
  38.2 0.9 pad_maximum_fusion.sent_ref
  39.1 6.2 %collective-permute-start.4 = (bf16[832,128]{1,0:T(8,128)(2,1)S(1)}, bf16[832,128]{1,0:T(8,128)(2,1)S(1)}, u32[]{:S(2)}, u32[]{:S(2)}) collective-permute-start(bf16[832,128]{1,0:T(8,128)(2,1)S(1)} %pad_maximum_fusion.sent_ref), channel_id=1, source_target_pairs={{0,4},{4,0},{8,12},{12,8},{16,20},{20,16},{24,28},{28,24},{32,36},... | collective-permute-start | bytes 638984 | tf_op jit(solution)/shard_map/ppermute | solution.py:58
  45.4 1.1 collective-permute-done.4.swap_ref
  46.5 1.0 shard_map.114
  47.5 21.6 %all_to_all.34 = bf16[4,1024,128]{2,1,0:T(8,128)(2,1)S(1)} all-to-all(bf16[4,1024,128]{2,1,0:T(8,128)(2,1)S(1)} %bitcast.14), channel_id=1, replica_groups=mesh['pts'=128,'chan'=4] {'chan'}, dimensions={0} | all-to-all | bytes 2097152 | tf_op jit(solution)/shard_map/all_to_all | solution.py:407
  69.1 3.1 %collective-permute-start.5 = (bf16[10240,128]{1,0:T(8,128)(2,1)}, bf16[10240,128]{1,0:T(8,128)(2,1)S(1)}, u32[]{:S(2)}, u32[]{:S(2)}) collective-permute-start(bf16[10240,128]{1,0:T(8,128)(2,1)} %all-gather.2.cloned.1.call-done.mine_ref), channel_id=1, source_target_pairs={{0,4},{4,0},{8,12},{12,8},{16,20},{20,16},{24,28},{28,24},{32,36},... | collective-permute-start | bytes 7864328 | tf_op jit(solution)/shard_map/ppermute | solution.py:58
  72.3 11.8 %shard_map.116 = bf16[512,256]{1,0:T(8,128)(2,1)S(1)} custom-call(bf16[4096,128]{1,0:T(8,128)(2,1)S(1)} %bitcast.10, f32[1,512]{1,0:T(1,128)S(1)} %bitcast.20, bf16[3,512,128]{2,1,0:T(8,128)(2,1)S(1)} %copy-done.3), custom_call_target="tpu_custom_call" | custom-call | flops 8999999488 | bytes 2000000 | tf_op jit(solution)/shard_map/pallas_call | solution.py:357
  84.1 8.9 %all_to_all.35 = bf16[4,128,256]{2,1,0:T(8,128)(2,1)S(1)} all-to-all(bf16[4,128,256]{2,1,0:T(8,128)(2,1)S(1)} %bitcast.16), channel_id=1, replica_groups=mesh['pts'=128,'chan'=4] {'chan'}, dimensions={0} | all-to-all | bytes 524288 | tf_op jit(solution)/shard_map/all_to_all | solution.py:422
  93.0 2.6 %shard_map.117 = (bf16[256,512]{1,0:T(8,128)(2,1)S(1)}, f32[128,512]{1,0:T(8,128)S(1)}, bf16[128,512]{1,0:T(8,128)(2,1)S(1)}, bf16[128,512]{1,0:T(8,128)(2,1)S(1)}) custom-call(bf16[512,256]{1,0:T(8,128)(2,1)S(1)} %bitcast.15, bf16[4096,128]{1,0:T(8,128)(2,1)S(1)} %bitcast.11, f32[1,512]{1,0:T(1,128)S(1)} %bitcast.19, s32[1,1024]{1,0:T(1,128)S(1)} %bitcast.18, ...), custom_call_target="tpu_custom_call" | custom-call | tf_op jit(solution)/shard_map/pallas_call | solution.py:357
  95.6 4.2 %collective-permute-start.6 = (bf16[128,512]{1,0:T(8,128)(2,1)S(1)}, bf16[128,512]{1,0:T(8,128)(2,1)S(1)}, u32[]{:S(2)}, u32[]{:S(2)}) collective-permute-start(bf16[128,512]{1,0:T(8,128)(2,1)S(1)} %get-tuple-element.31), channel_id=1, source_target_pairs={{0,508},{4,8},{8,4},{12,16},{16,12},{20,24},{24,20},{28,32},{32,28... | collective-permute-start | bytes 393224 | tf_op jit(solution)/shard_map/ppermute | solution.py:58
  99.8 5.9 %collective-permute-start.7 = (bf16[128,512]{1,0:T(8,128)(2,1)S(1)}, bf16[128,512]{1,0:T(8,128)(2,1)S(1)}, u32[]{:S(2)}, u32[]{:S(2)}) collective-permute-start(bf16[128,512]{1,0:T(8,128)(2,1)S(1)} %get-tuple-element.32), channel_id=1, source_target_pairs={{0,4},{4,0},{8,12},{12,8},{16,20},{20,16},{24,28},{28,24},{32,36},... | collective-permute-start | bytes 393224 | tf_op jit(solution)/shard_map/ppermute | solution.py:58
  105.7 1.0 collective-permute-done.7.swap_ref
  106.7 0.1 shard_map.118
  106.8 10.2 %all_to_all.36 = bf16[4,384,128]{2,1,0:T(8,128)(2,1)S(1)} all-to-all(bf16[4,384,128]{2,1,0:T(8,128)(2,1)S(1)} %bitcast.13), channel_id=1, replica_groups=mesh['pts'=128,'chan'=4] {'chan'}, dimensions={0} | all-to-all | bytes 786432 | tf_op jit(solution)/shard_map/all_to_all | solution.py:437
  117.0 0.7 shard_map.119
  (18 shorter events, 0.1 us)
Async XLA Ops:
  7.2 61.9 %all-gather.2.cloned.1.call-start = ((), (), s32[]{:S(2)}) async-start(), calls=%async_computation.3 | async-start | bytes 3276800 | tf_op jit(solution)/shard_map/all_gather | solution.py:380
  9.3 62.9 %copy-start.3 = (bf16[3,512,128]{2,1,0:T(8,128)(2,1)S(1)}, bf16[3,512,128]{2,1,0:T(8,128)(2,1)}, u32[]{:S(2)}) copy-start(bf16[3,512,128]{2,1,0:T(8,128)(2,1)} %w_ref.1) | copy-start | bytes 1179652
  9.3 62.9 %copy-start.4 = (f32[512]{0:T(512)S(1)}, f32[512]{0:T(512)}, u32[]{:S(2)}) copy-start(f32[512]{0:T(512)} %param.13) | copy-start | bytes 6148
  13.0 19.1 %collective-permute-start = (bf16[208,128]{1,0:T(8,128)(2,1)}, bf16[208,128]{1,0:T(8,128)(2,1)S(1)}, u32[]{:S(2)}, u32[]{:S(2)}) collective-permute-start(bf16[208,128]{1,0:T(8,128)(2,1)} %get-tuple-element.20), channel_id=1, source_target_pairs={{0,500},{4,16},{8,508},{12,24},{16,4},{20,32},{24,12},{28,40},{32,... | collective-permute-start | bytes 159752 | tf_op jit(solution)/shard_map/ppermute | solution.py:58
  19.3 12.8 %collective-permute-start.1 = (bf16[208,128]{1,0:T(8,128)(2,1)}, bf16[208,128]{1,0:T(8,128)(2,1)S(1)}, u32[]{:S(2)}, u32[]{:S(2)}) collective-permute-start(bf16[208,128]{1,0:T(8,128)(2,1)} %get-tuple-element.21), channel_id=1, source_target_pairs={{0,256},{4,260},{8,264},{12,268},{16,272},{20,276},{24,280},{28,28... | collective-permute-start | bytes 159752 | tf_op jit(solution)/shard_map/ppermute | solution.py:58
  24.0 10.5 %collective-permute-start.3 = (bf16[416,128]{1,0:T(8,128)(2,1)}, bf16[416,128]{1,0:T(8,128)(2,1)S(1)}, u32[]{:S(2)}, u32[]{:S(2)}) collective-permute-start(bf16[416,128]{1,0:T(8,128)(2,1)} %get-tuple-element.23), channel_id=1, source_target_pairs={{0,504},{4,508},{8,16},{12,20},{16,8},{20,12},{24,32},{28,36},{32,... | collective-permute-start | bytes 319496 | tf_op jit(solution)/shard_map/ppermute | solution.py:58
  32.2 6.1 %collective-permute-start.2 = (bf16[416,128]{1,0:T(8,128)(2,1)}, bf16[416,128]{1,0:T(8,128)(2,1)S(1)}, u32[]{:S(2)}, u32[]{:S(2)}) collective-permute-start(bf16[416,128]{1,0:T(8,128)(2,1)} %get-tuple-element.22), channel_id=1, source_target_pairs={{0,8},{4,12},{8,0},{12,4},{16,24},{20,28},{24,16},{28,20},{32,40},... | collective-permute-start | bytes 319496 | tf_op jit(solution)/shard_map/ppermute | solution.py:58
  39.1 7.3 %collective-permute-start.4 = (bf16[832,128]{1,0:T(8,128)(2,1)S(1)}, bf16[832,128]{1,0:T(8,128)(2,1)S(1)}, u32[]{:S(2)}, u32[]{:S(2)}) collective-permute-start(bf16[832,128]{1,0:T(8,128)(2,1)S(1)} %pad_maximum_fusion.sent_ref), channel_id=1, source_target_pairs={{0,4},{4,0},{8,12},{12,8},{16,20},{20,16},{24,28},{28,24},{32,36},... | collective-permute-start | bytes 638984 | tf_op jit(solution)/shard_map/ppermute | solution.py:58
  69.1 23.9 %collective-permute-start.5 = (bf16[10240,128]{1,0:T(8,128)(2,1)}, bf16[10240,128]{1,0:T(8,128)(2,1)S(1)}, u32[]{:S(2)}, u32[]{:S(2)}) collective-permute-start(bf16[10240,128]{1,0:T(8,128)(2,1)} %all-gather.2.cloned.1.call-done.mine_ref), channel_id=1, source_target_pairs={{0,4},{4,0},{8,12},{12,8},{16,20},{20,16},{24,28},{28,24},{32,36},... | collective-permute-start | bytes 7864328 | tf_op jit(solution)/shard_map/ppermute | solution.py:58
  72.2 20.7 %copy-start = (bf16[10240,128]{1,0:T(8,128)(2,1)S(1)}, bf16[10240,128]{1,0:T(8,128)(2,1)}, u32[]{:S(2)}) copy-start(bf16[10240,128]{1,0:T(8,128)(2,1)} %all-gather.2.cloned.1.call-done.mine_ref) | copy-start | bytes 7864324
  72.2 20.7 %copy-start.1 = (s32[1024]{0:T(1024)S(1)}, s32[1024]{0:T(1024)}, u32[]{:S(2)}) copy-start(s32[1024]{0:T(1024)} %param.12) | copy-start | bytes 12292
  72.3 20.7 %copy-start.2 = (f32[512]{0:T(512)S(1)}, f32[512]{0:T(512)}, u32[]{:S(2)}) copy-start(f32[512]{0:T(512)} %param.16) | copy-start | bytes 6148
  95.6 10.1 %collective-permute-start.6 = (bf16[128,512]{1,0:T(8,128)(2,1)S(1)}, bf16[128,512]{1,0:T(8,128)(2,1)S(1)}, u32[]{:S(2)}, u32[]{:S(2)}) collective-permute-start(bf16[128,512]{1,0:T(8,128)(2,1)S(1)} %get-tuple-element.31), channel_id=1, source_target_pairs={{0,508},{4,8},{8,4},{12,16},{16,12},{20,24},{24,20},{28,32},{32,28... | collective-permute-start | bytes 393224 | tf_op jit(solution)/shard_map/ppermute | solution.py:58
  99.8 6.9 %collective-permute-start.7 = (bf16[128,512]{1,0:T(8,128)(2,1)S(1)}, bf16[128,512]{1,0:T(8,128)(2,1)S(1)}, u32[]{:S(2)}, u32[]{:S(2)}) collective-permute-start(bf16[128,512]{1,0:T(8,128)(2,1)S(1)} %get-tuple-element.32), channel_id=1, source_target_pairs={{0,4},{4,0},{8,12},{12,8},{16,20},{20,16},{24,28},{28,24},{32,36},... | collective-permute-start | bytes 393224 | tf_op jit(solution)/shard_map/ppermute | solution.py:58
Sparse Core Ops, SparseCore 0:
  10.1 51.4 all-gather.1
